TPU v7x, 256 devices: a whole 4x4x8 slice. The times are simulated.
256 devices in a mesh: row: 16 (over y, x), col: 16 (over z, core).
Axes of the slice: x: 4, y: 4, z: 8, core: 2. Of those that a mesh axis runs over, the one named last changes fastest.
Arguments:
- kernel_matrix: float32 [16384, 16384], P('row', 'col'), may hold values from -0.04 to 32, as said below
Outputs:
- factored: float32 [16384, 16384], P('row', 'col')
Inputs may be any that keep to these rules, and one draw needn't show every extreme that they name: kernel_matrix's logical matrix is symmetric positive definite with eigenvalues of 0.1 or more.
All inputs are finite; a program needn't handle non-finite values.
Results may differ from a plain program's by a relative error of at most 0.00017.
Values sent between devices are 32-bit elements; how exact they have to be, the bound alone decides.
No kernel may reach another device: no remote copies, remote signals or barrier semaphores. Data moves between devices by JAX's collectives and lax.ppermute only.
A program may use at most 64 MiB of HBM per device.

v0:
```python
import jax
import jax.numpy as jnp
from jax import lax
from jax.sharding import PartitionSpec as P

BLOCK = 128
PANELS = 4


def spread(shard, axis, root):
    mine = lax.axis_index(axis) == root
    return lax.psum(jnp.where(mine, shard, jnp.zeros_like(shard)), axis)


def right_product(left, right):
    return lax.dot_general(
        left,
        right,
        (((1,), (1,)), ((), ())),
        precision=lax.Precision.HIGHEST,
        preferred_element_type=jnp.float32,
    )


def factor_block(column, panel_id, row_count):
    width = column.shape[1]
    local_row = panel_id // row_count * width
    diagonal = column[local_row : local_row + width]
    factor = jnp.linalg.cholesky(diagonal)
    inverse = jax.scipy.linalg.solve_triangular(
        factor, jnp.eye(width, dtype=jnp.float32), lower=True
    )
    return (
        spread(factor, "row", panel_id % row_count),
        spread(inverse, "row", panel_id % row_count),
    )


def apply_inverse(source, block_ids, factor, inverse, panel_id):
    width = factor.shape[0]
    product = right_product(source, inverse).reshape(-1, width, width)
    chosen = block_ids[:, None, None]
    result = jnp.where(
        chosen < panel_id,
        jnp.zeros_like(product),
        jnp.where(chosen == panel_id, factor[None], product),
    )
    return result.reshape(source.shape)


def share_column(block, panel_id, col_count):
    return spread(block, "col", panel_id % col_count)


def transposed(rows_data, col_index, row_count, col_count):
    width = rows_data.shape[1]
    col_ratio = col_count // row_count
    grouped = rows_data.reshape(-1, col_ratio, width, width)
    picked = lax.dynamic_index_in_dim(grouped, col_index // row_count, axis=1, keepdims=False)
    picked = picked.reshape(-1, width)
    return spread(picked, "row", col_index % row_count)


def shards(kernel_matrix):
    row_count = lax.axis_size("row")
    col_count = lax.axis_size("col")
    row_index = lax.axis_index("row")
    col_index = lax.axis_index("col")
    width = BLOCK
    local_rows, local_cols = kernel_matrix.shape
    row_ids = jnp.arange(local_rows // width, dtype=jnp.int32) * row_count + row_index
    col_ids = jnp.arange(local_cols // width, dtype=jnp.int32) * col_count + col_index
    matrix = kernel_matrix
    panel_rows = []
    panel_cols = []
    for panel_id in range(PANELS):
        lead = panel_id // col_count * width
        column = matrix[:, lead : lead + width]
        factor, inverse = factor_block(column, panel_id, row_count)
        row_panel = share_column(
            apply_inverse(column, row_ids, factor, inverse, panel_id), panel_id, col_count
        )
        col_panel = transposed(row_panel, col_index, row_count, col_count)
        panel_rows.append(row_panel)
        panel_cols.append(col_panel)
        matrix = matrix - right_product(row_panel, col_panel)
    result = matrix
    for panel_id in range(PANELS):
        lead = panel_id // col_count * width
        chosen = jnp.where(
            col_index == panel_id % col_count, panel_rows[panel_id], result[:, lead : lead + width]
        )
        result = result.at[:, lead : lead + width].set(chosen)
    row_upper = jnp.repeat(row_ids < PANELS, width)
    col_later = jnp.repeat(col_ids >= PANELS, width)
    return jnp.where(row_upper[:, None] & col_later[None, :], jnp.zeros_like(result), result)


def solution(mesh):
    placed = (P("row", "col"),)
    return jax.shard_map(
        shards, mesh=mesh, in_specs=placed, out_specs=P("row", "col"), check_vma=False
    )
```

profile of v0, /device:TPU:1, one launch (start us, length us, event | category | flops | bytes accessed | tf_op | source)
XLA Modules:
  0.0 1380.8 jit_solution(17513776417127865715)
XLA Ops:
  6.5 5.3 copy.5
  11.9 0.8 slice.128
  12.8 0.9 fusion.26
  13.7 11.7 cholesky.74
  25.4 0.7 compare_reduce_fusion.3
  26.1 1.3 fusion.27
  27.5 9.8 custom-call.8
  37.3 0.9 convolution_select_fusion.6
  38.4 95.0 %all-reduce.39.cloned.1.call-done = (f32[128,128]{1,0:T(8,128)}, f32[128,128]{1,0:T(8,128)}) async-done(((f32[128,128]{1,0:T(8,128)}, f32[128,128]{1,0:T(8,128)}), (f32[128,128]{1,0:T(8,128)}, f32[128,128]{1,0:T(8,128)})) %all-reduce.39.cloned.1.call-update) | async-done | bytes 131088 | tf_op jit(solution)/shard_map/psum | solution.py:12
  133.4 0.9 copy.4
  134.4 2.6 fusion.8
  137.0 110.4 %all-reduce.17.cloned.1.call-done = f32[1024,128]{0,1:T(8,128)} async-done(((f32[1024,128]{0,1:T(8,128)}), f32[1024,128]{0,1:T(8,128)}) %all-reduce.17.cloned.1.call-update) | async-done | bytes 524304 | tf_op jit(solution)/shard_map/psum | solution.py:12
  247.4 0.9 broadcast_select_fusion.2
  249.0 96.0 %all-reduce.19.cloned.1.call-done = f32[1024,128]{0,1:T(8,128)} async-done(((f32[1024,128]{0,1:T(8,128)}), f32[1024,128]{0,1:T(8,128)}) %all-reduce.19.cloned.1.call-update) | async-done | bytes 524304 | tf_op jit(solution)/shard_map/psum | solution.py:12
  345.0 6.2 convolution_subtract_fusion.3
  351.2 2.0 copy-done
  353.3 0.9 fusion.24
  354.1 11.7 cholesky.85
  365.9 0.7 compare_reduce_fusion.2
  366.6 1.3 fusion.28
  367.9 9.8 custom-call.9
  377.7 0.9 convolution_select_fusion.5
  378.8 91.9 %all-reduce.37.cloned.1.call-done = (f32[128,128]{1,0:T(8,128)}, f32[128,128]{1,0:T(8,128)}) async-done(((f32[128,128]{1,0:T(8,128)}, f32[128,128]{1,0:T(8,128)}), (f32[128,128]{1,0:T(8,128)}, f32[128,128]{1,0:T(8,128)})) %all-reduce.37.cloned.1.call-update) | async-done | bytes 131088 | tf_op jit(solution)/shard_map/psum | solution.py:12
  470.7 0.9 copy.8
  471.7 2.6 fusion.5
  474.3 110.4 %all-reduce.21.cloned.1.call-done = f32[1024,128]{0,1:T(8,128)} async-done(((f32[1024,128]{0,1:T(8,128)}), f32[1024,128]{0,1:T(8,128)}) %all-reduce.21.cloned.1.call-update) | async-done | bytes 524304 | tf_op jit(solution)/shard_map/psum | solution.py:12
  584.8 0.9 broadcast_select_fusion
  586.0 96.5 %all-reduce.23.cloned.1.call-done = f32[1024,128]{0,1:T(8,128)} async-done(((f32[1024,128]{0,1:T(8,128)}), f32[1024,128]{0,1:T(8,128)}) %all-reduce.23.cloned.1.call-update) | async-done | bytes 524304 | tf_op jit(solution)/shard_map/psum | solution.py:12
  682.5 6.2 convolution_subtract_fusion.2
  688.7 2.0 copy-done.1
  690.8 0.9 fusion.22
  691.7 11.7 cholesky.96
  703.4 0.7 compare_reduce_fusion.1
  704.1 1.3 fusion.29
  705.4 9.8 custom-call.10
  715.3 0.9 convolution_select_fusion.4
  716.3 91.9 %all-reduce.35.cloned.1.call-done = (f32[128,128]{1,0:T(8,128)}, f32[128,128]{1,0:T(8,128)}) async-done(((f32[128,128]{1,0:T(8,128)}, f32[128,128]{1,0:T(8,128)}), (f32[128,128]{1,0:T(8,128)}, f32[128,128]{1,0:T(8,128)})) %all-reduce.35.cloned.1.call-update) | async-done | bytes 131088 | tf_op jit(solution)/shard_map/psum | solution.py:12
  808.2 0.9 copy.12
  809.2 2.6 fusion.3
  811.8 110.4 %all-reduce.25.cloned.1.call-done = f32[1024,128]{0,1:T(8,128)} async-done(((f32[1024,128]{0,1:T(8,128)}), f32[1024,128]{0,1:T(8,128)}) %all-reduce.25.cloned.1.call-update) | async-done | bytes 524304 | tf_op jit(solution)/shard_map/psum | solution.py:12
  922.3 0.8 broadcast_select_fusion.3
  923.5 96.3 %all-reduce.27.cloned.1.call-done = f32[1024,128]{0,1:T(8,128)} async-done(((f32[1024,128]{0,1:T(8,128)}), f32[1024,128]{0,1:T(8,128)}) %all-reduce.27.cloned.1.call-update) | async-done | bytes 524304 | tf_op jit(solution)/shard_map/psum | solution.py:12
  1019.8 6.2 convolution_subtract_fusion.1
  1026.0 2.0 copy-done.2
  1028.1 0.9 fusion.20
  1029.0 11.7 cholesky.107
  1040.7 0.7 compare_reduce_fusion
  1041.4 1.2 fusion.30
  1042.6 9.8 custom-call.11
  1052.4 0.9 convolution_select_fusion.3
  1053.5 91.9 %all-reduce.33.cloned.1.call-done = (f32[128,128]{1,0:T(8,128)}, f32[128,128]{1,0:T(8,128)}) async-done(((f32[128,128]{1,0:T(8,128)}, f32[128,128]{1,0:T(8,128)}), (f32[128,128]{1,0:T(8,128)}, f32[128,128]{1,0:T(8,128)})) %all-reduce.33.cloned.1.call-update) | async-done | bytes 131088 | tf_op jit(solution)/shard_map/psum | solution.py:12
  1145.4 0.9 copy.16
  1146.4 2.5 fusion.1
  1149.3 0.6 compare_reduce_fusion.4
  1149.9 109.6 %all-reduce.29.cloned.1.call-done = f32[1024,128]{0,1:T(8,128)} async-done(((f32[1024,128]{0,1:T(8,128)}), f32[1024,128]{0,1:T(8,128)}) %all-reduce.29.cloned.1.call-update) | async-done | bytes 524304 | tf_op jit(solution)/shard_map/psum | solution.py:12
  1259.4 0.9 broadcast_select_fusion.1
  1260.5 96.7 %all-reduce.31.cloned.1.call-done = f32[1024,128]{0,1:T(8,128)} async-done(((f32[1024,128]{0,1:T(8,128)}), f32[1024,128]{0,1:T(8,128)}) %all-reduce.31.cloned.1.call-update) | async-done | bytes 524304 | tf_op jit(solution)/shard_map/psum | solution.py:12
  1357.2 6.0 convolution_subtract_fusion
  1363.2 0.8 constant_dynamic-update-slice_fusion.1
  1364.0 0.6 fusion.14
  1364.6 0.7 constant_dynamic-update-slice_fusion
  1365.4 0.6 fusion.9
  1366.0 2.4 and_select_fusion
  1368.4 5.3 copy.19
  (66 shorter events, 3.3 us)
Async XLA Ops:
  6.5 126.8 %all-reduce.39.cloned.1.call-start = ((), (), s32[]{:S(2)}) async-start(), calls=%async_computation.11 | async-start | bytes 262144 | tf_op jit(solution)/shard_map/psum | solution.py:12
  38.2 209.2 %all-reduce.17.cloned.1.call-start = ((), (), s32[]{:S(2)}) async-start(), calls=%async_computation | async-start | bytes 1048576 | tf_op jit(solution)/shard_map/psum | solution.py:12
  136.9 208.0 %all-reduce.19.cloned.1.call-start = ((), (), s32[]{:S(2)}) async-start(), calls=%async_computation.1 | async-start | bytes 1048576 | tf_op jit(solution)/shard_map/psum | solution.py:12
  248.3 222.4 %all-reduce.37.cloned.1.call-start = ((), (), s32[]{:S(2)}) async-start(), calls=%async_computation.10 | async-start | bytes 262144 | tf_op jit(solution)/shard_map/psum | solution.py:12
  351.2 2.0 copy-start
  378.7 206.1 %all-reduce.21.cloned.1.call-start = ((), (), s32[]{:S(2)}) async-start(), calls=%async_computation.2 | async-start | bytes 1048576 | tf_op jit(solution)/shard_map/psum | solution.py:12
  474.3 208.2 %all-reduce.23.cloned.1.call-start = ((), (), s32[]{:S(2)}) async-start(), calls=%async_computation.3 | async-start | bytes 1048576 | tf_op jit(solution)/shard_map/psum | solution.py:12
  585.6 222.6 %all-reduce.35.cloned.1.call-start = ((), (), s32[]{:S(2)}) async-start(), calls=%async_computation.9 | async-start | bytes 262144 | tf_op jit(solution)/shard_map/psum | solution.py:12
  688.7 2.0 copy-start.1
  716.2 206.1 %all-reduce.25.cloned.1.call-start = ((), (), s32[]{:S(2)}) async-start(), calls=%async_computation.4 | async-start | bytes 1048576 | tf_op jit(solution)/shard_map/psum | solution.py:12
  811.8 208.0 %all-reduce.27.cloned.1.call-start = ((), (), s32[]{:S(2)}) async-start(), calls=%async_computation.5 | async-start | bytes 1048576 | tf_op jit(solution)/shard_map/psum | solution.py:12
  923.1 222.3 %all-reduce.33.cloned.1.call-start = ((), (), s32[]{:S(2)}) async-start(), calls=%async_computation.8 | async-start | bytes 262144 | tf_op jit(solution)/shard_map/psum | solution.py:12
  1026.0 2.0 copy-start.2
  1053.4 206.1 %all-reduce.29.cloned.1.call-start = ((), (), s32[]{:S(2)}) async-start(), calls=%async_computation.6 | async-start | bytes 1048576 | tf_op jit(solution)/shard_map/psum | solution.py:12
  1149.0 208.2 %all-reduce.31.cloned.1.call-start = ((), (), s32[]{:S(2)}) async-start(), calls=%async_computation.7 | async-start | bytes 1048576 | tf_op jit(solution)/shard_map/psum | solution.py:12
  1260.5 102.7 %copy-start.4 = (f32[1024,128]{0,1:T(8,128)S(1)}, f32[1024,128]{0,1:T(8,128)}, u32[]{:S(2)}) copy-start(f32[1024,128]{0,1:T(8,128)} %all-reduce.17.cloned.1.call-done) | copy-start | bytes 1572868
  1260.5 103.5 %copy-start.3 = (f32[1024,128]{0,1:T(8,128)S(1)}, f32[1024,128]{0,1:T(8,128)}, u32[]{:S(2)}) copy-start(f32[1024,128]{0,1:T(8,128)} %all-reduce.21.cloned.1.call-done) | copy-start | bytes 1572868
  1260.5 104.1 %copy-start.5 = (f32[1024,128]{0,1:T(8,128)S(1)}, f32[1024,128]{0,1:T(8,128)}, u32[]{:S(2)}) copy-start(f32[1024,128]{0,1:T(8,128)} %all-reduce.25.cloned.1.call-done) | copy-start | bytes 1572868
  1363.2 2.2 copy-start.6
Sparse Core Ops, SparseCore 0:
  38.3 95.0 all-reduce.38
  137.1 110.3 all-reduce.16
  250.6 94.3 all-reduce.18
  378.8 91.8 all-reduce.36
  474.4 110.3 all-reduce.20
  588.1 94.3 all-reduce.22
  716.3 91.8 all-reduce.34
  811.9 110.3 all-reduce.24
  925.5 94.3 all-reduce.26
  1053.5 91.8 all-reduce.32
  1149.1 110.3 all-reduce.28
  1262.8 94.3 all-reduce.30
where the time goes:
time: 1390 us; the launch traced here: 1380 us
  waiting for transfers between devices  1200 us (86%)
  other arithmetic  107 us (8%)
  matrix products  38.3 us (3%)
  local copies, waits for them, and re-layouts  22.5 us (2%)
  between operations  14.2 us (1%)
    psum x12, waiting for transfers between devices, spread(): return lax.psum(jnp.where(mine, shard, jnp.zeros_like(shard)), axis)  1200 us
    another operation x12, other arithmetic, factor_block(): factor = jnp.linalg.cholesky(diagonal)  49.8 us
    another operation x4, other arithmetic, factor_block(): jax.scipy.linalg.solve_triangular(factor, jnp.eye(width, dtype=jnp.float3...  39.2 us
    dot_general x8, matrix products, right_product(): lax.dot_general(left, right, (((1,), (1,)), ((), ())), precision=lax.Prec...  34.7 us
  transfers between devices with their start and end apart: 12, of which 12 were waited for; matrix products, arithmetic and copies ran while one was open for 0% of the time, Pallas kernels for 0%

commit v1 on v0

v1 whole, which is shorter than its diff:
```python
import jax
import jax.numpy as jnp
from jax import lax
from jax.experimental import pallas as pl
from jax.experimental.pallas import tpu as pltpu
from jax.sharding import Mesh, PartitionSpec as P

BLOCK = 128
PANELS = 4
SPAN = BLOCK * PANELS
SUB = 8
F32 = jnp.float32
BF16 = jnp.bfloat16


def exact_dot(left, right, left_dim, right_dim):
    return lax.dot_general(
        left,
        right,
        (((left_dim,), (right_dim,)), ((), ())),
        precision=lax.Precision.HIGHEST,
        preferred_element_type=F32,
    )


def split(value):
    high = value.astype(BF16)
    low = (value - high.astype(F32)).astype(BF16)
    return high, low


def split_dot(left, right, left_dim, right_dim):
    def dot(a, b):
        return lax.dot_general(
            a, b, (((left_dim,), (right_dim,)), ((), ())), preferred_element_type=F32
        )

    return dot(left[0], right[0]) + (dot(left[0], right[1]) + dot(left[1], right[0]))


def lane_fill(value, lane):
    return jnp.broadcast_to(value[:, lane : lane + 1], (SUB, BLOCK))


def row_fill(value, row):
    return jnp.broadcast_to(value[row : row + 1, :], (SUB, BLOCK))


def eliminate(a, e):
    a, e = list(a), list(e)
    groups = len(a)
    sub = lax.broadcasted_iota(jnp.int32, (SUB, BLOCK), 0)
    for c in range(groups):
        base = SUB * c
        cols = {g: [lane_fill(a[g], base + j) for j in range(SUB)] for g in range(c, groups)}
        s = [[row_fill(cols[c][j], i) if i >= j else None for j in range(SUB)] for i in range(SUB)]
        ra = [row_fill(a[c], j) for j in range(SUB)]
        re = [row_fill(e[c], j) for j in range(SUB)]
        for j in range(SUB):
            inv = lax.rsqrt(s[j][j])
            for i in range(j + 1, SUB):
                s[i][j] = s[i][j] * inv
            for k in range(j + 1, SUB):
                for i in range(k, SUB):
                    s[i][k] = s[i][k] - s[i][j] * s[k][j]
            ra[j] = ra[j] * inv
            re[j] = re[j] * inv
            for k in range(j + 1, SUB):
                ra[k] = ra[k] - s[k][j] * ra[j]
                re[k] = re[k] - s[k][j] * re[j]
            for g in range(c + 1, groups):
                cols[g][j] = cols[g][j] * inv
                for k in range(j + 1, SUB):
                    cols[g][k] = cols[g][k] - cols[g][j] * s[k][j]
                a[g] = a[g] - cols[g][j] * ra[j]
                e[g] = e[g] - cols[g][j] * re[j]
        ua, ue = ra[0], re[0]
        for j in range(1, SUB):
            ua = jnp.where(sub == j, ra[j], ua)
            ue = jnp.where(sub == j, re[j], ue)
        a[c], e[c] = ua, ue
    return a, e


def head_kernel(place, r0, r1, r2, r3, o0, o1, o2, o3, u_ref, v_ref):
    x, c = place[1], place[3]
    for step, (own, other) in enumerate(((r0, o0), (r1, o1), (r2, o2), (r3, o3))):
        rows = pl.ds(pl.multiple_of(((x - step + PANELS) % PANELS) * BLOCK, BLOCK), BLOCK)
        for half in range(2):
            lanes = slice(half * BLOCK, (half + 1) * BLOCK)
            mine = pl.ds(pl.multiple_of((c + 2 * half) * BLOCK, BLOCK), BLOCK)
            theirs = pl.ds(pl.multiple_of((1 - c + 2 * half) * BLOCK, BLOCK), BLOCK)
            u_ref[rows, mine] = own[:, lanes]
            u_ref[rows, theirs] = other[:, lanes]
    row = lax.broadcasted_iota(jnp.int32, (BLOCK, BLOCK), 0)
    col = lax.broadcasted_iota(jnp.int32, (BLOCK, BLOCK), 1)
    eye = (row == col).astype(F32)
    all_rows = lax.broadcasted_iota(jnp.int32, (SPAN, SPAN), 0)
    all_cols = lax.broadcasted_iota(jnp.int32, (SPAN, SPAN), 1)
    v_ref[...] = (all_rows == all_cols).astype(F32)
    lane = lax.broadcasted_iota(jnp.int32, (BLOCK, SPAN), 1)

    def panel(k, carry):
        at = pl.multiple_of(k * BLOCK, BLOCK)
        here = pl.ds(at, BLOCK)
        block = u_ref[here, here]
        groups = range(0, BLOCK, SUB)
        a, e = eliminate([block[g : g + SUB] for g in groups], [eye[g : g + SUB] for g in groups])
        factor = jnp.where(row <= col, jnp.concatenate(a, 0), 0.0)
        inverse = jnp.where(row >= col, jnp.concatenate(e, 0), 0.0)
        upper = exact_dot(inverse, u_ref[here, :], 1, 0)
        lower = exact_dot(inverse, v_ref[here, :], 1, 0)
        u_ref[here, :] = upper
        v_ref[here, :] = lower
        u_ref[here, here] = factor
        later = jnp.where(lane >= at + BLOCK, upper, 0.0)
        u_ref[...] -= exact_dot(later, upper, 0, 0)
        v_ref[...] -= exact_dot(later, lower, 0, 0)
        return carry

    lax.fori_loop(0, PANELS, panel, 0)
    u_ref[...] = jnp.where(all_rows <= all_cols, u_ref[...], 0.0)


def factor_head(place, own, other):
    shape = jax.ShapeDtypeStruct((SPAN, SPAN), F32)
    vmem = pl.BlockSpec(memory_space=pltpu.VMEM)
    return pl.pallas_call(
        head_kernel,
        out_shape=[shape, shape],
        in_specs=[pl.BlockSpec(memory_space=pltpu.SMEM)] + [vmem] * 8,
        out_specs=[vmem, vmem],
        compiler_params=pltpu.CompilerParams(vmem_limit_bytes=48 * 2**20),
    )(place, *own, *other)


TILE = 256


def update_kernel(place, a_ref, own, other, cols, u_ref, v_ref, out_ref, w_hi, w_lo, v_hi, v_lo):
    y, x, z, c = place[0], place[1], place[2], place[3]
    t = pl.program_id(0)

    @pl.when(t == 0)
    def _():
        values = cols[...]
        column = jnp.concatenate(
            [values[:, k].reshape(BLOCK, values.shape[-1]) for k in range(PANELS)], 0
        )
        high, low = split(split_dot(split(v_ref[...]), split(column), 1, 0))
        w_hi[...] = high
        w_lo[...] = low
        for slot, k in enumerate((c, c + 2, 1 - c, 3 - c)):
            piece = v_ref[:, pl.ds(pl.multiple_of(k * BLOCK, BLOCK), BLOCK)]
            high, low = split(piece)
            v_hi[:, slot * BLOCK : (slot + 1) * BLOCK] = high
            v_lo[:, slot * BLOCK : (slot + 1) * BLOCK] = low

    first = (z + t) % 8
    second = (z - 1 - t + 8) % 8
    rows = jnp.concatenate([own[first], own[second], other[first], other[second]], 1)
    panel = split_dot(split(rows), (v_hi[...], v_lo[...]), 1, 1)
    out_ref[...] = a_ref[...] - split_dot(split(panel), (w_hi[...], w_lo[...]), 1, 0)
    q = 2 * z + c
    for k in range(PANELS):

        @pl.when(q == k)
        def _():
            out_ref[:, :BLOCK] = panel[:, k * BLOCK : (k + 1) * BLOCK]

    @pl.when((t == 0) & (y == 0))
    def _():
        out_ref[:BLOCK, :] = jnp.zeros((BLOCK, out_ref.shape[1]), F32)

    @pl.when((t == 0) & (y == 0) & (q < PANELS))
    def _():
        at_row = pl.ds(pl.multiple_of(jnp.minimum(q, PANELS - 1) * BLOCK, BLOCK), BLOCK)
        at_col = pl.ds(pl.multiple_of(x * BLOCK, BLOCK), BLOCK)
        out_ref[:BLOCK, :BLOCK] = u_ref[at_row, at_col].T


def update(place, matrix, own, other, cols, upper, inverse):
    rows, width = matrix.shape
    vmem = pl.BlockSpec(memory_space=pltpu.VMEM)
    tile = pl.BlockSpec((TILE, width), lambda t: (t, 0))
    return pl.pallas_call(
        update_kernel,
        grid=(rows // TILE,),
        out_shape=jax.ShapeDtypeStruct(matrix.shape, F32),
        in_specs=[pl.BlockSpec(memory_space=pltpu.SMEM), tile] + [vmem] * 5,
        out_specs=tile,
        scratch_shapes=[
            pltpu.VMEM((SPAN, width), BF16),
            pltpu.VMEM((SPAN, width), BF16),
            pltpu.VMEM((SPAN, SPAN), BF16),
            pltpu.VMEM((SPAN, SPAN), BF16),
        ],
        compiler_params=pltpu.CompilerParams(vmem_limit_bytes=56 * 2**20),
    )(place, matrix, own, other, cols, upper, inverse)


def send(value, axis, pairs):
    return lax.ppermute(value, axis, pairs)


def shift(value, axis, step):
    size = lax.axis_size(axis)
    return lax.ppermute(value, axis, [(i, (i + step) % size) for i in range(size)])


def swap(value):
    return lax.ppermute(value, "core", [(0, 1), (1, 0)])


def shards(matrix):
    y, x = lax.axis_index("y"), lax.axis_index("x")
    z, c = lax.axis_index("z"), lax.axis_index("core")
    place = jnp.stack([y, x, z, c]).astype(jnp.int32)
    depth = lax.axis_size("z")

    head = matrix[:BLOCK, :BLOCK]
    got = {m: send(head, "z", [(0, m), (1, (m + 1) % depth)]) for m in range(1, depth)}
    first, second = head, head
    for m in range(1, depth):
        first = jnp.where(z == m, got[m], first)
        second = jnp.where(z == (m + 1) % depth, got[m], second)
    pair = jnp.concatenate([first, second], 1)
    for m, value in enumerate([send(pair, "y", [(0, m)]) for m in (1, 2, 3)], 1):
        pair = jnp.where(y == m, value, pair)
    own = [pair] + [shift(pair, "x", s) for s in (1, 2, 3)]
    other = [swap(value) for value in own]
    upper, inverse = factor_head(place, own, other)

    lead = matrix[:, :BLOCK]
    quarter = lead.shape[0] // 4
    mine = lead[:quarter]
    for m in (1, 2, 3):
        value = send(lead[m * quarter : (m + 1) * quarter], "z", [(0, depth - m), (1, 1 + m)])
        mine = jnp.where((z == depth - m) | (z == 1 + m), value, mine)
    rows = jnp.stack([mine] + [shift(mine, "z", s) for s in range(1, depth)])
    rows_other = swap(rows)

    top = matrix[:BLOCK]
    slab = BLOCK // 4
    part = top[:slab]
    for m in (1, 2, 3):
        value = send(top[m * slab : (m + 1) * slab], "y", [(0, m)])
        part = jnp.where(y == m, value, part)
    cols = lax.all_gather(part, ("y", "x")).reshape(4, 4, slab, top.shape[1])
    cols = cols.reshape(4, 4, slab, top.shape[1])
    return update(place, matrix, rows, rows_other, cols, upper, inverse)


def solution(mesh):
    grid = Mesh(mesh.devices.reshape(4, 4, 8, 2), ("y", "x", "z", "core"))
    spec = P(("y", "x"), ("z", "core"))
    return jax.shard_map(shards, mesh=grid, in_specs=(spec,), out_specs=spec, check_vma=False)
```

time: 1390 us -> 190 us (0.14)
  waiting for transfers between devices: 1200 us -> 50.1 us
  other arithmetic: 107 us -> 3.52 us
  starting transfers between devices: 1.62 us -> 74.4 us
  Pallas kernels: 0 us -> 41.8 us
  matrix products: 38.3 us -> 0 us
  local copies, waits for them, and re-layouts: 22.5 us -> 6.01 us
    psum x12 -> x0, waiting for transfers between devices: 1200 us -> none  [spread(): return lax.psum(jnp.where(mine, shard, jnp.zeros_like(shard)), axis)]
    another operation x17 -> x1, other arithmetic: 89.6 us -> 0.08 us  [shards(): place = jnp.stack([y, x, z, c]).astype(jnp.int32)]
    ppermute x0 -> x31, starting transfers between devices: none -> 74.4 us  [the longest x16 45.5 us: send(): return lax.ppermute(value, axis, pairs)]
    ppermute x0 -> x31, waiting for transfers between devices: none -> 50.1 us  [the longest x10 41 us: shift(): lax.ppermute(value, axis, [(i, (i + step) % size) for i in range(size)])]
    pallas_call x0 -> x2, Pallas kernels: none -> 41.8 us  [the longest x1 29.2 us: factor_head(): pl.pallas_call(head_kernel, out_shape=[shape, shape], in_specs=[pl.BlockS...]
    dot_general x8 -> x0, matrix products: 34.7 us -> none  [right_product(): lax.dot_general(left, right, (((1,), (1,)), ((), ())), precision=lax.Prec...]
  transfers between devices with their start and end apart: 12 -> 32, of which waited for: 12 -> 12; matrix products, arithmetic and copies ran while one was open for 0% -> 2% of each run, Pallas kernels for 0% -> 15%
where the time goes in v1:
time: 190 us
  starting transfers between devices  74.4 us (39%)
  waiting for transfers between devices  50.1 us (26%)
  Pallas kernels  41.8 us (22%)
  between operations  13.8 us (7%)
  local copies, waits for them, and re-layouts  6.01 us (3%)
  other arithmetic  3.52 us (2%)
    ppermute x16, starting transfers between devices, send(): return lax.ppermute(value, axis, pairs)  45.5 us
    ppermute x10, waiting for transfers between devices, shift(): lax.ppermute(value, axis, [(i, (i + step) % size) for i in range(size)])  41 us
    pallas_call x1, Pallas kernels, factor_head(): pl.pallas_call(head_kernel, out_shape=[shape, shape], in_specs=[pl.BlockS...  29.2 us
    ppermute x5, starting transfers between devices, swap(): return lax.ppermute(value, 'core', [(0, 1), (1, 0)])  18.9 us
    pallas_call x1, Pallas kernels, update(): pl.pallas_call(update_kernel, grid=(rows // TILE,), out_shape=jax.ShapeDt...  12.6 us
    ppermute x10, starting transfers between devices, shift(): lax.ppermute(value, axis, [(i, (i + step) % size) for i in range(size)])  10 us
    ppermute x16, waiting for transfers between devices, send(): return lax.ppermute(value, axis, pairs)  8.24 us
  transfers between devices with their start and end apart: 32, of which 12 were waited for; matrix products, arithmetic and copies ran while one was open for 2% of the time, Pallas kernels for 15%

profile of v1, /device:TPU:1, one launch (start us, length us, event | category | flops | bytes accessed | tf_op | source)
XLA Modules:
  0.0 189.6 jit_solution(9229033276213959444)
XLA Ops:
  6.5 1.1 fusion
  7.6 4.0 %collective-permute-start.13 = (f32[32,1024]{1,0:T(8,128)S(1)}, f32[32,1024]{1,0:T(8,128)S(1)}, u32[]{:S(2)}, u32[]{:S(2)}) collective-permute-start(f32[32,1024]{1,0:T(8,128)S(1)} %get-tuple-element.13), channel_id=1, source_target_pairs={{0,64},{1,65},{2,66},{3,67},{4,68},{5,69},{6,70},{7,71},{8,72},{9,... | collective-permute-start | bytes 393224 | tf_op jit(solution)/shard_map/ppermute | solution.py:203
  11.6 2.3 %collective-permute-start.12 = (f32[32,1024]{1,0:T(8,128)S(1)}, f32[32,1024]{1,0:T(8,128)S(1)}, u32[]{:S(2)}, u32[]{:S(2)}) collective-permute-start(f32[32,1024]{1,0:T(8,128)S(1)} %get-tuple-element.14), channel_id=1, source_target_pairs={{0,128},{1,129},{2,130},{3,131},{4,132},{5,133},{6,134},{7,135},{8... | collective-permute-start | bytes 393224 | tf_op jit(solution)/shard_map/ppermute | solution.py:203
  13.9 1.3 collective-permute-start.11
  15.3 0.0 collective-permute-done.13
  15.3 1.8 collective-permute-done.12
  17.1 0.3 collective-permute-done.11
  17.4 1.6 select_select_fusion.1
  19.0 0.0 all-gather.3.cloned.1.call-update
  19.0 1.1 fusion.1
  20.1 7.5 %collective-permute-start.2 = (f32[256,128]{1,0:T(8,128)S(1)}, f32[256,128]{1,0:T(8,128)S(1)}, u32[]{:S(2)}, u32[]{:S(2)}) collective-permute-start(f32[256,128]{1,0:T(8,128)S(1)} %get-tuple-element.16), channel_id=1, source_target_pairs={{0,14},{2,4},{1,15},{3,5},{16,30},{18,20},{17,31},{19,21},{32,46},... | collective-permute-start | bytes 393224 | tf_op jit(solution)/shard_map/ppermute | solution.py:203
  27.6 1.3 collective-permute-start.1
  28.9 1.3 collective-permute-start
  30.2 1.4 collective-permute-done.1
  31.6 2.8 %collective-permute-done = f32[256,128]{1,0:T(8,128)S(1)} collective-permute-done((f32[256,128]{1,0:T(8,128)S(1)}, f32[256,128]{1,0:T(8,128)S(1)}, u32[]{:S(2)}, u32[]{:S(2)}) %collective-permute-start) | collective-permute-done | bytes 131104 | tf_op jit(solution)/shard_map/ppermute | solution.py:203
  34.4 0.9 bitcast_dynamic-update-slice_fusion.7
  35.3 0.1 collective-permute-start.3
  35.4 0.8 slice.45
  36.3 1.3 collective-permute-start.20
  37.6 1.3 collective-permute-start.19
  38.9 5.7 %collective-permute-start.18 = (f32[128,128]{1,0:T(8,128)S(1)}, f32[128,128]{1,0:T(8,128)S(1)}, u32[]{:S(2)}, u32[]{:S(2)}) collective-permute-start(f32[128,128]{1,0:T(8,128)S(1)} %slice.45), channel_id=1, source_target_pairs={{0,6},{2,8},{1,7},{3,9},{16,22},{18,24},{17,23},{19,25},{32,38},{3... | collective-permute-start | bytes 196616 | tf_op jit(solution)/shard_map/ppermute | solution.py:203
  44.6 2.3 %collective-permute-start.17 = (f32[128,128]{1,0:T(8,128)S(1)}, f32[128,128]{1,0:T(8,128)S(1)}, u32[]{:S(2)}, u32[]{:S(2)}) collective-permute-start(f32[128,128]{1,0:T(8,128)S(1)} %slice.45), channel_id=1, source_target_pairs={{0,8},{2,10},{1,9},{3,11},{16,24},{18,26},{17,25},{19,27},{32,40},... | collective-permute-start | bytes 196616 | tf_op jit(solution)/shard_map/ppermute | solution.py:203
  46.9 0.1 collective-permute-start.4
  47.0 6.0 %collective-permute-done.4 = f32[256,128]{1,0:T(8,128)S(1)} collective-permute-done((f32[256,128]{1,0:T(8,128)S(1)}, f32[256,128]{1,0:T(8,128)S(1)}, u32[]{:S(2)}, u32[]{:S(2)}) %collective-permute-start.4) | collective-permute-done | bytes 131104 | tf_op jit(solution)/shard_map/ppermute | solution.py:208
  53.0 5.6 %collective-permute-start.5 = (f32[256,128]{1,0:T(8,128)S(1)}, f32[256,128]{1,0:T(8,128)S(1)}, u32[]{:S(2)}, u32[]{:S(2)}) collective-permute-start(f32[256,128]{1,0:T(8,128)S(1)} %get-tuple-element.10), channel_id=1, source_target_pairs={{0,6},{2,8},{4,10},{6,12},{8,14},{10,0},{12,2},{14,4},{1,7},{3,9},... | collective-permute-start | bytes 393224 | tf_op jit(solution)/shard_map/ppermute | solution.py:208
  58.6 8.6 %collective-permute-done.5 = f32[256,128]{1,0:T(8,128)S(1)} collective-permute-done((f32[256,128]{1,0:T(8,128)S(1)}, f32[256,128]{1,0:T(8,128)S(1)}, u32[]{:S(2)}, u32[]{:S(2)}) %collective-permute-start.5) | collective-permute-done | bytes 131104 | tf_op jit(solution)/shard_map/ppermute | solution.py:208
  67.2 11.0 %collective-permute-done.6 = f32[256,128]{1,0:T(8,128)S(1)} collective-permute-done((f32[256,128]{1,0:T(8,128)S(1)}, f32[256,128]{1,0:T(8,128)S(1)}, u32[]{:S(2)}, u32[]{:S(2)}) %collective-permute-start.6) | collective-permute-done | bytes 131104 | tf_op jit(solution)/shard_map/ppermute | solution.py:208
  78.2 0.0 collective-permute-start.7
  78.2 9.5 %collective-permute-done.7 = f32[256,128]{1,0:T(8,128)S(1)} collective-permute-done((f32[256,128]{1,0:T(8,128)S(1)}, f32[256,128]{1,0:T(8,128)S(1)}, u32[]{:S(2)}, u32[]{:S(2)}) %collective-permute-start.7) | collective-permute-done | bytes 131104 | tf_op jit(solution)/shard_map/ppermute | solution.py:208
  87.8 0.0 collective-permute-start.8
  87.8 5.8 %collective-permute-done.8 = f32[256,128]{1,0:T(8,128)S(1)} collective-permute-done((f32[256,128]{1,0:T(8,128)S(1)}, f32[256,128]{1,0:T(8,128)S(1)}, u32[]{:S(2)}, u32[]{:S(2)}) %collective-permute-start.8) | collective-permute-done | bytes 131104 | tf_op jit(solution)/shard_map/ppermute | solution.py:208
  93.6 0.6 collective-permute-start.9
  94.2 4.7 %collective-permute-start.16 = (f32[128,128]{1,0:T(8,128)S(1)}, f32[128,128]{1,0:T(8,128)S(1)}, u32[]{:S(2)}, u32[]{:S(2)}) collective-permute-start(f32[128,128]{1,0:T(8,128)S(1)} %slice.45), channel_id=1, source_target_pairs={{0,10},{2,12},{1,11},{3,13},{16,26},{18,28},{17,27},{19,29},{32,42... | collective-permute-start | bytes 196616 | tf_op jit(solution)/shard_map/ppermute | solution.py:203
  99.0 0.0 collective-permute-done.19
  99.0 1.6 collective-permute-start.15
  100.6 0.0 collective-permute-done.9
  100.6 1.9 %collective-permute-start.14 = (f32[128,128]{1,0:T(8,128)S(1)}, f32[128,128]{1,0:T(8,128)S(1)}, u32[]{:S(2)}, u32[]{:S(2)}) collective-permute-start(f32[128,128]{1,0:T(8,128)S(1)} %slice.45), channel_id=1, source_target_pairs={{0,14},{2,0},{1,15},{3,1},{16,30},{18,16},{17,31},{19,17},{32,46},... | collective-permute-start | bytes 196616 | tf_op jit(solution)/shard_map/ppermute | solution.py:203
  102.5 0.0 collective-permute-done.18
  102.5 7.4 %collective-permute-start.10 = (f32[8,256,128]{2,1,0:T(8,128)S(1)}, f32[8,256,128]{2,1,0:T(8,128)S(1)}, u32[]{:S(2)}, u32[]{:S(2)}) collective-permute-start(f32[8,256,128]{2,1,0:T(8,128)S(1)} %bitcast_dynamic-update-slice_fusion.own), channel_id=1, source_target_pairs={{0,1},{1,0},{2,3},{3,2},{4,5},{5,4},{6,7},{7,6},{8,9},{9,8},{10,11... | collective-permute-start | bytes 3145736 | tf_op jit(solution)/shard_map/ppermute | solution.py:212
  109.9 0.0 collective-permute-done.17
  109.9 0.0 collective-permute-done.16
  109.9 0.0 collective-permute-done.15
  109.9 0.9 select_select_fusion.4
  110.8 1.3 collective-permute-start.23
  112.1 6.4 %collective-permute-start.22 = (f32[128,256]{1,0:T(8,128)S(1)}, f32[128,256]{1,0:T(8,128)S(1)}, u32[]{:S(2)}, u32[]{:S(2)}) collective-permute-start(f32[128,256]{1,0:T(8,128)S(1)} %pad_maximum_fusion), channel_id=1, source_target_pairs={{0,128},{1,129},{2,130},{3,131},{4,132},{5,133},{6,134},{7,135},{8... | collective-permute-start | bytes 393224 | tf_op jit(solution)/shard_map/ppermute | solution.py:203
  118.5 1.3 collective-permute-start.21
  119.8 0.0 collective-permute-done.23
  119.8 0.6 collective-permute-done.22
  120.4 1.3 collective-permute-done.21
  121.8 2.6 %collective-permute-start.26 = (f32[128,256]{1,0:T(8,128)S(1)}, f32[128,256]{1,0:T(8,128)S(1)}, u32[]{:S(2)}, u32[]{:S(2)}) collective-permute-start(f32[128,256]{1,0:T(8,128)S(1)} %select_select_fusion.r0), channel_id=1, source_target_pairs={{0,48},{16,0},{32,16},{48,32},{1,49},{17,1},{33,17},{49,33},{2,50}... | collective-permute-start | bytes 393224 | tf_op jit(solution)/shard_map/ppermute | solution.py:208
  124.3 0.5 collective-permute-start.25
  124.8 0.6 collective-permute-start.24
  125.4 5.3 %collective-permute-start.27 = (f32[128,256]{1,0:T(8,128)S(1)}, f32[128,256]{1,0:T(8,128)S(1)}, u32[]{:S(2)}, u32[]{:S(2)}) collective-permute-start(f32[128,256]{1,0:T(8,128)S(1)} %select_select_fusion.r0), channel_id=1, source_target_pairs={{0,1},{1,0},{2,3},{3,2},{4,5},{5,4},{6,7},{7,6},{8,9},{9,8},{10,11... | collective-permute-start | bytes 393224 | tf_op jit(solution)/shard_map/ppermute | solution.py:212
  130.8 2.2 %collective-permute-start.30 = (f32[128,256]{1,0:T(8,128)S(1)}, f32[128,256]{1,0:T(8,128)S(1)}, u32[]{:S(2)}, u32[]{:S(2)}) collective-permute-start(f32[128,256]{1,0:T(8,128)S(1)} %collective-permute-done.26.r3), channel_id=1, source_target_pairs={{0,1},{1,0},{2,3},{3,2},{4,5},{5,4},{6,7},{7,6},{8,9},{9,8},{10,11... | collective-permute-start | bytes 393224 | tf_op jit(solution)/shard_map/ppermute | solution.py:212
  133.0 2.6 %collective-permute-start.29 = (f32[128,256]{1,0:T(8,128)S(1)}, f32[128,256]{1,0:T(8,128)S(1)}, u32[]{:S(2)}, u32[]{:S(2)}) collective-permute-start(f32[128,256]{1,0:T(8,128)S(1)} %collective-permute-done.25.r2), channel_id=1, source_target_pairs={{0,1},{1,0},{2,3},{3,2},{4,5},{5,4},{6,7},{7,6},{8,9},{9,8},{10,11... | collective-permute-start | bytes 393224 | tf_op jit(solution)/shard_map/ppermute | solution.py:212
  135.6 0.0 collective-permute-done.24.r1
  135.6 1.3 collective-permute-start.28
  136.9 0.1 pad_add_fusion.place
  137.0 0.9 collective-permute-done.28.o1
  137.9 29.2 %shard_map.17 = (f32[512,512]{1,0:T(8,128)S(1)}, f32[512,512]{1,0:T(8,128)S(1)}) custom-call(s32[4]{0:T(128)S(1)} %pad_add_fusion.place, f32[128,256]{1,0:T(8,128)S(1)} %select_select_fusion.r0, f32[128,256]{1,0:T(8,128)S(1)} %collective-permute-done.24.r1, f32[128,256]{1,0:T(8,128)S(1)} %collective-permute-done.25.r2, ...), custom_call_target="tpu_custom_call" | custom-call | tf_op jit(solution)/shard_map/pallas_call | solution.py:128
  167.2 1.0 copy-done
  168.1 1.0 copy-done.1
  169.2 1.0 copy-done.4
  170.1 12.6 %shard_map.18 = f32[1024,1024]{1,0:T(8,128)} custom-call(s32[4]{0:T(128)} %copy-done.2, f32[1024,1024]{1,0:T(8,128)} %a_ref.1, f32[8,256,128]{2,1,0:T(8,128)} %copy-done.3, f32[8,256,128]{2,1,0:T(8,128)} %copy-done.4, f32[4,4,32,1024]{3,2,1,0:T(8,128)} %bitcast.21, f32[512,512]{1,0:T(8,128)} %copy-done, f32[512,512]{1,0:T(8,128)} %copy-done.1), custom_call_target="tpu_custom_call" | custom-call | tf_op jit(solution)/shard_map/pallas_call | solution.py:186
  (29 shorter events, 0.2 us)
Async XLA Ops:
  6.5 162.6 %all-gather.3.cloned.1.call-start = ((), (), s32[]{:S(2)}) async-start(), calls=%async_computation | async-start | bytes 2228224 | tf_op jit(solution)/shard_map/all_gather | solution.py:249
  7.6 7.7 %collective-permute-start.13 = (f32[32,1024]{1,0:T(8,128)S(1)}, f32[32,1024]{1,0:T(8,128)S(1)}, u32[]{:S(2)}, u32[]{:S(2)}) collective-permute-start(f32[32,1024]{1,0:T(8,128)S(1)} %get-tuple-element.13), channel_id=1, source_target_pairs={{0,64},{1,65},{2,66},{3,67},{4,68},{5,69},{6,70},{7,71},{8,72},{9,... | collective-permute-start | bytes 393224 | tf_op jit(solution)/shard_map/ppermute | solution.py:203
  11.6 5.5 %collective-permute-start.12 = (f32[32,1024]{1,0:T(8,128)S(1)}, f32[32,1024]{1,0:T(8,128)S(1)}, u32[]{:S(2)}, u32[]{:S(2)}) collective-permute-start(f32[32,1024]{1,0:T(8,128)S(1)} %get-tuple-element.14), channel_id=1, source_target_pairs={{0,128},{1,129},{2,130},{3,131},{4,132},{5,133},{6,134},{7,135},{8... | collective-permute-start | bytes 393224 | tf_op jit(solution)/shard_map/ppermute | solution.py:203
  13.9 3.4 %collective-permute-start.11 = (f32[32,1024]{1,0:T(8,128)S(1)}, f32[32,1024]{1,0:T(8,128)S(1)}, u32[]{:S(2)}, u32[]{:S(2)}) collective-permute-start(f32[32,1024]{1,0:T(8,128)S(1)} %get-tuple-element.15), channel_id=1, source_target_pairs={{0,192},{1,193},{2,194},{3,195},{4,196},{5,197},{6,198},{7,199},{8... | collective-permute-start | bytes 393224 | tf_op jit(solution)/shard_map/ppermute | solution.py:203
  20.1 10.1 %collective-permute-start.2 = (f32[256,128]{1,0:T(8,128)S(1)}, f32[256,128]{1,0:T(8,128)S(1)}, u32[]{:S(2)}, u32[]{:S(2)}) collective-permute-start(f32[256,128]{1,0:T(8,128)S(1)} %get-tuple-element.16), channel_id=1, source_target_pairs={{0,14},{2,4},{1,15},{3,5},{16,30},{18,20},{17,31},{19,21},{32,46},... | collective-permute-start | bytes 393224 | tf_op jit(solution)/shard_map/ppermute | solution.py:203
  27.6 4.0 %collective-permute-start.1 = (f32[256,128]{1,0:T(8,128)S(1)}, f32[256,128]{1,0:T(8,128)S(1)}, u32[]{:S(2)}, u32[]{:S(2)}) collective-permute-start(f32[256,128]{1,0:T(8,128)S(1)} %get-tuple-element.17), channel_id=1, source_target_pairs={{0,12},{2,6},{1,13},{3,7},{16,28},{18,22},{17,29},{19,23},{32,44},... | collective-permute-start | bytes 393224 | tf_op jit(solution)/shard_map/ppermute | solution.py:203
  28.9 5.5 %collective-permute-start = (f32[256,128]{1,0:T(8,128)S(1)}, f32[256,128]{1,0:T(8,128)S(1)}, u32[]{:S(2)}, u32[]{:S(2)}) collective-permute-start(f32[256,128]{1,0:T(8,128)S(1)} %get-tuple-element.18), channel_id=1, source_target_pairs={{0,10},{2,8},{1,11},{3,9},{16,26},{18,24},{17,27},{19,25},{32,42},... | collective-permute-start | bytes 393224 | tf_op jit(solution)/shard_map/ppermute | solution.py:203
  35.3 11.6 %collective-permute-start.3 = (f32[256,128]{1,0:T(8,128)S(1)}, f32[256,128]{1,0:T(8,128)S(1)}, u32[]{:S(2)}, u32[]{:S(2)}) collective-permute-start(f32[256,128]{1,0:T(8,128)S(1)} %get-tuple-element.10), channel_id=1, source_target_pairs={{0,2},{2,4},{4,6},{6,8},{8,10},{10,12},{12,14},{14,0},{1,3},{3,5},... | collective-permute-start | bytes 393224 | tf_op jit(solution)/shard_map/ppermute | solution.py:208
  36.3 57.9 %collective-permute-start.20 = (f32[128,128]{1,0:T(8,128)S(1)}, f32[128,128]{1,0:T(8,128)S(1)}, u32[]{:S(2)}, u32[]{:S(2)}) collective-permute-start(f32[128,128]{1,0:T(8,128)S(1)} %slice.45), channel_id=1, source_target_pairs={{0,2},{2,4},{1,3},{3,5},{16,18},{18,20},{17,19},{19,21},{32,34},{3... | collective-permute-start | bytes 196616 | tf_op jit(solution)/shard_map/ppermute | solution.py:203
  37.6 61.4 %collective-permute-start.19 = (f32[128,128]{1,0:T(8,128)S(1)}, f32[128,128]{1,0:T(8,128)S(1)}, u32[]{:S(2)}, u32[]{:S(2)}) collective-permute-start(f32[128,128]{1,0:T(8,128)S(1)} %slice.45), channel_id=1, source_target_pairs={{0,4},{2,6},{1,5},{3,7},{16,20},{18,22},{17,21},{19,23},{32,36},{3... | collective-permute-start | bytes 196616 | tf_op jit(solution)/shard_map/ppermute | solution.py:203
  38.9 63.7 %collective-permute-start.18 = (f32[128,128]{1,0:T(8,128)S(1)}, f32[128,128]{1,0:T(8,128)S(1)}, u32[]{:S(2)}, u32[]{:S(2)}) collective-permute-start(f32[128,128]{1,0:T(8,128)S(1)} %slice.45), channel_id=1, source_target_pairs={{0,6},{2,8},{1,7},{3,9},{16,22},{18,24},{17,23},{19,25},{32,38},{3... | collective-permute-start | bytes 196616 | tf_op jit(solution)/shard_map/ppermute | solution.py:203
  44.6 65.3 %collective-permute-start.17 = (f32[128,128]{1,0:T(8,128)S(1)}, f32[128,128]{1,0:T(8,128)S(1)}, u32[]{:S(2)}, u32[]{:S(2)}) collective-permute-start(f32[128,128]{1,0:T(8,128)S(1)} %slice.45), channel_id=1, source_target_pairs={{0,8},{2,10},{1,9},{3,11},{16,24},{18,26},{17,25},{19,27},{32,40},... | collective-permute-start | bytes 196616 | tf_op jit(solution)/shard_map/ppermute | solution.py:203
  46.9 6.1 %collective-permute-start.4 = (f32[256,128]{1,0:T(8,128)S(1)}, f32[256,128]{1,0:T(8,128)S(1)}, u32[]{:S(2)}, u32[]{:S(2)}) collective-permute-start(f32[256,128]{1,0:T(8,128)S(1)} %get-tuple-element.10), channel_id=1, source_target_pairs={{0,4},{2,6},{4,8},{6,10},{8,12},{10,14},{12,0},{14,2},{1,5},{3,7},... | collective-permute-start | bytes 393224 | tf_op jit(solution)/shard_map/ppermute | solution.py:208
  53.0 14.2 %collective-permute-start.5 = (f32[256,128]{1,0:T(8,128)S(1)}, f32[256,128]{1,0:T(8,128)S(1)}, u32[]{:S(2)}, u32[]{:S(2)}) collective-permute-start(f32[256,128]{1,0:T(8,128)S(1)} %get-tuple-element.10), channel_id=1, source_target_pairs={{0,6},{2,8},{4,10},{6,12},{8,14},{10,0},{12,2},{14,4},{1,7},{3,9},... | collective-permute-start | bytes 393224 | tf_op jit(solution)/shard_map/ppermute | solution.py:208
  67.2 11.0 %collective-permute-start.6 = (f32[256,128]{1,0:T(8,128)S(1)}, f32[256,128]{1,0:T(8,128)S(1)}, u32[]{:S(2)}, u32[]{:S(2)}) collective-permute-start(f32[256,128]{1,0:T(8,128)S(1)} %get-tuple-element.10), channel_id=1, source_target_pairs={{0,8},{2,10},{4,12},{6,14},{8,0},{10,2},{12,4},{14,6},{1,9},{3,11}... | collective-permute-start | bytes 393224 | tf_op jit(solution)/shard_map/ppermute | solution.py:208
  78.2 9.5 %collective-permute-start.7 = (f32[256,128]{1,0:T(8,128)S(1)}, f32[256,128]{1,0:T(8,128)S(1)}, u32[]{:S(2)}, u32[]{:S(2)}) collective-permute-start(f32[256,128]{1,0:T(8,128)S(1)} %get-tuple-element.10), channel_id=1, source_target_pairs={{0,10},{2,12},{4,14},{6,0},{8,2},{10,4},{12,6},{14,8},{1,11},{3,13... | collective-permute-start | bytes 393224 | tf_op jit(solution)/shard_map/ppermute | solution.py:208
  87.8 5.9 %collective-permute-start.8 = (f32[256,128]{1,0:T(8,128)S(1)}, f32[256,128]{1,0:T(8,128)S(1)}, u32[]{:S(2)}, u32[]{:S(2)}) collective-permute-start(f32[256,128]{1,0:T(8,128)S(1)} %get-tuple-element.10), channel_id=1, source_target_pairs={{0,12},{2,14},{4,0},{6,2},{8,4},{10,6},{12,8},{14,10},{1,13},{3,15... | collective-permute-start | bytes 393224 | tf_op jit(solution)/shard_map/ppermute | solution.py:208
  93.6 6.9 %collective-permute-start.9 = (f32[256,128]{1,0:T(8,128)S(1)}, f32[256,128]{1,0:T(8,128)S(1)}, u32[]{:S(2)}, u32[]{:S(2)}) collective-permute-start(f32[256,128]{1,0:T(8,128)S(1)} %get-tuple-element.10), channel_id=1, source_target_pairs={{0,14},{2,0},{4,2},{6,4},{8,6},{10,8},{12,10},{14,12},{1,15},{3,1}... | collective-permute-start | bytes 393224 | tf_op jit(solution)/shard_map/ppermute | solution.py:208
  94.2 15.7 %collective-permute-start.16 = (f32[128,128]{1,0:T(8,128)S(1)}, f32[128,128]{1,0:T(8,128)S(1)}, u32[]{:S(2)}, u32[]{:S(2)}) collective-permute-start(f32[128,128]{1,0:T(8,128)S(1)} %slice.45), channel_id=1, source_target_pairs={{0,10},{2,12},{1,11},{3,13},{16,26},{18,28},{17,27},{19,29},{32,42... | collective-permute-start | bytes 196616 | tf_op jit(solution)/shard_map/ppermute | solution.py:203
  99.0 10.9 %collective-permute-start.15 = (f32[128,128]{1,0:T(8,128)S(1)}, f32[128,128]{1,0:T(8,128)S(1)}, u32[]{:S(2)}, u32[]{:S(2)}) collective-permute-start(f32[128,128]{1,0:T(8,128)S(1)} %slice.45), channel_id=1, source_target_pairs={{0,12},{2,14},{1,13},{3,15},{16,28},{18,30},{17,29},{19,31},{32,44... | collective-permute-start | bytes 196616 | tf_op jit(solution)/shard_map/ppermute | solution.py:203
  100.6 9.4 %collective-permute-start.14 = (f32[128,128]{1,0:T(8,128)S(1)}, f32[128,128]{1,0:T(8,128)S(1)}, u32[]{:S(2)}, u32[]{:S(2)}) collective-permute-start(f32[128,128]{1,0:T(8,128)S(1)} %slice.45), channel_id=1, source_target_pairs={{0,14},{2,0},{1,15},{3,1},{16,30},{18,16},{17,31},{19,17},{32,46},... | collective-permute-start | bytes 196616 | tf_op jit(solution)/shard_map/ppermute | solution.py:203
  102.5 66.6 %copy-start.3 = (f32[8,256,128]{2,1,0:T(8,128)}, f32[8,256,128]{2,1,0:T(8,128)S(1)}, u32[]{:S(2)}) copy-start(f32[8,256,128]{2,1,0:T(8,128)S(1)} %bitcast_dynamic-update-slice_fusion.own) | copy-start | bytes 3145732
  102.5 66.6 %collective-permute-start.10 = (f32[8,256,128]{2,1,0:T(8,128)S(1)}, f32[8,256,128]{2,1,0:T(8,128)S(1)}, u32[]{:S(2)}, u32[]{:S(2)}) collective-permute-start(f32[8,256,128]{2,1,0:T(8,128)S(1)} %bitcast_dynamic-update-slice_fusion.own), channel_id=1, source_target_pairs={{0,1},{1,0},{2,3},{3,2},{4,5},{5,4},{6,7},{7,6},{8,9},{9,8},{10,11... | collective-permute-start | bytes 3145736 | tf_op jit(solution)/shard_map/ppermute | solution.py:212
  110.8 9.0 %collective-permute-start.23 = (f32[128,256]{1,0:T(8,128)S(1)}, f32[128,256]{1,0:T(8,128)S(1)}, u32[]{:S(2)}, u32[]{:S(2)}) collective-permute-start(f32[128,256]{1,0:T(8,128)S(1)} %pad_maximum_fusion), channel_id=1, source_target_pairs={{0,64},{1,65},{2,66},{3,67},{4,68},{5,69},{6,70},{7,71},{8,72},{9,... | collective-permute-start | bytes 393224 | tf_op jit(solution)/shard_map/ppermute | solution.py:203
  112.1 8.3 %collective-permute-start.22 = (f32[128,256]{1,0:T(8,128)S(1)}, f32[128,256]{1,0:T(8,128)S(1)}, u32[]{:S(2)}, u32[]{:S(2)}) collective-permute-start(f32[128,256]{1,0:T(8,128)S(1)} %pad_maximum_fusion), channel_id=1, source_target_pairs={{0,128},{1,129},{2,130},{3,131},{4,132},{5,133},{6,134},{7,135},{8... | collective-permute-start | bytes 393224 | tf_op jit(solution)/shard_map/ppermute | solution.py:203
  118.5 3.2 %collective-permute-start.21 = (f32[128,256]{1,0:T(8,128)S(1)}, f32[128,256]{1,0:T(8,128)S(1)}, u32[]{:S(2)}, u32[]{:S(2)}) collective-permute-start(f32[128,256]{1,0:T(8,128)S(1)} %pad_maximum_fusion), channel_id=1, source_target_pairs={{0,192},{1,193},{2,194},{3,195},{4,196},{5,197},{6,198},{7,199},{8... | collective-permute-start | bytes 393224 | tf_op jit(solution)/shard_map/ppermute | solution.py:203
  121.8 9.0 %collective-permute-start.26 = (f32[128,256]{1,0:T(8,128)S(1)}, f32[128,256]{1,0:T(8,128)S(1)}, u32[]{:S(2)}, u32[]{:S(2)}) collective-permute-start(f32[128,256]{1,0:T(8,128)S(1)} %select_select_fusion.r0), channel_id=1, source_target_pairs={{0,48},{16,0},{32,16},{48,32},{1,49},{17,1},{33,17},{49,33},{2,50}... | collective-permute-start | bytes 393224 | tf_op jit(solution)/shard_map/ppermute | solution.py:208
  124.3 8.7 %collective-permute-start.25 = (f32[128,256]{1,0:T(8,128)S(1)}, f32[128,256]{1,0:T(8,128)S(1)}, u32[]{:S(2)}, u32[]{:S(2)}) collective-permute-start(f32[128,256]{1,0:T(8,128)S(1)} %select_select_fusion.r0), channel_id=1, source_target_pairs={{0,32},{16,48},{32,0},{48,16},{1,33},{17,49},{33,1},{49,17},{2,34}... | collective-permute-start | bytes 393224 | tf_op jit(solution)/shard_map/ppermute | solution.py:208
  124.8 10.8 %collective-permute-start.24 = (f32[128,256]{1,0:T(8,128)S(1)}, f32[128,256]{1,0:T(8,128)S(1)}, u32[]{:S(2)}, u32[]{:S(2)}) collective-permute-start(f32[128,256]{1,0:T(8,128)S(1)} %select_select_fusion.r0), channel_id=1, source_target_pairs={{0,16},{16,32},{32,48},{48,0},{1,17},{17,33},{33,49},{49,1},{2,18}... | collective-permute-start | bytes 393224 | tf_op jit(solution)/shard_map/ppermute | solution.py:208
  125.4 11.6 %collective-permute-start.27 = (f32[128,256]{1,0:T(8,128)S(1)}, f32[128,256]{1,0:T(8,128)S(1)}, u32[]{:S(2)}, u32[]{:S(2)}) collective-permute-start(f32[128,256]{1,0:T(8,128)S(1)} %select_select_fusion.r0), channel_id=1, source_target_pairs={{0,1},{1,0},{2,3},{3,2},{4,5},{5,4},{6,7},{7,6},{8,9},{9,8},{10,11... | collective-permute-start | bytes 393224 | tf_op jit(solution)/shard_map/ppermute | solution.py:212
  130.8 6.3 %collective-permute-start.30 = (f32[128,256]{1,0:T(8,128)S(1)}, f32[128,256]{1,0:T(8,128)S(1)}, u32[]{:S(2)}, u32[]{:S(2)}) collective-permute-start(f32[128,256]{1,0:T(8,128)S(1)} %collective-permute-done.26.r3), channel_id=1, source_target_pairs={{0,1},{1,0},{2,3},{3,2},{4,5},{5,4},{6,7},{7,6},{8,9},{9,8},{10,11... | collective-permute-start | bytes 393224 | tf_op jit(solution)/shard_map/ppermute | solution.py:212
  133.0 4.0 %collective-permute-start.29 = (f32[128,256]{1,0:T(8,128)S(1)}, f32[128,256]{1,0:T(8,128)S(1)}, u32[]{:S(2)}, u32[]{:S(2)}) collective-permute-start(f32[128,256]{1,0:T(8,128)S(1)} %collective-permute-done.25.r2), channel_id=1, source_target_pairs={{0,1},{1,0},{2,3},{3,2},{4,5},{5,4},{6,7},{7,6},{8,9},{9,8},{10,11... | collective-permute-start | bytes 393224 | tf_op jit(solution)/shard_map/ppermute | solution.py:212
  135.6 2.3 %collective-permute-start.28 = (f32[128,256]{1,0:T(8,128)S(1)}, f32[128,256]{1,0:T(8,128)S(1)}, u32[]{:S(2)}, u32[]{:S(2)}) collective-permute-start(f32[128,256]{1,0:T(8,128)S(1)} %collective-permute-done.24.r1), channel_id=1, source_target_pairs={{0,1},{1,0},{2,3},{3,2},{4,5},{5,4},{6,7},{7,6},{8,9},{9,8},{10,11... | collective-permute-start | bytes 393224 | tf_op jit(solution)/shard_map/ppermute | solution.py:212
  137.0 32.1 %copy-start.2 = (s32[4]{0:T(128)}, s32[4]{0:T(128)S(1)}, u32[]{:S(2)}) copy-start(s32[4]{0:T(128)S(1)} %pad_add_fusion.place) | copy-start | bytes 52
  167.1 1.0 copy-start
  168.1 1.0 copy-start.1
  169.1 1.0 copy-start.4
Sparse Core Ops, SparseCore 0:
  19.1 53.4 all-gather.2

commit v2 on v1

--- a/solution.py
+++ b/solution.py
@@ -82,16 +82,13 @@
     return a, e
 
 
-def head_kernel(place, r0, r1, r2, r3, o0, o1, o2, o3, u_ref, v_ref):
+def head_kernel(place, own, other, u_ref, v_ref):
     x, c = place[1], place[3]
-    for step, (own, other) in enumerate(((r0, o0), (r1, o1), (r2, o2), (r3, o3))):
+    half = SPAN // 2
+    for step in range(PANELS):
         rows = pl.ds(pl.multiple_of(((x - step + PANELS) % PANELS) * BLOCK, BLOCK), BLOCK)
-        for half in range(2):
-            lanes = slice(half * BLOCK, (half + 1) * BLOCK)
-            mine = pl.ds(pl.multiple_of((c + 2 * half) * BLOCK, BLOCK), BLOCK)
-            theirs = pl.ds(pl.multiple_of((1 - c + 2 * half) * BLOCK, BLOCK), BLOCK)
-            u_ref[rows, mine] = own[:, lanes]
-            u_ref[rows, theirs] = other[:, lanes]
+        u_ref[rows, pl.ds(pl.multiple_of(c * half, half), half)] = own[step]
+        u_ref[rows, pl.ds(pl.multiple_of((1 - c) * half, half), half)] = other[step]
     row = lax.broadcasted_iota(jnp.int32, (BLOCK, BLOCK), 0)
     col = lax.broadcasted_iota(jnp.int32, (BLOCK, BLOCK), 1)
     eye = (row == col).astype(F32)
@@ -128,26 +125,37 @@
     return pl.pallas_call(
         head_kernel,
         out_shape=[shape, shape],
-        in_specs=[pl.BlockSpec(memory_space=pltpu.SMEM)] + [vmem] * 8,
+        in_specs=[pl.BlockSpec(memory_space=pltpu.SMEM), vmem, vmem],
         out_specs=[vmem, vmem],
+        cost_estimate=pl.CostEstimate(
+            flops=30_000_000_000, transcendentals=0, bytes_accessed=4 * 2**20
+        ),
         compiler_params=pltpu.CompilerParams(vmem_limit_bytes=48 * 2**20),
-    )(place, *own, *other)
+    )(place, own, other)
 
 
 TILE = 256
 
 
-def update_kernel(place, a_ref, own, other, cols, u_ref, v_ref, out_ref, w_hi, w_lo, v_hi, v_lo):
+def update_kernel(
+    place, a_ref, own, other, left0, left1, left2, left3, right0, right1, right2, right3, u_ref, v_ref,
+    out_ref, column, w_hi, w_lo, v_hi, v_lo,
+):
     y, x, z, c = place[0], place[1], place[2], place[3]
     t = pl.program_id(0)
 
     @pl.when(t == 0)
     def _():
-        values = cols[...]
-        column = jnp.concatenate(
-            [values[:, k].reshape(BLOCK, values.shape[-1]) for k in range(PANELS)], 0
-        )
-        high, low = split(split_dot(split(v_ref[...]), split(column), 1, 0))
+        slab, half = left0.shape[1:]
+        for i, (left, right) in enumerate(
+            ((left0, right0), (left1, right1), (left2, right2), (left3, right3))
+        ):
+            for j in range(4):
+                at = ((x - j + 4) % 4) * BLOCK + ((y - i + 4) % 4) * slab
+                column[pl.ds(pl.multiple_of(at, slab), slab), :half] = left[j]
+                at = ((x - i + 4) % 4) * BLOCK + ((y - j + 4) % 4) * slab
+                column[pl.ds(pl.multiple_of(at, slab), slab), half:] = right[j]
+        high, low = split(split_dot(split(v_ref[...]), split(column[...]), 1, 0))
         w_hi[...] = high
         w_lo[...] = low
         for slot, k in enumerate((c, c + 2, 1 - c, 3 - c)):
@@ -156,9 +164,7 @@
             v_hi[:, slot * BLOCK : (slot + 1) * BLOCK] = high
             v_lo[:, slot * BLOCK : (slot + 1) * BLOCK] = low
 
-    first = (z + t) % 8
-    second = (z - 1 - t + 8) % 8
-    rows = jnp.concatenate([own[first], own[second], other[first], other[second]], 1)
+    rows = jnp.concatenate([own[(8 - t) % 8], own[t + 1], other[(8 - t) % 8], other[t + 1]], 1)
     panel = split_dot(split(rows), (v_hi[...], v_lo[...]), 1, 1)
     out_ref[...] = a_ref[...] - split_dot(split(panel), (w_hi[...], w_lo[...]), 1, 0)
     q = 2 * z + c
@@ -179,7 +185,7 @@
         out_ref[:BLOCK, :BLOCK] = u_ref[at_row, at_col].T
 
 
-def update(place, matrix, own, other, cols, upper, inverse):
+def update(place, matrix, own, other, lefts, rights, upper, inverse):
     rows, width = matrix.shape
     vmem = pl.BlockSpec(memory_space=pltpu.VMEM)
     tile = pl.BlockSpec((TILE, width), lambda t: (t, 0))
@@ -187,16 +193,17 @@
         update_kernel,
         grid=(rows // TILE,),
         out_shape=jax.ShapeDtypeStruct(matrix.shape, F32),
-        in_specs=[pl.BlockSpec(memory_space=pltpu.SMEM), tile] + [vmem] * 5,
+        in_specs=[pl.BlockSpec(memory_space=pltpu.SMEM), tile] + [vmem] * 12,
         out_specs=tile,
         scratch_shapes=[
+            pltpu.VMEM((SPAN, width), F32),
             pltpu.VMEM((SPAN, width), BF16),
             pltpu.VMEM((SPAN, width), BF16),
             pltpu.VMEM((SPAN, SPAN), BF16),
             pltpu.VMEM((SPAN, SPAN), BF16),
         ],
         compiler_params=pltpu.CompilerParams(vmem_limit_bytes=56 * 2**20),
-    )(place, matrix, own, other, cols, upper, inverse)
+    )(place, matrix, own, other, *lefts, *rights, upper, inverse)
 
 
 def send(value, axis, pairs):
@@ -219,36 +226,45 @@
     depth = lax.axis_size("z")
 
     head = matrix[:BLOCK, :BLOCK]
-    got = {m: send(head, "z", [(0, m), (1, (m + 1) % depth)]) for m in range(1, depth)}
-    first, second = head, head
-    for m in range(1, depth):
-        first = jnp.where(z == m, got[m], first)
-        second = jnp.where(z == (m + 1) % depth, got[m], second)
-    pair = jnp.concatenate([first, second], 1)
-    for m, value in enumerate([send(pair, "y", [(0, m)]) for m in (1, 2, 3)], 1):
-        pair = jnp.where(y == m, value, pair)
-    own = [pair] + [shift(pair, "x", s) for s in (1, 2, 3)]
-    other = [swap(value) for value in own]
-    upper, inverse = factor_head(place, own, other)
+    twin = swap(head)
+    pair = jnp.concatenate([jnp.where(c == 0, head, twin), jnp.where(c == 0, twin, head)], 1)
+    pairs = [[] for _ in range(4)]
+    for (source_z, source_c), targets in (
+        ((0, 0), (1, 2, 3, 4)),
+        ((0, 1), (7, 6, 5)),
+        ((1, 0), (2, 3, 4, 5)),
+        ((1, 1), (0, 7, 6)),
+    ):
+        for turn, target in enumerate(targets):
+            pairs[turn].append((source_z * 2 + source_c, target * 2 + source_z))
+    got = [lax.ppermute(pair, ("z", "core"), turn) for turn in pairs]
+    mine = z == c
+    pair = jnp.where(mine, pair, got[0] + got[1] + got[2] + got[3])
+    got = [send(pair, "y", [(0, m)]) for m in (1, 2, 3)]
+    pair = jnp.where(y == 0, pair, got[0] + got[1] + got[2])
+    own = jnp.stack([pair] + [shift(pair, "x", s) for s in (1, 2, 3)])
+    upper, inverse = factor_head(place, own, swap(own))
 
     lead = matrix[:, :BLOCK]
     quarter = lead.shape[0] // 4
-    mine = lead[:quarter]
-    for m in (1, 2, 3):
-        value = send(lead[m * quarter : (m + 1) * quarter], "z", [(0, depth - m), (1, 1 + m)])
-        mine = jnp.where((z == depth - m) | (z == 1 + m), value, mine)
-    rows = jnp.stack([mine] + [shift(mine, "z", s) for s in range(1, depth)])
-    rows_other = swap(rows)
+    got = [
+        send(lead[m * quarter : (m + 1) * quarter], "z", [(0, depth - m), (1, 1 + m)])
+        for m in (1, 2, 3)
+    ]
+    part = jnp.where(z < 2, lead[:quarter], got[0] + got[1] + got[2])
+    rows = lax.all_gather(part, "z")
 
     top = matrix[:BLOCK]
     slab = BLOCK // 4
-    part = top[:slab]
-    for m in (1, 2, 3):
-        value = send(top[m * slab : (m + 1) * slab], "y", [(0, m)])
-        part = jnp.where(y == m, value, part)
-    cols = lax.all_gather(part, ("y", "x")).reshape(4, 4, slab, top.shape[1])
-    cols = cols.reshape(4, 4, slab, top.shape[1])
-    return update(place, matrix, rows, rows_other, cols, upper, inverse)
+    got = [send(top[m * slab : (m + 1) * slab], "y", [(0, m)]) for m in (1, 2, 3)]
+    part = jnp.where(y == 0, top[:slab], got[0] + got[1] + got[2])
+    half = part.shape[1] // 2
+    left, right = part[:, :half], part[:, half:]
+    left = jnp.stack([left] + [shift(left, "x", s) for s in (1, 2, 3)])
+    right = jnp.stack([right] + [shift(right, "y", s) for s in (1, 2, 3)])
+    lefts = [left] + [shift(left, "y", s) for s in (1, 2, 3)]
+    rights = [right] + [shift(right, "x", s) for s in (1, 2, 3)]
+    return update(place, matrix, rows, swap(rows), lefts, rights, upper, inverse)
 
 
 def solution(mesh):

time: 190 us -> 138 us (0.73)
  waiting for transfers between devices: 50.1 us -> 22.8 us
  starting transfers between devices: 74.4 us -> 48.5 us
    ppermute x16 -> x9, starting transfers between devices: 45.5 us -> 19.9 us  [send(): return lax.ppermute(value, axis, pairs)]
    ppermute x10 -> x15, waiting for transfers between devices: 41 us -> 18.9 us  [shift(): lax.ppermute(value, axis, [(i, (i + step) % size) for i in range(size)])]
    ppermute x5 -> x3, starting transfers between devices: 18.9 us -> 5.89 us  [swap(): return lax.ppermute(value, 'core', [(0, 1), (1, 0)])]
    ppermute x0 -> x4, starting transfers between devices: none -> 8.55 us  [shards(): got = [lax.ppermute(pair, ('z', 'core'), turn) for turn in pairs]]
    ppermute x16 -> x9, waiting for transfers between devices: 8.24 us -> 0.88 us  [send(): return lax.ppermute(value, axis, pairs)]
    ppermute x10 -> x15, starting transfers between devices: 10 us -> 14.2 us  [shift(): lax.ppermute(value, axis, [(i, (i + step) % size) for i in range(size)])]
    ppermute x0 -> x4, waiting for transfers between devices: none -> 2.98 us  [shards(): got = [lax.ppermute(pair, ('z', 'core'), turn) for turn in pairs]]
  transfers between devices with their start and end apart: 32 -> 32, of which waited for: 12 -> 12; matrix products, arithmetic and copies ran while one was open for 2% -> 4% of each run, Pallas kernels for 15% -> 21%
where the time goes in v2:
time: 138 us; the launch traced here: 137 us
  starting transfers between devices  48.5 us (35%)
  Pallas kernels  42 us (30%)
  waiting for transfers between devices  22.8 us (17%)
  between operations  13.8 us (10%)
  local copies, waits for them, and re-layouts  6.18 us (4%)
  other arithmetic  3.6 us (3%)
    pallas_call x1, Pallas kernels, factor_head(): pl.pallas_call(head_kernel, out_shape=[shape, shape], in_specs=[pl.BlockS...  29.2 us
    ppermute x9, starting transfers between devices, send(): return lax.ppermute(value, axis, pairs)  19.9 us
    ppermute x15, waiting for transfers between devices, shift(): lax.ppermute(value, axis, [(i, (i + step) % size) for i in range(size)])  18.9 us
    ppermute x15, starting transfers between devices, shift(): lax.ppermute(value, axis, [(i, (i + step) % size) for i in range(size)])  14.2 us
    pallas_call x1, Pallas kernels, update(): pl.pallas_call(update_kernel, grid=(rows // TILE,), out_shape=jax.ShapeDt...  12.8 us
    ppermute x4, starting transfers between devices, shards(): got = [lax.ppermute(pair, ('z', 'core'), turn) for turn in pairs]  8.55 us
    ppermute x3, starting transfers between devices, swap(): return lax.ppermute(value, 'core', [(0, 1), (1, 0)])  5.89 us
    unnamed x24, local copies, waits for them, and re-layouts  3.2 us
  transfers between devices with their start and end apart: 32, of which 12 were waited for; matrix products, arithmetic and copies ran while one was open for 4% of the time, Pallas kernels for 21%

profile of v2, /device:TPU:1, one launch (start us, length us, event | category | flops | bytes accessed | tf_op | source)
XLA Modules:
  0.0 137.0 jit_solution(11954065935737659085)
XLA Ops:
  6.5 0.8 slice.53
  7.4 3.2 %collective-permute-start.19 = (f32[128,128]{1,0:T(8,128)S(1)}, f32[128,128]{1,0:T(8,128)S(1)}, u32[]{:S(2)}, u32[]{:S(2)}) collective-permute-start(f32[128,128]{1,0:T(8,128)S(1)} %slice.53), channel_id=1, source_target_pairs={{0,1},{1,0},{2,3},{3,2},{4,5},{5,4},{6,7},{7,6},{8,9},{9,8},{10,11... | collective-permute-start | bytes 196616 | tf_op jit(solution)/shard_map/ppermute | solution.py:219
  10.6 1.1 fusion.1
  11.7 6.2 %collective-permute-start.1 = (f32[256,128]{1,0:T(8,128)S(1)}, f32[256,128]{1,0:T(8,128)S(1)}, u32[]{:S(2)}, u32[]{:S(2)}) collective-permute-start(f32[256,128]{1,0:T(8,128)S(1)} %get-tuple-element.14), channel_id=1, source_target_pairs={{0,12},{2,6},{1,13},{3,7},{16,28},{18,22},{17,29},{19,23},{32,44},... | collective-permute-start | bytes 393224 | tf_op jit(solution)/shard_map/ppermute | solution.py:210
  17.9 1.3 collective-permute-start.2
  19.2 1.3 collective-permute-start
  20.5 0.9 broadcast_select_fusion.1
  21.4 0.7 collective-permute-start.23
  22.1 1.3 collective-permute-start.22
  23.4 4.7 %collective-permute-start.21 = (f32[128,256]{1,0:T(8,128)S(1)}, f32[128,256]{1,0:T(8,128)S(1)}, u32[]{:S(2)}, u32[]{:S(2)}) collective-permute-start(f32[128,256]{1,0:T(8,128)S(1)} %pad_maximum_fusion.3), channel_id=1, source_target_pairs={{0,4},{1,12},{2,7},{3,15},{16,20},{17,28},{18,23},{19,31},{32,36},... | collective-permute-start | bytes 393224 | tf_op jit(solution)/shard_map/ppermute | solution.py:240
  28.1 0.0 collective-permute-done.2
  28.1 1.9 %collective-permute-start.20 = (f32[128,256]{1,0:T(8,128)S(1)}, f32[128,256]{1,0:T(8,128)S(1)}, u32[]{:S(2)}, u32[]{:S(2)}) collective-permute-start(f32[128,256]{1,0:T(8,128)S(1)} %pad_maximum_fusion.3), channel_id=1, source_target_pairs={{0,2},{1,14},{2,5},{3,1},{16,18},{17,30},{18,21},{19,17},{32,34},{... | collective-permute-start | bytes 393224 | tf_op jit(solution)/shard_map/ppermute | solution.py:240
  30.0 0.6 collective-permute-done
  30.6 1.6 %add_select_fusion.3 = f32[256,128]{1,0:T(8,128)} fusion(f32[256,128]{1,0:T(8,128)S(1)} %collective-permute-done.2, f32[256,128]{1,0:T(8,128)S(1)} %collective-permute-done, f32[256,128]{1,0:T(8,128)S(1)} %collective-permute-done.1, f32[1024,1024]{1,0:T(8,128)} %a_ref.1, pred[]{:T(512)S(6)} %lt.3), kind=kLoop, calls=%fused_computation.7 | loop fusion | flops 98304 | bytes 655361 | tf_op jit(solution)/shard_map/jit(_where)/select_n | solution.py:254
  32.2 0.0 all-gather.3.cloned.1.call-update
  32.2 0.2 collective-permute-done.22
  32.4 1.4 %collective-permute-done.21 = f32[128,256]{1,0:T(8,128)S(1)} collective-permute-done((f32[128,256]{1,0:T(8,128)S(1)}, f32[128,256]{1,0:T(8,128)S(1)}, u32[]{:S(2)}, u32[]{:S(2)}) %collective-permute-start.21) | collective-permute-done | bytes 131104 | tf_op jit(solution)/shard_map/ppermute | solution.py:240
  33.8 1.4 %collective-permute-done.20 = f32[128,256]{1,0:T(8,128)S(1)} collective-permute-done((f32[128,256]{1,0:T(8,128)S(1)}, f32[128,256]{1,0:T(8,128)S(1)}, u32[]{:S(2)}, u32[]{:S(2)}) %collective-permute-start.20) | collective-permute-done | bytes 131104 | tf_op jit(solution)/shard_map/ppermute | solution.py:240
  35.3 4.6 %collective-permute-start.26 = (f32[128,256]{1,0:T(8,128)S(1)}, f32[128,256]{1,0:T(8,128)S(1)}, u32[]{:S(2)}, u32[]{:S(2)}) collective-permute-start(f32[128,256]{1,0:T(8,128)S(1)} %add_select_fusion.1), channel_id=1, source_target_pairs={{0,192},{1,193},{2,194},{3,195},{4,196},{5,197},{6,198},{7,199},{8... | collective-permute-start | bytes 393224 | tf_op jit(solution)/shard_map/ppermute | solution.py:210
  39.9 1.3 collective-permute-start.25
  41.2 1.3 collective-permute-start.24
  42.5 1.1 fusion
  43.6 1.3 collective-permute-start.5
  44.9 1.3 collective-permute-start.6
  46.2 1.3 collective-permute-start.4
  47.5 0.0 collective-permute-done.25
  47.5 0.0 collective-permute-done.24
  47.6 2.6 %collective-permute-start.29 = (f32[128,256]{1,0:T(8,128)S(1)}, f32[128,256]{1,0:T(8,128)S(1)}, u32[]{:S(2)}, u32[]{:S(2)}) collective-permute-start(f32[128,256]{1,0:T(8,128)S(1)} %add_select_fusion), channel_id=1, source_target_pairs={{0,48},{16,0},{32,16},{48,32},{1,49},{17,1},{33,17},{49,33},{2,50}... | collective-permute-start | bytes 393224 | tf_op jit(solution)/shard_map/ppermute | solution.py:215
  50.2 0.5 collective-permute-start.28
  50.7 0.7 collective-permute-start.27
  51.4 0.0 collective-permute-done.6
  51.4 0.2 collective-permute-done.4
  51.6 0.9 add_select_fusion.2
  52.6 2.7 %collective-permute-done.29 = f32[128,256]{1,0:T(8,128)S(1)} collective-permute-done((f32[128,256]{1,0:T(8,128)S(1)}, f32[128,256]{1,0:T(8,128)S(1)}, u32[]{:S(2)}, u32[]{:S(2)}) %collective-permute-start.29) | collective-permute-done | bytes 131104 | tf_op jit(solution)/shard_map/ppermute | solution.py:215
  55.2 1.6 %collective-permute-done.28 = f32[128,256]{1,0:T(8,128)S(1)} collective-permute-done((f32[128,256]{1,0:T(8,128)S(1)}, f32[128,256]{1,0:T(8,128)S(1)}, u32[]{:S(2)}, u32[]{:S(2)}) %collective-permute-start.28) | collective-permute-done | bytes 131104 | tf_op jit(solution)/shard_map/ppermute | solution.py:215
  56.8 2.5 %collective-permute-done.27 = f32[128,256]{1,0:T(8,128)S(1)} collective-permute-done((f32[128,256]{1,0:T(8,128)S(1)}, f32[128,256]{1,0:T(8,128)S(1)}, u32[]{:S(2)}, u32[]{:S(2)}) %collective-permute-start.27) | collective-permute-done | bytes 131104 | tf_op jit(solution)/shard_map/ppermute | solution.py:215
  59.4 0.3 collective-permute-start.30
  59.7 0.6 collective-permute-start.8
  60.3 0.0 collective-permute-start.7
  60.3 2.7 %collective-permute-start.9 = (f32[32,512]{1,0:T(8,128)S(1)}, f32[32,512]{1,0:T(8,128)S(1)}, u32[]{:S(2)}, u32[]{:S(2)}) collective-permute-start(f32[32,512]{1,0:T(8,128)S(1)} %get-tuple-element.20), channel_id=1, source_target_pairs={{0,48},{16,0},{32,16},{48,32},{1,49},{17,1},{33,17},{49,33},{2,50}... | collective-permute-start | bytes 196616 | tf_op jit(solution)/shard_map/ppermute | solution.py:215
  63.0 0.5 collective-permute-start.14
  63.5 1.0 collective-permute-done.8
  64.5 2.1 %collective-permute-done.7 = f32[32,512]{1,0:T(8,128)S(1)} collective-permute-done((f32[32,512]{1,0:T(8,128)S(1)}, f32[32,512]{1,0:T(8,128)S(1)}, u32[]{:S(2)}, u32[]{:S(2)}) %collective-permute-start.7) | collective-permute-done | bytes 65568 | tf_op jit(solution)/shard_map/ppermute | solution.py:215
  66.7 0.1 collective-permute-start.12
  66.8 2.2 %collective-permute-start.11 = (f32[4,32,512]{2,1,0:T(8,128)S(1)}, f32[4,32,512]{2,1,0:T(8,128)S(1)}, u32[]{:S(2)}, u32[]{:S(2)}) collective-permute-start(f32[4,32,512]{2,1,0:T(8,128)S(1)} %pad_maximum_fusion.1.left0), channel_id=1, source_target_pairs={{0,128},{64,192},{128,0},{192,64},{1,129},{65,193},{129,1},{193,65... | collective-permute-start | bytes 786440 | tf_op jit(solution)/shard_map/ppermute | solution.py:215
  69.0 0.0 collective-permute-done.14
  69.0 2.7 %collective-permute-start.15 = (f32[32,512]{1,0:T(8,128)S(1)}, f32[32,512]{1,0:T(8,128)S(1)}, u32[]{:S(2)}, u32[]{:S(2)}) collective-permute-start(f32[32,512]{1,0:T(8,128)S(1)} %get-tuple-element.19), channel_id=1, source_target_pairs={{0,192},{64,0},{128,64},{192,128},{1,193},{65,1},{129,65},{193,129... | collective-permute-start | bytes 196616 | tf_op jit(solution)/shard_map/ppermute | solution.py:215
  71.7 0.1 pad_add_fusion.place
  71.7 6.3 %collective-permute-done.13 = f32[32,512]{1,0:T(8,128)S(1)} collective-permute-done((f32[32,512]{1,0:T(8,128)S(1)}, f32[32,512]{1,0:T(8,128)S(1)}, u32[]{:S(2)}, u32[]{:S(2)}) %collective-permute-start.13) | collective-permute-done | bytes 65568 | tf_op jit(solution)/shard_map/ppermute | solution.py:215
  78.0 0.0 collective-permute-start.10
  78.0 2.8 %collective-permute-done.15 = f32[32,512]{1,0:T(8,128)S(1)} collective-permute-done((f32[32,512]{1,0:T(8,128)S(1)}, f32[32,512]{1,0:T(8,128)S(1)}, u32[]{:S(2)}, u32[]{:S(2)}) %collective-permute-start.15) | collective-permute-done | bytes 65568 | tf_op jit(solution)/shard_map/ppermute | solution.py:215
  80.8 0.1 collective-permute-start.18
  80.9 0.3 collective-permute-start.17
  81.2 1.2 collective-permute-start.16
  82.5 2.3 %collective-permute-start.3 = (f32[8,256,128]{2,1,0:T(8,128)}, f32[8,256,128]{2,1,0:T(8,128)S(1)}, u32[]{:S(2)}, u32[]{:S(2)}) collective-permute-start(f32[8,256,128]{2,1,0:T(8,128)} %bitcast.19), channel_id=1, source_target_pairs={{0,1},{1,0},{2,3},{3,2},{4,5},{5,4},{6,7},{7,6},{8,9},{9,8},{10,11... | collective-permute-start | bytes 3145736 | tf_op jit(solution)/shard_map/ppermute | solution.py:219
  84.8 29.2 %shard_map.17 = (f32[512,512]{1,0:T(8,128)S(1)}, f32[512,512]{1,0:T(8,128)S(1)}) custom-call(s32[4]{0:T(128)S(1)} %pad_add_fusion.place, f32[4,128,256]{2,1,0:T(8,128)S(1)} %pad_maximum_fusion.own, f32[4,128,256]{2,1,0:T(8,128)S(1)} %collective-permute-done.30.other), custom_call_target="tpu_custom_call" | custom-call | flops 30000001024 | bytes 4194304 | tf_op jit(solution)/shard_map/pallas_call | solution.py:125
  114.0 1.0 copy-done
  115.0 1.0 copy-done.1
  116.1 0.6 copy-done.8
  116.7 0.1 copy-done.9
  116.8 0.1 copy-done.10
  116.9 0.1 copy-done.11
  117.0 0.3 copy-done.5
  117.3 12.8 %shard_map.18 = f32[1024,1024]{1,0:T(8,128)} custom-call(s32[4]{0:T(128)} %copy-done.2, f32[1024,1024]{1,0:T(8,128)} %a_ref.1, f32[8,256,128]{2,1,0:T(8,128)} %bitcast.20, f32[8,256,128]{2,1,0:T(8,128)} %copy-done.5, f32[4,32,512]{2,1,0:T(8,128)} %copy-done.3, f32[4,32,512]{2,1,0:T(8,128)} %copy-done.8, f32[4,32,512]{2,1,0:T(8,128)} %copy-done.7, ...), custom_call_target="tpu_custom_call" | custom-call | tf_op jit(solution)/shard_map/pallas_call | solution.py:192
  (41 shorter events, 0.3 us)
Async XLA Ops:
  6.5 75.9 %all-gather.3.cloned.1.call-start = ((), (), s32[]{:S(2)}) async-start(), calls=%async_computation | async-start | bytes 1179648 | tf_op jit(solution)/shard_map/all_gather | solution.py:255
  7.4 13.1 %collective-permute-start.19 = (f32[128,128]{1,0:T(8,128)S(1)}, f32[128,128]{1,0:T(8,128)S(1)}, u32[]{:S(2)}, u32[]{:S(2)}) collective-permute-start(f32[128,128]{1,0:T(8,128)S(1)} %slice.53), channel_id=1, source_target_pairs={{0,1},{1,0},{2,3},{3,2},{4,5},{5,4},{6,7},{7,6},{8,9},{9,8},{10,11... | collective-permute-start | bytes 196616 | tf_op jit(solution)/shard_map/ppermute | solution.py:219
  11.7 11.7 %collective-permute-start.1 = (f32[256,128]{1,0:T(8,128)S(1)}, f32[256,128]{1,0:T(8,128)S(1)}, u32[]{:S(2)}, u32[]{:S(2)}) collective-permute-start(f32[256,128]{1,0:T(8,128)S(1)} %get-tuple-element.14), channel_id=1, source_target_pairs={{0,12},{2,6},{1,13},{3,7},{16,28},{18,22},{17,29},{19,23},{32,44},... | collective-permute-start | bytes 393224 | tf_op jit(solution)/shard_map/ppermute | solution.py:210
  17.9 10.2 %collective-permute-start.2 = (f32[256,128]{1,0:T(8,128)S(1)}, f32[256,128]{1,0:T(8,128)S(1)}, u32[]{:S(2)}, u32[]{:S(2)}) collective-permute-start(f32[256,128]{1,0:T(8,128)S(1)} %get-tuple-element.15), channel_id=1, source_target_pairs={{0,10},{2,8},{1,11},{3,9},{16,26},{18,24},{17,27},{19,25},{32,42},... | collective-permute-start | bytes 393224 | tf_op jit(solution)/shard_map/ppermute | solution.py:210
  19.2 11.4 %collective-permute-start = (f32[256,128]{1,0:T(8,128)S(1)}, f32[256,128]{1,0:T(8,128)S(1)}, u32[]{:S(2)}, u32[]{:S(2)}) collective-permute-start(f32[256,128]{1,0:T(8,128)S(1)} %get-tuple-element.16), channel_id=1, source_target_pairs={{0,14},{2,4},{1,15},{3,5},{16,30},{18,20},{17,31},{19,21},{32,46},... | collective-permute-start | bytes 393224 | tf_op jit(solution)/shard_map/ppermute | solution.py:210
  21.4 10.8 %collective-permute-start.23 = (f32[128,256]{1,0:T(8,128)S(1)}, f32[128,256]{1,0:T(8,128)S(1)}, u32[]{:S(2)}, u32[]{:S(2)}) collective-permute-start(f32[128,256]{1,0:T(8,128)S(1)} %pad_maximum_fusion.3), channel_id=1, source_target_pairs={{0,8},{2,11},{16,24},{18,27},{32,40},{34,43},{48,56},{50,59},{64,7... | collective-permute-start | bytes 393224 | tf_op jit(solution)/shard_map/ppermute | solution.py:240
  22.1 10.3 %collective-permute-start.22 = (f32[128,256]{1,0:T(8,128)S(1)}, f32[128,256]{1,0:T(8,128)S(1)}, u32[]{:S(2)}, u32[]{:S(2)}) collective-permute-start(f32[128,256]{1,0:T(8,128)S(1)} %pad_maximum_fusion.3), channel_id=1, source_target_pairs={{0,6},{1,10},{2,9},{3,13},{16,22},{17,26},{18,25},{19,29},{32,38},... | collective-permute-start | bytes 393224 | tf_op jit(solution)/shard_map/ppermute | solution.py:240
  23.4 10.4 %collective-permute-start.21 = (f32[128,256]{1,0:T(8,128)S(1)}, f32[128,256]{1,0:T(8,128)S(1)}, u32[]{:S(2)}, u32[]{:S(2)}) collective-permute-start(f32[128,256]{1,0:T(8,128)S(1)} %pad_maximum_fusion.3), channel_id=1, source_target_pairs={{0,4},{1,12},{2,7},{3,15},{16,20},{17,28},{18,23},{19,31},{32,36},... | collective-permute-start | bytes 393224 | tf_op jit(solution)/shard_map/ppermute | solution.py:240
  28.1 7.2 %collective-permute-start.20 = (f32[128,256]{1,0:T(8,128)S(1)}, f32[128,256]{1,0:T(8,128)S(1)}, u32[]{:S(2)}, u32[]{:S(2)}) collective-permute-start(f32[128,256]{1,0:T(8,128)S(1)} %pad_maximum_fusion.3), channel_id=1, source_target_pairs={{0,2},{1,14},{2,5},{3,1},{16,18},{17,30},{18,21},{19,17},{32,34},{... | collective-permute-start | bytes 393224 | tf_op jit(solution)/shard_map/ppermute | solution.py:240
  35.3 10.9 %collective-permute-start.26 = (f32[128,256]{1,0:T(8,128)S(1)}, f32[128,256]{1,0:T(8,128)S(1)}, u32[]{:S(2)}, u32[]{:S(2)}) collective-permute-start(f32[128,256]{1,0:T(8,128)S(1)} %add_select_fusion.1), channel_id=1, source_target_pairs={{0,192},{1,193},{2,194},{3,195},{4,196},{5,197},{6,198},{7,199},{8... | collective-permute-start | bytes 393224 | tf_op jit(solution)/shard_map/ppermute | solution.py:210
  39.9 7.6 %collective-permute-start.25 = (f32[128,256]{1,0:T(8,128)S(1)}, f32[128,256]{1,0:T(8,128)S(1)}, u32[]{:S(2)}, u32[]{:S(2)}) collective-permute-start(f32[128,256]{1,0:T(8,128)S(1)} %add_select_fusion.1), channel_id=1, source_target_pairs={{0,128},{1,129},{2,130},{3,131},{4,132},{5,133},{6,134},{7,135},{8... | collective-permute-start | bytes 393224 | tf_op jit(solution)/shard_map/ppermute | solution.py:210
  41.2 6.3 %collective-permute-start.24 = (f32[128,256]{1,0:T(8,128)S(1)}, f32[128,256]{1,0:T(8,128)S(1)}, u32[]{:S(2)}, u32[]{:S(2)}) collective-permute-start(f32[128,256]{1,0:T(8,128)S(1)} %add_select_fusion.1), channel_id=1, source_target_pairs={{0,64},{1,65},{2,66},{3,67},{4,68},{5,69},{6,70},{7,71},{8,72},{9,... | collective-permute-start | bytes 393224 | tf_op jit(solution)/shard_map/ppermute | solution.py:210
  43.6 7.1 %collective-permute-start.5 = (f32[32,1024]{1,0:T(8,128)S(1)}, f32[32,1024]{1,0:T(8,128)S(1)}, u32[]{:S(2)}, u32[]{:S(2)}) collective-permute-start(f32[32,1024]{1,0:T(8,128)S(1)} %get-tuple-element.11), channel_id=1, source_target_pairs={{0,128},{1,129},{2,130},{3,131},{4,132},{5,133},{6,134},{7,135},{8... | collective-permute-start | bytes 393224 | tf_op jit(solution)/shard_map/ppermute | solution.py:210
  44.9 6.5 %collective-permute-start.6 = (f32[32,1024]{1,0:T(8,128)S(1)}, f32[32,1024]{1,0:T(8,128)S(1)}, u32[]{:S(2)}, u32[]{:S(2)}) collective-permute-start(f32[32,1024]{1,0:T(8,128)S(1)} %get-tuple-element.12), channel_id=1, source_target_pairs={{0,192},{1,193},{2,194},{3,195},{4,196},{5,197},{6,198},{7,199},{8... | collective-permute-start | bytes 393224 | tf_op jit(solution)/shard_map/ppermute | solution.py:210
  46.2 5.4 %collective-permute-start.4 = (f32[32,1024]{1,0:T(8,128)S(1)}, f32[32,1024]{1,0:T(8,128)S(1)}, u32[]{:S(2)}, u32[]{:S(2)}) collective-permute-start(f32[32,1024]{1,0:T(8,128)S(1)} %get-tuple-element.13), channel_id=1, source_target_pairs={{0,64},{1,65},{2,66},{3,67},{4,68},{5,69},{6,70},{7,71},{8,72},{9,... | collective-permute-start | bytes 393224 | tf_op jit(solution)/shard_map/ppermute | solution.py:210
  47.6 7.7 %collective-permute-start.29 = (f32[128,256]{1,0:T(8,128)S(1)}, f32[128,256]{1,0:T(8,128)S(1)}, u32[]{:S(2)}, u32[]{:S(2)}) collective-permute-start(f32[128,256]{1,0:T(8,128)S(1)} %add_select_fusion), channel_id=1, source_target_pairs={{0,48},{16,0},{32,16},{48,32},{1,49},{17,1},{33,17},{49,33},{2,50}... | collective-permute-start | bytes 393224 | tf_op jit(solution)/shard_map/ppermute | solution.py:215
  50.2 6.7 %collective-permute-start.28 = (f32[128,256]{1,0:T(8,128)S(1)}, f32[128,256]{1,0:T(8,128)S(1)}, u32[]{:S(2)}, u32[]{:S(2)}) collective-permute-start(f32[128,256]{1,0:T(8,128)S(1)} %add_select_fusion), channel_id=1, source_target_pairs={{0,32},{16,48},{32,0},{48,16},{1,33},{17,49},{33,1},{49,17},{2,34}... | collective-permute-start | bytes 393224 | tf_op jit(solution)/shard_map/ppermute | solution.py:215
  50.7 8.7 %collective-permute-start.27 = (f32[128,256]{1,0:T(8,128)S(1)}, f32[128,256]{1,0:T(8,128)S(1)}, u32[]{:S(2)}, u32[]{:S(2)}) collective-permute-start(f32[128,256]{1,0:T(8,128)S(1)} %add_select_fusion), channel_id=1, source_target_pairs={{0,16},{16,32},{32,48},{48,0},{1,17},{17,33},{33,49},{49,1},{2,18}... | collective-permute-start | bytes 393224 | tf_op jit(solution)/shard_map/ppermute | solution.py:215
  59.4 23.1 %collective-permute-start.30 = (f32[4,128,256]{2,1,0:T(8,128)S(1)}, f32[4,128,256]{2,1,0:T(8,128)S(1)}, u32[]{:S(2)}, u32[]{:S(2)}) collective-permute-start(f32[4,128,256]{2,1,0:T(8,128)S(1)} %pad_maximum_fusion.own), channel_id=1, source_target_pairs={{0,1},{1,0},{2,3},{3,2},{4,5},{5,4},{6,7},{7,6},{8,9},{9,8},{10,11... | collective-permute-start | bytes 1572872 | tf_op jit(solution)/shard_map/ppermute | solution.py:219
  59.7 4.8 %collective-permute-start.8 = (f32[32,512]{1,0:T(8,128)S(1)}, f32[32,512]{1,0:T(8,128)S(1)}, u32[]{:S(2)}, u32[]{:S(2)}) collective-permute-start(f32[32,512]{1,0:T(8,128)S(1)} %get-tuple-element.20), channel_id=1, source_target_pairs={{0,32},{16,48},{32,0},{48,16},{1,33},{17,49},{33,1},{49,17},{2,34}... | collective-permute-start | bytes 196616 | tf_op jit(solution)/shard_map/ppermute | solution.py:215
  60.3 6.3 %collective-permute-start.7 = (f32[32,512]{1,0:T(8,128)S(1)}, f32[32,512]{1,0:T(8,128)S(1)}, u32[]{:S(2)}, u32[]{:S(2)}) collective-permute-start(f32[32,512]{1,0:T(8,128)S(1)} %get-tuple-element.20), channel_id=1, source_target_pairs={{0,16},{16,32},{32,48},{48,0},{1,17},{17,33},{33,49},{49,1},{2,18}... | collective-permute-start | bytes 196616 | tf_op jit(solution)/shard_map/ppermute | solution.py:215
  60.3 6.3 %collective-permute-start.9 = (f32[32,512]{1,0:T(8,128)S(1)}, f32[32,512]{1,0:T(8,128)S(1)}, u32[]{:S(2)}, u32[]{:S(2)}) collective-permute-start(f32[32,512]{1,0:T(8,128)S(1)} %get-tuple-element.20), channel_id=1, source_target_pairs={{0,48},{16,0},{32,16},{48,32},{1,49},{17,1},{33,17},{49,33},{2,50}... | collective-permute-start | bytes 196616 | tf_op jit(solution)/shard_map/ppermute | solution.py:215
  63.0 6.0 %collective-permute-start.14 = (f32[32,512]{1,0:T(8,128)S(1)}, f32[32,512]{1,0:T(8,128)S(1)}, u32[]{:S(2)}, u32[]{:S(2)}) collective-permute-start(f32[32,512]{1,0:T(8,128)S(1)} %get-tuple-element.19), channel_id=1, source_target_pairs={{0,128},{64,192},{128,0},{192,64},{1,129},{65,193},{129,1},{193,65... | collective-permute-start | bytes 196616 | tf_op jit(solution)/shard_map/ppermute | solution.py:215
  66.7 47.3 %copy-start.3 = (f32[4,32,512]{2,1,0:T(8,128)}, f32[4,32,512]{2,1,0:T(8,128)S(1)}, u32[]{:S(2)}) copy-start(f32[4,32,512]{2,1,0:T(8,128)S(1)} %pad_maximum_fusion.1.left0) | copy-start | bytes 786436
  66.7 14.2 %collective-permute-start.12 = (f32[4,32,512]{2,1,0:T(8,128)S(1)}, f32[4,32,512]{2,1,0:T(8,128)S(1)}, u32[]{:S(2)}, u32[]{:S(2)}) collective-permute-start(f32[4,32,512]{2,1,0:T(8,128)S(1)} %pad_maximum_fusion.1.left0), channel_id=1, source_target_pairs={{0,192},{64,0},{128,64},{192,128},{1,193},{65,1},{129,65},{193,129... | collective-permute-start | bytes 786440 | tf_op jit(solution)/shard_map/ppermute | solution.py:215
  66.8 14.4 %collective-permute-start.11 = (f32[4,32,512]{2,1,0:T(8,128)S(1)}, f32[4,32,512]{2,1,0:T(8,128)S(1)}, u32[]{:S(2)}, u32[]{:S(2)}) collective-permute-start(f32[4,32,512]{2,1,0:T(8,128)S(1)} %pad_maximum_fusion.1.left0), channel_id=1, source_target_pairs={{0,128},{64,192},{128,0},{192,64},{1,129},{65,193},{129,1},{193,65... | collective-permute-start | bytes 786440 | tf_op jit(solution)/shard_map/ppermute | solution.py:215
  69.0 9.0 %collective-permute-start.13 = (f32[32,512]{1,0:T(8,128)S(1)}, f32[32,512]{1,0:T(8,128)S(1)}, u32[]{:S(2)}, u32[]{:S(2)}) collective-permute-start(f32[32,512]{1,0:T(8,128)S(1)} %get-tuple-element.19), channel_id=1, source_target_pairs={{0,64},{64,128},{128,192},{192,0},{1,65},{65,129},{129,193},{193,1... | collective-permute-start | bytes 196616 | tf_op jit(solution)/shard_map/ppermute | solution.py:215
  69.0 11.8 %collective-permute-start.15 = (f32[32,512]{1,0:T(8,128)S(1)}, f32[32,512]{1,0:T(8,128)S(1)}, u32[]{:S(2)}, u32[]{:S(2)}) collective-permute-start(f32[32,512]{1,0:T(8,128)S(1)} %get-tuple-element.19), channel_id=1, source_target_pairs={{0,192},{64,0},{128,64},{192,128},{1,193},{65,1},{129,65},{193,129... | collective-permute-start | bytes 196616 | tf_op jit(solution)/shard_map/ppermute | solution.py:215
  71.7 42.3 %copy-start.2 = (s32[4]{0:T(128)}, s32[4]{0:T(128)S(1)}, u32[]{:S(2)}) copy-start(s32[4]{0:T(128)S(1)} %pad_add_fusion.place) | copy-start | bytes 52
  78.0 38.0 %collective-permute-start.10 = (f32[4,32,512]{2,1,0:T(8,128)S(1)}, f32[4,32,512]{2,1,0:T(8,128)S(1)}, u32[]{:S(2)}, u32[]{:S(2)}) collective-permute-start(f32[4,32,512]{2,1,0:T(8,128)S(1)} %pad_maximum_fusion.1.left0), channel_id=1, source_target_pairs={{0,64},{64,128},{128,192},{192,0},{1,65},{65,129},{129,193},{193,1... | collective-permute-start | bytes 786440 | tf_op jit(solution)/shard_map/ppermute | solution.py:215
  80.8 33.2 %copy-start.4 = (f32[4,32,512]{2,1,0:T(8,128)}, f32[4,32,512]{2,1,0:T(8,128)S(1)}, u32[]{:S(2)}) copy-start(f32[4,32,512]{2,1,0:T(8,128)S(1)} %pad_maximum_fusion.2.right0) | copy-start | bytes 786436
  80.8 35.2 %collective-permute-start.18 = (f32[4,32,512]{2,1,0:T(8,128)S(1)}, f32[4,32,512]{2,1,0:T(8,128)S(1)}, u32[]{:S(2)}, u32[]{:S(2)}) collective-permute-start(f32[4,32,512]{2,1,0:T(8,128)S(1)} %pad_maximum_fusion.2.right0), channel_id=1, source_target_pairs={{0,48},{16,0},{32,16},{48,32},{1,49},{17,1},{33,17},{49,33},{2,50}... | collective-permute-start | bytes 786440 | tf_op jit(solution)/shard_map/ppermute | solution.py:215
  80.9 33.1 %copy-start.6 = (f32[4,32,512]{2,1,0:T(8,128)}, f32[4,32,512]{2,1,0:T(8,128)S(1)}, u32[]{:S(2)}) copy-start(f32[4,32,512]{2,1,0:T(8,128)S(1)} %collective-permute-done.12.left3) | copy-start | bytes 786436
  80.9 35.1 %collective-permute-start.17 = (f32[4,32,512]{2,1,0:T(8,128)S(1)}, f32[4,32,512]{2,1,0:T(8,128)S(1)}, u32[]{:S(2)}, u32[]{:S(2)}) collective-permute-start(f32[4,32,512]{2,1,0:T(8,128)S(1)} %pad_maximum_fusion.2.right0), channel_id=1, source_target_pairs={{0,32},{16,48},{32,0},{48,16},{1,33},{17,49},{33,1},{49,17},{2,34}... | collective-permute-start | bytes 786440 | tf_op jit(solution)/shard_map/ppermute | solution.py:215
  81.2 32.8 %copy-start.7 = (f32[4,32,512]{2,1,0:T(8,128)}, f32[4,32,512]{2,1,0:T(8,128)S(1)}, u32[]{:S(2)}) copy-start(f32[4,32,512]{2,1,0:T(8,128)S(1)} %collective-permute-done.11.left2) | copy-start | bytes 786436
  81.2 34.8 %collective-permute-start.16 = (f32[4,32,512]{2,1,0:T(8,128)S(1)}, f32[4,32,512]{2,1,0:T(8,128)S(1)}, u32[]{:S(2)}, u32[]{:S(2)}) collective-permute-start(f32[4,32,512]{2,1,0:T(8,128)S(1)} %pad_maximum_fusion.2.right0), channel_id=1, source_target_pairs={{0,16},{16,32},{32,48},{48,0},{1,17},{17,33},{33,49},{49,1},{2,18}... | collective-permute-start | bytes 786440 | tf_op jit(solution)/shard_map/ppermute | solution.py:215
  82.5 33.6 %collective-permute-start.3 = (f32[8,256,128]{2,1,0:T(8,128)}, f32[8,256,128]{2,1,0:T(8,128)S(1)}, u32[]{:S(2)}, u32[]{:S(2)}) collective-permute-start(f32[8,256,128]{2,1,0:T(8,128)} %bitcast.19), channel_id=1, source_target_pairs={{0,1},{1,0},{2,3},{3,2},{4,5},{5,4},{6,7},{7,6},{8,9},{9,8},{10,11... | collective-permute-start | bytes 3145736 | tf_op jit(solution)/shard_map/ppermute | solution.py:219
  114.0 1.0 copy-start
  115.0 1.0 copy-start.1
  116.0 0.7 copy-start.8
  116.0 0.8 copy-start.9
  116.0 0.9 copy-start.10
  116.0 0.9 copy-start.11
  116.0 1.2 copy-start.5
Sparse Core Ops, SparseCore 0:
  32.4 33.7 all-gather.2

commit v3 on v2

v3 whole, which is shorter than its diff:
```python
import jax
import jax.numpy as jnp
from jax import lax
from jax.experimental import pallas as pl
from jax.experimental.pallas import tpu as pltpu
from jax.sharding import Mesh, PartitionSpec as P

BLOCK = 128
PANELS = 4
SPAN = BLOCK * PANELS
SUB = 8
F32 = jnp.float32
BF16 = jnp.bfloat16


def split(value):
    high = value.astype(BF16)
    low = (value - high.astype(F32)).astype(BF16)
    return high, low


def split_dot(left, right, left_dim, right_dim):
    def dot(a, b):
        return lax.dot_general(
            a, b, (((left_dim,), (right_dim,)), ((), ())), preferred_element_type=F32
        )

    return dot(left[0], right[0]) + (dot(left[0], right[1]) + dot(left[1], right[0]))


def lane_fill(value, lane):
    return jnp.broadcast_to(value[:, lane : lane + 1], (SUB, BLOCK))


def eliminate(a, scratch):
    a = list(a)
    groups = len(a)
    sub = lax.broadcasted_iota(jnp.int32, (SUB, BLOCK), 0)
    lane = lax.broadcasted_iota(jnp.int32, (SUB, BLOCK), 1)
    upper, lower = [None] * groups, [None] * groups
    columns = [lane_fill(a[0], j) for j in range(SUB)]

    def stored_row(at):
        return jnp.broadcast_to(scratch[at : at + 1, :], (SUB, BLOCK))

    for c in range(groups):
        base = SUB * c
        inside = (lane >= base) & (lane < base + SUB)
        at = (c % 2) * (SUB + 1 + SUB) * SUB
        scratch[at : at + SUB, :] = a[c]
        for j in range(SUB):
            scratch[at + SUB * (j + 1) : at + SUB * (j + 2), :] = columns[j]
        s = [
            [stored_row(at + SUB * (j + 1) + i) if i >= j else None for j in range(SUB)]
            for i in range(SUB)
        ]
        rows = [stored_row(at + j) for j in range(SUB)]
        units = [(lane == base + j).astype(F32) for j in range(SUB)]
        more = c + 1 < groups
        if more:
            left = [lane_fill(a[c + 1], base + j) for j in range(SUB)]
            columns = [lane_fill(a[c + 1], base + SUB + j) for j in range(SUB)]
            a[c + 1] = jnp.where(inside, 0.0, a[c + 1])
        inv, merged = [None] * SUB, [None] * SUB
        for j in range(SUB):
            inv[j] = lax.rsqrt(s[j][j])
            for i in range(j + 1, SUB):
                s[i][j] = s[i][j] * inv[j]
            for k in range(j + 1, SUB):
                for i in range(k, SUB):
                    s[i][k] = s[i][k] - s[i][j] * s[k][j]
            rows[j] = rows[j] * inv[j]
            units[j] = units[j] * inv[j]
            for k in range(j + 1, SUB):
                rows[k] = rows[k] - s[k][j] * rows[j]
                units[k] = units[k] - s[k][j] * units[j]
            merged[j] = jnp.where(inside, units[j], rows[j])
            if more:
                left[j] = left[j] * inv[j]
                for k in range(j + 1, SUB):
                    left[k] = left[k] - left[j] * s[k][j]
                a[c + 1] = a[c + 1] - left[j] * merged[j]
                spot = at + (SUB + 1 + j) * SUB
                scratch[spot : spot + SUB, :] = left[j]
                for k in range(SUB):
                    columns[k] = columns[k] - left[j] * stored_row(spot + k)
        upper[c], lower[c] = rows[0], merged[0]
        for j in range(1, SUB):
            upper[c] = jnp.where(sub == j, rows[j], upper[c])
            lower[c] = jnp.where(sub == j, merged[j], lower[c])
        if c + 2 < groups:
            solved = list(merged)
            for j in range(SUB - 1, -1, -1):
                solved[j] = solved[j] * inv[j]
                for k in range(j):
                    solved[k] = solved[k] - s[j][k] * solved[j]
            for g in range(c + 2, groups):
                value = jnp.where(inside, 0.0, a[g])
                for j in range(SUB):
                    value = value - lane_fill(a[g], base + j) * solved[j]
                a[g] = value
    return upper, lower


def split3(value):
    high = value.astype(BF16)
    rest = value - high.astype(F32)
    middle = rest.astype(BF16)
    low = (rest - middle.astype(F32)).astype(BF16)
    return high, middle, low


def stack_left(value):
    high, middle, low = split3(value)
    return jnp.concatenate([high, high, middle, middle, high, low], 1)


def stack_right(value):
    high, middle, low = split3(value)
    return jnp.concatenate([high, middle, high, middle, low, high], 0)


def stacked_dot(left, right):
    return lax.dot_general(left, right, (((1,), (0,)), ((), ())), preferred_element_type=F32)


def head_kernel(place, own, other, u_ref, v_ref, head, scratch):
    x, c = place[1], place[3]
    half = SPAN // 2
    for step in range(PANELS):
        rows = pl.ds(pl.multiple_of(((x - step + PANELS) % PANELS) * BLOCK, BLOCK), BLOCK)
        for n in range(2):
            block = slice(n * BLOCK, (n + 1) * BLOCK)
            at = pl.multiple_of(c * half + n * BLOCK, BLOCK)
            head[rows, pl.ds(at, BLOCK)] = own[step, block]
            at = pl.multiple_of((1 - c) * half + n * BLOCK, BLOCK)
            head[rows, pl.ds(at, BLOCK)] = other[step, block]
    row = lax.broadcasted_iota(jnp.int32, (BLOCK, BLOCK), 0)
    col = lax.broadcasted_iota(jnp.int32, (BLOCK, BLOCK), 1)
    spans = [slice(k * BLOCK, (k + 1) * BLOCK) for k in range(PANELS)]
    work = {(i, j): head[spans[i], spans[j]] for i in range(PANELS) for j in range(i, PANELS)}
    unit = {}
    for k in range(PANELS):
        block = work[k, k]
        upper, lower = eliminate([block[g : g + SUB] for g in range(0, BLOCK, SUB)], scratch)
        factor = jnp.where(row <= col, jnp.concatenate(upper, 0), 0.0)
        inverse = jnp.where(row >= col, jnp.concatenate(lower, 0), 0.0)
        u_ref[spans[k], spans[k]] = factor
        v_ref[spans[k], spans[k]] = inverse
        sources = [work[k, j] for j in range(k + 1, PANELS)] + [unit[k, j] for j in range(k)]
        solved = stacked_dot(stack_left(inverse), stack_right(jnp.concatenate(sources, 1)))
        pieces = [solved[:, spans[i]] for i in range(PANELS - 1)]
        right = {j: pieces[j - k - 1] for j in range(k + 1, PANELS)}
        left = {j: pieces[PANELS - 1 - k + j] for j in range(k)}
        for j, value in right.items():
            u_ref[spans[k], spans[j]] = value
        for j, value in left.items():
            v_ref[spans[k], spans[j]] = value
        left[k] = inverse
        for i in range(k + 1, PANELS):
            factors = stack_left(right[i].T)
            first = i
            if i == k + 1:
                work[i, i] = work[i, i] - stacked_dot(factors, stack_right(right[i]))
                first = i + 1
            values = [right[j] for j in range(first, PANELS)] + [left[j] for j in range(k + 1)]
            change = stacked_dot(factors, stack_right(jnp.concatenate(values, 1)))
            parts = [change[:, n * BLOCK : (n + 1) * BLOCK] for n in range(len(values))]
            for j in range(first, PANELS):
                work[i, j] = work[i, j] - parts.pop(0)
            for j in range(k + 1):
                part = parts.pop(0)
                unit[i, j] = unit[i, j] - part if (i, j) in unit else -part
    for i in range(PANELS):
        for j in range(i):
            u_ref[spans[i], spans[j]] = jnp.zeros((BLOCK, BLOCK), F32)
            v_ref[spans[j], spans[i]] = jnp.zeros((BLOCK, BLOCK), F32)


def factor_head(place, own, other):
    shape = jax.ShapeDtypeStruct((SPAN, SPAN), F32)
    vmem = pl.BlockSpec(memory_space=pltpu.VMEM)
    return pl.pallas_call(
        head_kernel,
        out_shape=[shape, shape],
        in_specs=[pl.BlockSpec(memory_space=pltpu.SMEM), vmem, vmem],
        out_specs=[vmem, vmem],
        scratch_shapes=[
            pltpu.VMEM((SPAN, SPAN), F32),
            pltpu.VMEM((2 * (2 * SUB + 1) * SUB, BLOCK), F32),
        ],
        cost_estimate=pl.CostEstimate(
            flops=30_000_000_000, transcendentals=0, bytes_accessed=4 * 2**20
        ),
        compiler_params=pltpu.CompilerParams(vmem_limit_bytes=48 * 2**20),
    )(place, own, other)


SLAB = BLOCK // 4


TILE = 256


def update_kernel(
    place, a_ref, rows0, rows1, rows2, rows3, c0, c1, c2, c3, u_ref, v_ref, out_ref, column, w_hi, w_lo, v_hi, v_lo
):
    y, x, z, c = place[0], place[1], place[2], place[3]
    t = pl.program_id(0)

    @pl.when(t == 0)
    def _():
        for late, ref in enumerate((c0, c1, c2, c3)):
            for early in range(4):
                dx = jnp.where(c == 0, early, late)
                dy = jnp.where(c == 0, late, early)
                at = ((x - dx + 4) % 4) * BLOCK + ((y - dy + 4) % 4) * SLAB
                column[pl.ds(pl.multiple_of(at, SLAB), SLAB), :] = ref[early]
        high, low = split(split_dot(split(v_ref[...]), split(column[...]), 1, 0))
        w_hi[...] = high
        w_lo[...] = low
        high, low = split(v_ref[...])
        v_hi[...] = high
        v_lo[...] = low

    rows = jnp.concatenate([rows0[0], rows1[0], rows2[0], rows3[0]], 1)
    panel = split_dot(split(rows), (v_hi[...], v_lo[...]), 1, 1)
    out_ref[...] = a_ref[...] - split_dot(split(panel), (w_hi[...], w_lo[...]), 1, 0)
    q = 2 * z + c
    for k in range(PANELS):

        @pl.when(q == k)
        def _():
            out_ref[:, :BLOCK] = panel[:, k * BLOCK : (k + 1) * BLOCK]

    @pl.when((t == 0) & (y == 0))
    def _():
        out_ref[:BLOCK, :] = jnp.zeros((BLOCK, out_ref.shape[1]), F32)

    @pl.when((t == 0) & (y == 0) & (q < PANELS))
    def _():
        at_row = pl.ds(pl.multiple_of(jnp.minimum(q, PANELS - 1) * BLOCK, BLOCK), BLOCK)
        at_col = pl.ds(pl.multiple_of(x * BLOCK, BLOCK), BLOCK)
        out_ref[:BLOCK, :BLOCK] = u_ref[at_row, at_col].T


def update(place, matrix, rows, cols, upper, inverse):
    height, width = matrix.shape
    vmem = pl.BlockSpec(memory_space=pltpu.VMEM)
    tile = pl.BlockSpec((TILE, width), lambda t: (t, 0))
    quarter = (1,) + rows.shape[1:]
    pieces = [
        pl.BlockSpec(quarter, lambda t: (2 * ((8 - t) % 8), 0, 0)),
        pl.BlockSpec(quarter, lambda t: (2 * ((8 - t) % 8) + 1, 0, 0)),
        pl.BlockSpec(quarter, lambda t: (2 * (t + 1), 0, 0)),
        pl.BlockSpec(quarter, lambda t: (2 * (t + 1) + 1, 0, 0)),
    ]
    return pl.pallas_call(
        update_kernel,
        grid=(height // TILE,),
        out_shape=jax.ShapeDtypeStruct(matrix.shape, F32),
        in_specs=[pl.BlockSpec(memory_space=pltpu.SMEM), tile] + pieces + [vmem] * 6,
        out_specs=tile,
        scratch_shapes=[
            pltpu.VMEM((SPAN, width), F32),
            pltpu.VMEM((SPAN, width), BF16),
            pltpu.VMEM((SPAN, width), BF16),
            pltpu.VMEM((SPAN, SPAN), BF16),
            pltpu.VMEM((SPAN, SPAN), BF16),
        ],
        compiler_params=pltpu.CompilerParams(vmem_limit_bytes=56 * 2**20),
    )(place, matrix, rows, rows, rows, rows, *cols, upper, inverse)


def send(value, axis, pairs):
    return lax.ppermute(value, axis, pairs)


def shift(value, axis, step):
    size = lax.axis_size(axis)
    return lax.ppermute(value, axis, [(i, (i + step) % size) for i in range(size)])


def swap(value):
    return lax.ppermute(value, "core", [(0, 1), (1, 0)])


def turn(value, step, first):
    pairs = []
    for y in range(4):
        for x in range(4):
            for core in range(2):
                to = (y, (x + step) % 4) if core == first else ((y + step) % 4, x)
                pairs.append(((y * 4 + x) * 2 + core, (to[0] * 4 + to[1]) * 2 + core))
    return lax.ppermute(value, ("y", "x", "core"), pairs)


def shards(matrix):
    y, x = lax.axis_index("y"), lax.axis_index("x")
    z, c = lax.axis_index("z"), lax.axis_index("core")
    place = jnp.stack([y, x, z, c]).astype(jnp.int32)
    depth = lax.axis_size("z")

    head = matrix[:BLOCK, :BLOCK]
    twin = swap(head)
    pair = jnp.concatenate([jnp.where(c == 0, head, twin), jnp.where(c == 0, twin, head)], 0)
    pairs = [[] for _ in range(4)]
    for (source_z, source_c), targets in (
        ((0, 0), (1, 2, 3, 4)),
        ((0, 1), (7, 6, 5)),
        ((1, 0), (2, 3, 4, 5)),
        ((1, 1), (0, 7, 6)),
    ):
        for n, target in enumerate(targets):
            pairs[n].append((source_z * 2 + source_c, target * 2 + source_z))
    got = [lax.ppermute(pair, ("z", "core"), group) for group in pairs]

    lead = matrix[:, :BLOCK]
    quarter = lead.shape[0] // 4
    sent = [
        send(lead[m * quarter : (m + 1) * quarter], "z", [(0, depth - m), (1, 1 + m)])
        for m in (1, 2, 3)
    ]
    part = jnp.where(z < 2, lead[:quarter], sent[0] + sent[1] + sent[2])
    rows = lax.all_gather(part, ("z", "core"))

    top = matrix[:BLOCK]
    sent = [send(top[m * SLAB : (m + 1) * SLAB], "y", [(0, m)]) for m in (1, 2, 3)]
    share = jnp.where(y == 0, top[:SLAB], sent[0] + sent[1] + sent[2])

    pair = jnp.where(z == c, pair, got[0] + got[1] + got[2] + got[3])
    got = [send(pair, "y", [(0, m)]) for m in (1, 2, 3)]
    some = jnp.stack([share] + [turn(share, s, 0) for s in (1, 2, 3)])
    pair = jnp.where(y == 0, pair, got[0] + got[1] + got[2])
    own = jnp.stack([pair] + [shift(pair, "x", s) for s in (1, 2, 3)])
    cols = [some] + [turn(some, s, 1) for s in (1, 2, 3)]
    upper, inverse = factor_head(place, own, swap(own))
    return update(place, matrix, rows, cols, upper, inverse)


def solution(mesh):
    grid = Mesh(mesh.devices.reshape(4, 4, 8, 2), ("y", "x", "z", "core"))
    spec = P(("y", "x"), ("z", "core"))
    return jax.shard_map(shards, mesh=grid, in_specs=(spec,), out_specs=spec, check_vma=False)
```

time: 138 us -> 114 us (0.83)
  the two profiles are of different devices: /device:TPU:1 before, /device:TPU:56 now
where the time goes in v3:
time: 114 us; the launch traced here: 113 us
  starting transfers between devices  44.3 us (39%)
  Pallas kernels  25 us (22%)
  waiting for transfers between devices  20.6 us (18%)
  between operations  13.7 us (12%)
  local copies, waits for them, and re-layouts  6.09 us (5%)
  other arithmetic  3.6 us (3%)
    ppermute x6, starting transfers between devices, turn(): return lax.ppermute(value, ('y', 'x', 'core'), pairs)  15.7 us
    pallas_call x1, Pallas kernels, update(): pl.pallas_call(update_kernel, grid=(height // TILE,), out_shape=jax.Shape...  12.7 us
    ppermute x4, starting transfers between devices, shards(): got = [lax.ppermute(pair, ('z', 'core'), group) for group in pairs]  12.5 us
    pallas_call x1, Pallas kernels, factor_head(): pl.pallas_call(head_kernel, out_shape=[shape, shape], in_specs=[pl.BlockS...  12.3 us
    ppermute x9, starting transfers between devices, send(): return lax.ppermute(value, axis, pairs)  11.5 us
    ppermute x9, waiting for transfers between devices, send(): return lax.ppermute(value, axis, pairs)  9.51 us
    ppermute x6, waiting for transfers between devices, turn(): return lax.ppermute(value, ('y', 'x', 'core'), pairs)  6.28 us
    ppermute x3, starting transfers between devices, shift(): lax.ppermute(value, axis, [(i, (i + step) % size) for i in range(size)])  4.52 us
  transfers between devices with their start and end apart: 25, of which 12 were waited for; matrix products, arithmetic and copies ran while one was open for 4% of the time, Pallas kernels for 11%

profile of v3, /device:TPU:56, one launch (start us, length us, event | category | flops | bytes accessed | tf_op | source)
XLA Modules:
  0.0 113.4 jit_solution(14111300795092180958)
XLA Ops:
  6.5 0.8 slice.45
  7.4 0.0 collective-permute-start.12
  7.4 1.3 %collective-permute-done.12 = f32[128,128]{1,0:T(8,128)S(1)} collective-permute-done((f32[128,128]{1,0:T(8,128)S(1)}, f32[128,128]{1,0:T(8,128)S(1)}, u32[]{:S(2)}, u32[]{:S(2)}) %collective-permute-start.12) | collective-permute-done | bytes 65568 | tf_op jit(solution)/shard_map/ppermute | solution.py:285
  8.6 0.9 broadcast_select_fusion.1
  9.5 8.0 %collective-permute-start.16 = (f32[256,128]{1,0:T(8,128)S(1)}, f32[256,128]{1,0:T(8,128)S(1)}, u32[]{:S(2)}, u32[]{:S(2)}) collective-permute-start(f32[256,128]{1,0:T(8,128)S(1)} %pad_maximum_fusion.2), channel_id=1, source_target_pairs={{0,8},{2,11},{16,24},{18,27},{32,40},{34,43},{48,56},{50,59},{64,7... | collective-permute-start | bytes 393224 | tf_op jit(solution)/shard_map/ppermute | solution.py:316
  17.5 1.3 %collective-permute-start.15 = (f32[256,128]{1,0:T(8,128)S(1)}, f32[256,128]{1,0:T(8,128)S(1)}, u32[]{:S(2)}, u32[]{:S(2)}) collective-permute-start(f32[256,128]{1,0:T(8,128)S(1)} %pad_maximum_fusion.2), channel_id=1, source_target_pairs={{0,6},{1,10},{2,9},{3,13},{16,22},{17,26},{18,25},{19,29},{32,38},... | collective-permute-start | bytes 393224 | tf_op jit(solution)/shard_map/ppermute | solution.py:316
  18.8 1.3 %collective-permute-start.14 = (f32[256,128]{1,0:T(8,128)S(1)}, f32[256,128]{1,0:T(8,128)S(1)}, u32[]{:S(2)}, u32[]{:S(2)}) collective-permute-start(f32[256,128]{1,0:T(8,128)S(1)} %pad_maximum_fusion.2), channel_id=1, source_target_pairs={{0,4},{1,12},{2,7},{3,15},{16,20},{17,28},{18,23},{19,31},{32,36},... | collective-permute-start | bytes 393224 | tf_op jit(solution)/shard_map/ppermute | solution.py:316
  20.1 1.9 %collective-permute-start.13 = (f32[256,128]{1,0:T(8,128)S(1)}, f32[256,128]{1,0:T(8,128)S(1)}, u32[]{:S(2)}, u32[]{:S(2)}) collective-permute-start(f32[256,128]{1,0:T(8,128)S(1)} %pad_maximum_fusion.2), channel_id=1, source_target_pairs={{0,2},{1,14},{2,5},{3,1},{16,18},{17,30},{18,21},{19,17},{32,34},{... | collective-permute-start | bytes 393224 | tf_op jit(solution)/shard_map/ppermute | solution.py:316
  22.0 1.1 fusion.1
  23.1 1.3 %collective-permute-start.1 = (f32[256,128]{1,0:T(8,128)S(1)}, f32[256,128]{1,0:T(8,128)S(1)}, u32[]{:S(2)}, u32[]{:S(2)}) collective-permute-start(f32[256,128]{1,0:T(8,128)S(1)} %get-tuple-element.14), channel_id=1, source_target_pairs={{0,12},{2,6},{1,13},{3,7},{16,28},{18,22},{17,29},{19,23},{32,44},... | collective-permute-start | bytes 393224 | tf_op jit(solution)/shard_map/ppermute | solution.py:276
  24.4 0.0 collective-permute-done.16
  24.4 3.7 %collective-permute-start.2 = (f32[256,128]{1,0:T(8,128)S(1)}, f32[256,128]{1,0:T(8,128)S(1)}, u32[]{:S(2)}, u32[]{:S(2)}) collective-permute-start(f32[256,128]{1,0:T(8,128)S(1)} %get-tuple-element.15), channel_id=1, source_target_pairs={{0,10},{2,8},{1,11},{3,9},{16,26},{18,24},{17,27},{19,25},{32,42},... | collective-permute-start | bytes 393224 | tf_op jit(solution)/shard_map/ppermute | solution.py:276
  28.1 0.0 collective-permute-done.15
  28.1 1.3 %collective-permute-start = (f32[256,128]{1,0:T(8,128)S(1)}, f32[256,128]{1,0:T(8,128)S(1)}, u32[]{:S(2)}, u32[]{:S(2)}) collective-permute-start(f32[256,128]{1,0:T(8,128)S(1)} %get-tuple-element.16), channel_id=1, source_target_pairs={{0,14},{2,4},{1,15},{3,5},{16,30},{18,20},{17,31},{19,21},{32,46},... | collective-permute-start | bytes 393224 | tf_op jit(solution)/shard_map/ppermute | solution.py:276
  29.4 0.0 collective-permute-done.14
  29.4 1.0 collective-permute-done.13
  30.5 1.3 %collective-permute-start.19 = (f32[256,128]{1,0:T(8,128)S(1)}, f32[256,128]{1,0:T(8,128)S(1)}, u32[]{:S(2)}, u32[]{:S(2)}) collective-permute-start(f32[256,128]{1,0:T(8,128)S(1)} %add_select_fusion.1), channel_id=1, source_target_pairs={{0,192},{1,193},{2,194},{3,195},{4,196},{5,197},{6,198},{7,199},{8... | collective-permute-start | bytes 393224 | tf_op jit(solution)/shard_map/ppermute | solution.py:276
  31.8 0.7 collective-permute-start.18
  32.5 0.8 collective-permute-done.1
  33.3 0.7 collective-permute-start.17
  33.9 0.7 collective-permute-done.2
  34.7 1.4 %collective-permute-done = f32[256,128]{1,0:T(8,128)S(1)} collective-permute-done((f32[256,128]{1,0:T(8,128)S(1)}, f32[256,128]{1,0:T(8,128)S(1)}, u32[]{:S(2)}, u32[]{:S(2)}) %collective-permute-start) | collective-permute-done | bytes 131104 | tf_op jit(solution)/shard_map/ppermute | solution.py:276
  36.1 1.6 %add_select_fusion.3 = f32[256,128]{1,0:T(8,128)} fusion(f32[256,128]{1,0:T(8,128)S(1)} %collective-permute-done.2, f32[256,128]{1,0:T(8,128)S(1)} %collective-permute-done, f32[256,128]{1,0:T(8,128)S(1)} %collective-permute-done.1, f32[1024,1024]{1,0:T(8,128)} %a_ref.1, pred[]{:T(512)S(6)} %lt.3), kind=kLoop, calls=%fused_computation.6 | loop fusion | flops 98304 | bytes 655361 | tf_op jit(solution)/shard_map/jit(_where)/select_n | solution.py:324
  37.7 0.0 all-gather.3.cloned.1.call-update
  37.7 0.9 collective-permute-done.19
  38.6 0.0 collective-permute-done.18
  38.6 0.0 collective-permute-done.17
  38.6 2.8 %collective-permute-start.22 = (f32[256,128]{1,0:T(8,128)S(1)}, f32[256,128]{1,0:T(8,128)S(1)}, u32[]{:S(2)}, u32[]{:S(2)}) collective-permute-start(f32[256,128]{1,0:T(8,128)S(1)} %add_select_fusion), channel_id=1, source_target_pairs={{0,48},{16,0},{32,16},{48,32},{1,49},{17,1},{33,17},{49,33},{2,50}... | collective-permute-start | bytes 393224 | tf_op jit(solution)/shard_map/ppermute | solution.py:281
  41.4 0.8 collective-permute-start.21
  42.2 0.9 collective-permute-start.20
  43.1 1.1 fusion
  44.2 0.7 collective-permute-start.4
  44.9 1.3 %collective-permute-start.5 = (f32[32,1024]{1,0:T(8,128)S(1)}, f32[32,1024]{1,0:T(8,128)S(1)}, u32[]{:S(2)}, u32[]{:S(2)}) collective-permute-start(f32[32,1024]{1,0:T(8,128)S(1)} %get-tuple-element.12), channel_id=1, source_target_pairs={{0,192},{1,193},{2,194},{3,195},{4,196},{5,197},{6,198},{7,199},{8... | collective-permute-start | bytes 393224 | tf_op jit(solution)/shard_map/ppermute | solution.py:276
  46.2 0.0 collective-permute-done.22
  46.2 0.7 collective-permute-start.3
  46.9 1.2 %collective-permute-done.21 = f32[256,128]{1,0:T(8,128)S(1)} collective-permute-done((f32[256,128]{1,0:T(8,128)S(1)}, f32[256,128]{1,0:T(8,128)S(1)}, u32[]{:S(2)}, u32[]{:S(2)}) %collective-permute-start.21) | collective-permute-done | bytes 131104 | tf_op jit(solution)/shard_map/ppermute | solution.py:281
  48.0 1.3 %collective-permute-done.20 = f32[256,128]{1,0:T(8,128)S(1)} collective-permute-done((f32[256,128]{1,0:T(8,128)S(1)}, f32[256,128]{1,0:T(8,128)S(1)}, u32[]{:S(2)}, u32[]{:S(2)}) %collective-permute-start.20) | collective-permute-done | bytes 131104 | tf_op jit(solution)/shard_map/ppermute | solution.py:281
  49.4 0.1 collective-permute-start.23
  49.5 0.0 collective-permute-done.4
  49.5 5.7 %collective-permute-done.5 = f32[32,1024]{1,0:T(8,128)S(1)} collective-permute-done((f32[32,1024]{1,0:T(8,128)S(1)}, f32[32,1024]{1,0:T(8,128)S(1)}, u32[]{:S(2)}, u32[]{:S(2)}) %collective-permute-start.5) | collective-permute-done | bytes 131104 | tf_op jit(solution)/shard_map/ppermute | solution.py:276
  55.2 0.0 collective-permute-done.3
  55.2 0.9 add_select_fusion.2
  56.1 2.4 %collective-permute-start.8 = (f32[32,1024]{1,0:T(8,128)S(1)}, f32[32,1024]{1,0:T(8,128)S(1)}, u32[]{:S(2)}, u32[]{:S(2)}) collective-permute-start(f32[32,1024]{1,0:T(8,128)S(1)} %add_select_fusion.2), channel_id=1, source_target_pairs={{0,48},{1,193},{16,0},{17,209},{32,16},{33,225},{48,32},{49,241},{... | collective-permute-start | bytes 393224 | tf_op jit(solution)/shard_map/ppermute | solution.py:295
  58.5 1.5 %collective-permute-start.7 = (f32[32,1024]{1,0:T(8,128)S(1)}, f32[32,1024]{1,0:T(8,128)S(1)}, u32[]{:S(2)}, u32[]{:S(2)}) collective-permute-start(f32[32,1024]{1,0:T(8,128)S(1)} %add_select_fusion.2), channel_id=1, source_target_pairs={{0,32},{1,129},{16,48},{17,145},{32,0},{33,161},{48,16},{49,177},{... | collective-permute-start | bytes 393224 | tf_op jit(solution)/shard_map/ppermute | solution.py:295
  60.1 0.0 collective-permute-start.6
  60.1 0.1 pad_add_fusion.place
  60.1 2.3 %collective-permute-done.8 = f32[32,1024]{1,0:T(8,128)S(1)} collective-permute-done((f32[32,1024]{1,0:T(8,128)S(1)}, f32[32,1024]{1,0:T(8,128)S(1)}, u32[]{:S(2)}, u32[]{:S(2)}) %collective-permute-start.8) | collective-permute-done | bytes 131104 | tf_op jit(solution)/shard_map/ppermute | solution.py:295
  62.5 2.6 %collective-permute-done.7 = f32[32,1024]{1,0:T(8,128)S(1)} collective-permute-done((f32[32,1024]{1,0:T(8,128)S(1)}, f32[32,1024]{1,0:T(8,128)S(1)}, u32[]{:S(2)}, u32[]{:S(2)}) %collective-permute-start.7) | collective-permute-done | bytes 131104 | tf_op jit(solution)/shard_map/ppermute | solution.py:295
  65.0 1.4 %collective-permute-done.6 = f32[32,1024]{1,0:T(8,128)S(1)} collective-permute-done((f32[32,1024]{1,0:T(8,128)S(1)}, f32[32,1024]{1,0:T(8,128)S(1)}, u32[]{:S(2)}, u32[]{:S(2)}) %collective-permute-start.6) | collective-permute-done | bytes 131104 | tf_op jit(solution)/shard_map/ppermute | solution.py:295
  66.5 0.1 collective-permute-start.11
  66.6 9.2 %collective-permute-start.10 = (f32[4,32,1024]{2,1,0:T(8,128)S(1)}, f32[4,32,1024]{2,1,0:T(8,128)S(1)}, u32[]{:S(2)}, u32[]{:S(2)}) collective-permute-start(f32[4,32,1024]{2,1,0:T(8,128)S(1)} %pad_maximum_fusion.c0), channel_id=1, source_target_pairs={{0,128},{1,33},{16,144},{17,49},{32,160},{33,1},{48,176},{49,17},{... | collective-permute-start | bytes 1572872 | tf_op jit(solution)/shard_map/ppermute | solution.py:295
  75.7 2.5 %collective-permute-start.9 = (f32[4,32,1024]{2,1,0:T(8,128)S(1)}, f32[4,32,1024]{2,1,0:T(8,128)S(1)}, u32[]{:S(2)}, u32[]{:S(2)}) collective-permute-start(f32[4,32,1024]{2,1,0:T(8,128)S(1)} %pad_maximum_fusion.c0), channel_id=1, source_target_pairs={{0,64},{1,17},{16,80},{17,33},{32,96},{33,49},{48,112},{49,1},{64,... | collective-permute-start | bytes 1572872 | tf_op jit(solution)/shard_map/ppermute | solution.py:295
  78.3 0.0 collective-permute-done.23.other
  78.3 12.3 %shard_map.17 = (f32[512,512]{1,0:T(8,128)S(1)}, f32[512,512]{1,0:T(8,128)S(1)}) custom-call(s32[4]{0:T(128)S(1)} %pad_add_fusion.place, f32[4,256,128]{2,1,0:T(8,128)S(1)} %pad_maximum_fusion.1.own, f32[4,256,128]{2,1,0:T(8,128)S(1)} %collective-permute-done.23.other), custom_call_target="tpu_custom_call" | custom-call | flops 30000001024 | bytes 4194304 | tf_op jit(solution)/shard_map/pallas_call | solution.py:183
  90.6 1.0 copy-done
  91.6 1.0 copy-done.1
  92.6 0.0 collective-permute-done.11.c3
  92.6 0.0 collective-permute-done.10.c2
  92.6 0.0 collective-permute-done.9.c1
  92.7 0.0 all-gather.3.cloned.1.call-done
  92.7 0.7 copy-done.4
  93.4 0.2 copy-done.5
  93.6 0.2 copy-done.6
  93.8 12.7 %shard_map.18 = f32[1024,1024]{1,0:T(8,128)} custom-call(s32[4]{0:T(128)} %copy-done.2, f32[1024,1024]{1,0:T(8,128)} %a_ref.1, f32[16,256,128]{2,1,0:T(8,128)} %bitcast.13, f32[16,256,128]{2,1,0:T(8,128)} %bitcast.14, f32[16,256,128]{2,1,0:T(8,128)} %bitcast.15, f32[16,256,128]{2,1,0:T(8,128)} %bitcast.16, f32[4,32,1024]{2,1,0:T(8,128)} %copy-done.3, ...), custom_call_target="tpu_custom_call" | custom-call | tf_op jit(solution)/shard_map/pallas_call | solution.py:258
  (15 shorter events, 0.2 us)
Async XLA Ops:
  6.5 86.1 %all-gather.3.cloned.1.call-start = ((), (), s32[]{:S(2)}) async-start(), calls=%async_computation | async-start | bytes 2228224 | tf_op jit(solution)/shard_map/all_gather | solution.py:325
  7.4 1.3 %collective-permute-start.12 = (f32[128,128]{1,0:T(8,128)S(1)}, f32[128,128]{1,0:T(8,128)S(1)}, u32[]{:S(2)}, u32[]{:S(2)}) collective-permute-start(f32[128,128]{1,0:T(8,128)S(1)} %slice.45), channel_id=1, source_target_pairs={{0,1},{1,0},{2,3},{3,2},{4,5},{5,4},{6,7},{7,6},{8,9},{9,8},{10,11... | collective-permute-start | bytes 196616 | tf_op jit(solution)/shard_map/ppermute | solution.py:285
  9.5 14.9 %collective-permute-start.16 = (f32[256,128]{1,0:T(8,128)S(1)}, f32[256,128]{1,0:T(8,128)S(1)}, u32[]{:S(2)}, u32[]{:S(2)}) collective-permute-start(f32[256,128]{1,0:T(8,128)S(1)} %pad_maximum_fusion.2), channel_id=1, source_target_pairs={{0,8},{2,11},{16,24},{18,27},{32,40},{34,43},{48,56},{50,59},{64,7... | collective-permute-start | bytes 393224 | tf_op jit(solution)/shard_map/ppermute | solution.py:316
  17.5 10.6 %collective-permute-start.15 = (f32[256,128]{1,0:T(8,128)S(1)}, f32[256,128]{1,0:T(8,128)S(1)}, u32[]{:S(2)}, u32[]{:S(2)}) collective-permute-start(f32[256,128]{1,0:T(8,128)S(1)} %pad_maximum_fusion.2), channel_id=1, source_target_pairs={{0,6},{1,10},{2,9},{3,13},{16,22},{17,26},{18,25},{19,29},{32,38},... | collective-permute-start | bytes 393224 | tf_op jit(solution)/shard_map/ppermute | solution.py:316
  18.8 10.6 %collective-permute-start.14 = (f32[256,128]{1,0:T(8,128)S(1)}, f32[256,128]{1,0:T(8,128)S(1)}, u32[]{:S(2)}, u32[]{:S(2)}) collective-permute-start(f32[256,128]{1,0:T(8,128)S(1)} %pad_maximum_fusion.2), channel_id=1, source_target_pairs={{0,4},{1,12},{2,7},{3,15},{16,20},{17,28},{18,23},{19,31},{32,36},... | collective-permute-start | bytes 393224 | tf_op jit(solution)/shard_map/ppermute | solution.py:316
  20.1 10.4 %collective-permute-start.13 = (f32[256,128]{1,0:T(8,128)S(1)}, f32[256,128]{1,0:T(8,128)S(1)}, u32[]{:S(2)}, u32[]{:S(2)}) collective-permute-start(f32[256,128]{1,0:T(8,128)S(1)} %pad_maximum_fusion.2), channel_id=1, source_target_pairs={{0,2},{1,14},{2,5},{3,1},{16,18},{17,30},{18,21},{19,17},{32,34},{... | collective-permute-start | bytes 393224 | tf_op jit(solution)/shard_map/ppermute | solution.py:316
  23.1 10.2 %collective-permute-start.1 = (f32[256,128]{1,0:T(8,128)S(1)}, f32[256,128]{1,0:T(8,128)S(1)}, u32[]{:S(2)}, u32[]{:S(2)}) collective-permute-start(f32[256,128]{1,0:T(8,128)S(1)} %get-tuple-element.14), channel_id=1, source_target_pairs={{0,12},{2,6},{1,13},{3,7},{16,28},{18,22},{17,29},{19,23},{32,44},... | collective-permute-start | bytes 393224 | tf_op jit(solution)/shard_map/ppermute | solution.py:276
  24.4 10.2 %collective-permute-start.2 = (f32[256,128]{1,0:T(8,128)S(1)}, f32[256,128]{1,0:T(8,128)S(1)}, u32[]{:S(2)}, u32[]{:S(2)}) collective-permute-start(f32[256,128]{1,0:T(8,128)S(1)} %get-tuple-element.15), channel_id=1, source_target_pairs={{0,10},{2,8},{1,11},{3,9},{16,26},{18,24},{17,27},{19,25},{32,42},... | collective-permute-start | bytes 393224 | tf_op jit(solution)/shard_map/ppermute | solution.py:276
  28.1 8.0 %collective-permute-start = (f32[256,128]{1,0:T(8,128)S(1)}, f32[256,128]{1,0:T(8,128)S(1)}, u32[]{:S(2)}, u32[]{:S(2)}) collective-permute-start(f32[256,128]{1,0:T(8,128)S(1)} %get-tuple-element.16), channel_id=1, source_target_pairs={{0,14},{2,4},{1,15},{3,5},{16,30},{18,20},{17,31},{19,21},{32,46},... | collective-permute-start | bytes 393224 | tf_op jit(solution)/shard_map/ppermute | solution.py:276
  30.5 8.1 %collective-permute-start.19 = (f32[256,128]{1,0:T(8,128)S(1)}, f32[256,128]{1,0:T(8,128)S(1)}, u32[]{:S(2)}, u32[]{:S(2)}) collective-permute-start(f32[256,128]{1,0:T(8,128)S(1)} %add_select_fusion.1), channel_id=1, source_target_pairs={{0,192},{1,193},{2,194},{3,195},{4,196},{5,197},{6,198},{7,199},{8... | collective-permute-start | bytes 393224 | tf_op jit(solution)/shard_map/ppermute | solution.py:276
  31.8 6.8 %collective-permute-start.18 = (f32[256,128]{1,0:T(8,128)S(1)}, f32[256,128]{1,0:T(8,128)S(1)}, u32[]{:S(2)}, u32[]{:S(2)}) collective-permute-start(f32[256,128]{1,0:T(8,128)S(1)} %add_select_fusion.1), channel_id=1, source_target_pairs={{0,128},{1,129},{2,130},{3,131},{4,132},{5,133},{6,134},{7,135},{8... | collective-permute-start | bytes 393224 | tf_op jit(solution)/shard_map/ppermute | solution.py:276
  33.3 5.3 %collective-permute-start.17 = (f32[256,128]{1,0:T(8,128)S(1)}, f32[256,128]{1,0:T(8,128)S(1)}, u32[]{:S(2)}, u32[]{:S(2)}) collective-permute-start(f32[256,128]{1,0:T(8,128)S(1)} %add_select_fusion.1), channel_id=1, source_target_pairs={{0,64},{1,65},{2,66},{3,67},{4,68},{5,69},{6,70},{7,71},{8,72},{9,... | collective-permute-start | bytes 393224 | tf_op jit(solution)/shard_map/ppermute | solution.py:276
  38.6 7.6 %collective-permute-start.22 = (f32[256,128]{1,0:T(8,128)S(1)}, f32[256,128]{1,0:T(8,128)S(1)}, u32[]{:S(2)}, u32[]{:S(2)}) collective-permute-start(f32[256,128]{1,0:T(8,128)S(1)} %add_select_fusion), channel_id=1, source_target_pairs={{0,48},{16,0},{32,16},{48,32},{1,49},{17,1},{33,17},{49,33},{2,50}... | collective-permute-start | bytes 393224 | tf_op jit(solution)/shard_map/ppermute | solution.py:281
  41.4 6.6 %collective-permute-start.21 = (f32[256,128]{1,0:T(8,128)S(1)}, f32[256,128]{1,0:T(8,128)S(1)}, u32[]{:S(2)}, u32[]{:S(2)}) collective-permute-start(f32[256,128]{1,0:T(8,128)S(1)} %add_select_fusion), channel_id=1, source_target_pairs={{0,32},{16,48},{32,0},{48,16},{1,33},{17,49},{33,1},{49,17},{2,34}... | collective-permute-start | bytes 393224 | tf_op jit(solution)/shard_map/ppermute | solution.py:281
  42.2 7.1 %collective-permute-start.20 = (f32[256,128]{1,0:T(8,128)S(1)}, f32[256,128]{1,0:T(8,128)S(1)}, u32[]{:S(2)}, u32[]{:S(2)}) collective-permute-start(f32[256,128]{1,0:T(8,128)S(1)} %add_select_fusion), channel_id=1, source_target_pairs={{0,16},{16,32},{32,48},{48,0},{1,17},{17,33},{33,49},{49,1},{2,18}... | collective-permute-start | bytes 393224 | tf_op jit(solution)/shard_map/ppermute | solution.py:281
  44.2 5.3 %collective-permute-start.4 = (f32[32,1024]{1,0:T(8,128)S(1)}, f32[32,1024]{1,0:T(8,128)S(1)}, u32[]{:S(2)}, u32[]{:S(2)}) collective-permute-start(f32[32,1024]{1,0:T(8,128)S(1)} %get-tuple-element.11), channel_id=1, source_target_pairs={{0,128},{1,129},{2,130},{3,131},{4,132},{5,133},{6,134},{7,135},{8... | collective-permute-start | bytes 393224 | tf_op jit(solution)/shard_map/ppermute | solution.py:276
  44.9 10.3 %collective-permute-start.5 = (f32[32,1024]{1,0:T(8,128)S(1)}, f32[32,1024]{1,0:T(8,128)S(1)}, u32[]{:S(2)}, u32[]{:S(2)}) collective-permute-start(f32[32,1024]{1,0:T(8,128)S(1)} %get-tuple-element.12), channel_id=1, source_target_pairs={{0,192},{1,193},{2,194},{3,195},{4,196},{5,197},{6,198},{7,199},{8... | collective-permute-start | bytes 393224 | tf_op jit(solution)/shard_map/ppermute | solution.py:276
  46.2 9.0 %collective-permute-start.3 = (f32[32,1024]{1,0:T(8,128)S(1)}, f32[32,1024]{1,0:T(8,128)S(1)}, u32[]{:S(2)}, u32[]{:S(2)}) collective-permute-start(f32[32,1024]{1,0:T(8,128)S(1)} %get-tuple-element.13), channel_id=1, source_target_pairs={{0,64},{1,65},{2,66},{3,67},{4,68},{5,69},{6,70},{7,71},{8,72},{9,... | collective-permute-start | bytes 393224 | tf_op jit(solution)/shard_map/ppermute | solution.py:276
  49.4 28.9 %collective-permute-start.23 = (f32[4,256,128]{2,1,0:T(8,128)S(1)}, f32[4,256,128]{2,1,0:T(8,128)S(1)}, u32[]{:S(2)}, u32[]{:S(2)}) collective-permute-start(f32[4,256,128]{2,1,0:T(8,128)S(1)} %pad_maximum_fusion.1.own), channel_id=1, source_target_pairs={{0,1},{1,0},{2,3},{3,2},{4,5},{5,4},{6,7},{7,6},{8,9},{9,8},{10,11... | collective-permute-start | bytes 1572872 | tf_op jit(solution)/shard_map/ppermute | solution.py:285
  56.1 6.4 %collective-permute-start.8 = (f32[32,1024]{1,0:T(8,128)S(1)}, f32[32,1024]{1,0:T(8,128)S(1)}, u32[]{:S(2)}, u32[]{:S(2)}) collective-permute-start(f32[32,1024]{1,0:T(8,128)S(1)} %add_select_fusion.2), channel_id=1, source_target_pairs={{0,48},{1,193},{16,0},{17,209},{32,16},{33,225},{48,32},{49,241},{... | collective-permute-start | bytes 393224 | tf_op jit(solution)/shard_map/ppermute | solution.py:295
  58.5 6.5 %collective-permute-start.7 = (f32[32,1024]{1,0:T(8,128)S(1)}, f32[32,1024]{1,0:T(8,128)S(1)}, u32[]{:S(2)}, u32[]{:S(2)}) collective-permute-start(f32[32,1024]{1,0:T(8,128)S(1)} %add_select_fusion.2), channel_id=1, source_target_pairs={{0,32},{1,129},{16,48},{17,145},{32,0},{33,161},{48,16},{49,177},{... | collective-permute-start | bytes 393224 | tf_op jit(solution)/shard_map/ppermute | solution.py:295
  60.1 6.4 %collective-permute-start.6 = (f32[32,1024]{1,0:T(8,128)S(1)}, f32[32,1024]{1,0:T(8,128)S(1)}, u32[]{:S(2)}, u32[]{:S(2)}) collective-permute-start(f32[32,1024]{1,0:T(8,128)S(1)} %add_select_fusion.2), channel_id=1, source_target_pairs={{0,16},{1,65},{16,32},{17,81},{32,48},{33,97},{48,0},{49,113},{64,... | collective-permute-start | bytes 393224 | tf_op jit(solution)/shard_map/ppermute | solution.py:295
  60.1 30.5 %copy-start.2 = (s32[4]{0:T(128)}, s32[4]{0:T(128)S(1)}, u32[]{:S(2)}) copy-start(s32[4]{0:T(128)S(1)} %pad_add_fusion.place) | copy-start | bytes 52
  66.5 24.2 %copy-start.3 = (f32[4,32,1024]{2,1,0:T(8,128)}, f32[4,32,1024]{2,1,0:T(8,128)S(1)}, u32[]{:S(2)}) copy-start(f32[4,32,1024]{2,1,0:T(8,128)S(1)} %pad_maximum_fusion.c0) | copy-start | bytes 1572868
  66.5 26.1 %collective-permute-start.11 = (f32[4,32,1024]{2,1,0:T(8,128)S(1)}, f32[4,32,1024]{2,1,0:T(8,128)S(1)}, u32[]{:S(2)}, u32[]{:S(2)}) collective-permute-start(f32[4,32,1024]{2,1,0:T(8,128)S(1)} %pad_maximum_fusion.c0), channel_id=1, source_target_pairs={{0,192},{1,49},{16,208},{17,1},{32,224},{33,17},{48,240},{49,33},{... | collective-permute-start | bytes 1572872 | tf_op jit(solution)/shard_map/ppermute | solution.py:295
  66.6 26.1 %collective-permute-start.10 = (f32[4,32,1024]{2,1,0:T(8,128)S(1)}, f32[4,32,1024]{2,1,0:T(8,128)S(1)}, u32[]{:S(2)}, u32[]{:S(2)}) collective-permute-start(f32[4,32,1024]{2,1,0:T(8,128)S(1)} %pad_maximum_fusion.c0), channel_id=1, source_target_pairs={{0,128},{1,33},{16,144},{17,49},{32,160},{33,1},{48,176},{49,17},{... | collective-permute-start | bytes 1572872 | tf_op jit(solution)/shard_map/ppermute | solution.py:295
  75.7 16.9 %collective-permute-start.9 = (f32[4,32,1024]{2,1,0:T(8,128)S(1)}, f32[4,32,1024]{2,1,0:T(8,128)S(1)}, u32[]{:S(2)}, u32[]{:S(2)}) collective-permute-start(f32[4,32,1024]{2,1,0:T(8,128)S(1)} %pad_maximum_fusion.c0), channel_id=1, source_target_pairs={{0,64},{1,17},{16,80},{17,33},{32,96},{33,49},{48,112},{49,1},{64,... | collective-permute-start | bytes 1572872 | tf_op jit(solution)/shard_map/ppermute | solution.py:295
  90.6 1.0 copy-start
  91.6 1.0 copy-start.1
  92.6 0.8 copy-start.4
  92.6 1.0 copy-start.5
  92.6 1.2 %copy-start.6 = (f32[4,32,1024]{2,1,0:T(8,128)}, f32[4,32,1024]{2,1,0:T(8,128)S(1)}, u32[]{:S(2)}) copy-start(f32[4,32,1024]{2,1,0:T(8,128)S(1)} %collective-permute-done.9.c1) | copy-start | bytes 1572868
Sparse Core Ops, SparseCore 0:
  37.8 39.5 all-gather.2

commit v4 on v3

--- a/solution.py
+++ b/solution.py
@@ -19,13 +19,14 @@
     return high, low
 
 
-def split_dot(left, right, left_dim, right_dim):
-    def dot(a, b):
-        return lax.dot_general(
-            a, b, (((left_dim,), (right_dim,)), ((), ())), preferred_element_type=F32
-        )
-
-    return dot(left[0], right[0]) + (dot(left[0], right[1]) + dot(left[1], right[0]))
+def plain_dot(left, right, left_dim, right_dim):
+    return lax.dot_general(
+        left, right, (((left_dim,), (right_dim,)), ((), ())), preferred_element_type=F32
+    )
+
+
+def pieces_left(high, low):
+    return jnp.concatenate([high, high, low], 1)
 
 
 def lane_fill(value, lane):
@@ -124,7 +125,7 @@
     return lax.dot_general(left, right, (((1,), (0,)), ((), ())), preferred_element_type=F32)
 
 
-def head_kernel(place, own, other, u_ref, v_ref, head, scratch):
+def head_kernel(place, own, other, corner, v_ref, head, u_ref, scratch):
     x, c = place[1], place[3]
     half = SPAN // 2
     for step in range(PANELS):
@@ -175,17 +176,21 @@
         for j in range(i):
             u_ref[spans[i], spans[j]] = jnp.zeros((BLOCK, BLOCK), F32)
             v_ref[spans[j], spans[i]] = jnp.zeros((BLOCK, BLOCK), F32)
+    q = jnp.minimum(2 * place[2] + c, PANELS - 1)
+    at_row = pl.ds(pl.multiple_of(q * BLOCK, BLOCK), BLOCK)
+    corner[...] = u_ref[at_row, pl.ds(pl.multiple_of(x * BLOCK, BLOCK), BLOCK)].T
 
 
 def factor_head(place, own, other):
-    shape = jax.ShapeDtypeStruct((SPAN, SPAN), F32)
+    shapes = [jax.ShapeDtypeStruct((n, n), F32) for n in (BLOCK, SPAN)]
     vmem = pl.BlockSpec(memory_space=pltpu.VMEM)
     return pl.pallas_call(
         head_kernel,
-        out_shape=[shape, shape],
+        out_shape=shapes,
         in_specs=[pl.BlockSpec(memory_space=pltpu.SMEM), vmem, vmem],
         out_specs=[vmem, vmem],
         scratch_shapes=[
+            pltpu.VMEM((SPAN, SPAN), F32),
             pltpu.VMEM((SPAN, SPAN), F32),
             pltpu.VMEM((2 * (2 * SUB + 1) * SUB, BLOCK), F32),
         ],
@@ -199,14 +204,19 @@
 SLAB = BLOCK // 4
 
 
+def after(value, ready):
+    return value + ready[(slice(0, 1),) * ready.ndim].reshape((1,) * value.ndim) * 0.0
+
+
 TILE = 256
 
 
 def update_kernel(
-    place, a_ref, rows0, rows1, rows2, rows3, c0, c1, c2, c3, u_ref, v_ref, out_ref, column, w_hi, w_lo, v_hi, v_lo
+    place, a_ref, rows0, rows1, rows2, rows3, c0, c1, c2, c3, corner, v_ref, out_ref, column, w_all, v_all
 ):
     y, x, z, c = place[0], place[1], place[2], place[3]
     t = pl.program_id(0)
+    half = SPAN // 2
 
     @pl.when(t == 0)
     def _():
@@ -216,16 +226,30 @@
                 dy = jnp.where(c == 0, late, early)
                 at = ((x - dx + 4) % 4) * BLOCK + ((y - dy + 4) % 4) * SLAB
                 column[pl.ds(pl.multiple_of(at, SLAB), SLAB), :] = ref[early]
-        high, low = split(split_dot(split(v_ref[...]), split(column[...]), 1, 0))
-        w_hi[...] = high
-        w_lo[...] = low
-        high, low = split(v_ref[...])
-        v_hi[...] = high
-        v_lo[...] = low
+        v_high, v_low = split(v_ref[...])
+        high, low = split(column[...])
+        for i in range(2):
+            rows, depth = slice(i * half, (i + 1) * half), (i + 1) * half
+            left = pieces_left(v_high[rows, :depth], v_low[rows, :depth])
+            right = jnp.concatenate([high[:depth], low[:depth], high[:depth]], 0)
+            w_high, w_low = split(plain_dot(left, right, 1, 0))
+            for n, value in enumerate((w_high, w_low, w_high)):
+                w_all[n * SPAN + i * half : n * SPAN + (i + 1) * half] = value
+            v_all[i, :, : 3 * depth] = jnp.concatenate(
+                [v_high[rows, :depth], v_low[rows, :depth], v_high[rows, :depth]], 1
+            )
 
     rows = jnp.concatenate([rows0[0], rows1[0], rows2[0], rows3[0]], 1)
-    panel = split_dot(split(rows), (v_hi[...], v_lo[...]), 1, 1)
-    out_ref[...] = a_ref[...] - split_dot(split(panel), (w_hi[...], w_lo[...]), 1, 0)
+    high, low = split(rows)
+    panel = jnp.concatenate(
+        [
+            plain_dot(pieces_left(high[:, :half], low[:, :half]), v_all[0, :, : 3 * half], 1, 1),
+            plain_dot(pieces_left(high, low), v_all[1], 1, 1),
+        ],
+        1,
+    )
+    high, low = split(panel)
+    out_ref[...] = a_ref[...] - plain_dot(pieces_left(high, low), w_all[...], 1, 0)
     q = 2 * z + c
     for k in range(PANELS):
 
@@ -239,37 +263,40 @@
 
     @pl.when((t == 0) & (y == 0) & (q < PANELS))
     def _():
-        at_row = pl.ds(pl.multiple_of(jnp.minimum(q, PANELS - 1) * BLOCK, BLOCK), BLOCK)
-        at_col = pl.ds(pl.multiple_of(x * BLOCK, BLOCK), BLOCK)
-        out_ref[:BLOCK, :BLOCK] = u_ref[at_row, at_col].T
-
-
-def update(place, matrix, rows, cols, upper, inverse):
+        out_ref[:BLOCK, :BLOCK] = corner[...]
+
+
+def update(place, matrix, rows, cols, corner, inverse):
     height, width = matrix.shape
     vmem = pl.BlockSpec(memory_space=pltpu.VMEM)
-    tile = pl.BlockSpec((TILE, width), lambda t: (t, 0))
-    quarter = (1,) + rows.shape[1:]
+    tile = pl.BlockSpec((TILE, width), lambda t, place: (t, 0))
+    part = (1,) + rows.shape[1:]
+
+    def whole(shape):
+        return pl.BlockSpec(shape, lambda t, place: (0,) * len(shape), pipeline_mode=pl.Buffered(1))
+
     pieces = [
-        pl.BlockSpec(quarter, lambda t: (2 * ((8 - t) % 8), 0, 0)),
-        pl.BlockSpec(quarter, lambda t: (2 * ((8 - t) % 8) + 1, 0, 0)),
-        pl.BlockSpec(quarter, lambda t: (2 * (t + 1), 0, 0)),
-        pl.BlockSpec(quarter, lambda t: (2 * (t + 1) + 1, 0, 0)),
+        pl.BlockSpec(part, lambda t, place: (2 * ((8 - t) % 8), 0, 0)),
+        pl.BlockSpec(part, lambda t, place: (2 * ((8 - t) % 8) + 1, 0, 0)),
+        pl.BlockSpec(part, lambda t, place: (2 * (t + 1), 0, 0)),
+        pl.BlockSpec(part, lambda t, place: (2 * (t + 1) + 1, 0, 0)),
     ]
     return pl.pallas_call(
         update_kernel,
-        grid=(height // TILE,),
         out_shape=jax.ShapeDtypeStruct(matrix.shape, F32),
-        in_specs=[pl.BlockSpec(memory_space=pltpu.SMEM), tile] + pieces + [vmem] * 6,
-        out_specs=tile,
-        scratch_shapes=[
-            pltpu.VMEM((SPAN, width), F32),
-            pltpu.VMEM((SPAN, width), BF16),
-            pltpu.VMEM((SPAN, width), BF16),
-            pltpu.VMEM((SPAN, SPAN), BF16),
-            pltpu.VMEM((SPAN, SPAN), BF16),
-        ],
-        compiler_params=pltpu.CompilerParams(vmem_limit_bytes=56 * 2**20),
-    )(place, matrix, rows, rows, rows, rows, *cols, upper, inverse)
+        grid_spec=pltpu.PrefetchScalarGridSpec(
+            num_scalar_prefetch=1,
+            grid=(height // TILE,),
+            in_specs=[tile] + pieces + [vmem] * 4 + [vmem, vmem],
+            out_specs=tile,
+            scratch_shapes=[
+                pltpu.VMEM((SPAN, width), F32),
+                pltpu.VMEM((3 * SPAN, width), BF16),
+                pltpu.VMEM((2, SPAN // 2, 3 * SPAN), BF16),
+            ],
+        ),
+        compiler_params=pltpu.CompilerParams(vmem_limit_bytes=52 * 2**20),
+    )(place, matrix, rows, rows, rows, rows, *cols, corner, inverse)
 
 
 def send(value, axis, pairs):
@@ -331,11 +358,11 @@
     pair = jnp.where(z == c, pair, got[0] + got[1] + got[2] + got[3])
     got = [send(pair, "y", [(0, m)]) for m in (1, 2, 3)]
     some = jnp.stack([share] + [turn(share, s, 0) for s in (1, 2, 3)])
-    pair = jnp.where(y == 0, pair, got[0] + got[1] + got[2])
+    pair = after(jnp.where(y == 0, pair, got[0] + got[1] + got[2]), share)
     own = jnp.stack([pair] + [shift(pair, "x", s) for s in (1, 2, 3)])
     cols = [some] + [turn(some, s, 1) for s in (1, 2, 3)]
-    upper, inverse = factor_head(place, own, swap(own))
-    return update(place, matrix, rows, cols, upper, inverse)
+    corner, inverse = factor_head(place, own, swap(own))
+    return update(place, matrix, rows, cols, corner, inverse)
 
 
 def solution(mesh):

time: 114 us -> 110 us (0.965)
  the two profiles are of different devices: /device:TPU:56 before, /device:TPU:1 now
where the time goes in v4:
time: 110 us; the launch traced here: 108 us
  starting transfers between devices  48.9 us (44%)
  Pallas kernels  23.8 us (22%)
  between operations  14.4 us (13%)
  waiting for transfers between devices  13 us (12%)
  local copies, waits for them, and re-layouts  4.54 us (4%)
  other arithmetic  3.61 us (3%)
    ppermute x9, starting transfers between devices, send(): return lax.ppermute(value, axis, pairs)  20.1 us
    ppermute x4, starting transfers between devices, shards(): got = [lax.ppermute(pair, ('z', 'core'), group) for group in pairs]  15.8 us
    pallas_call x1, Pallas kernels, factor_head(): pl.pallas_call(head_kernel, out_shape=shapes, in_specs=[pl.BlockSpec(memo...  12.3 us
    pallas_call x1, Pallas kernels, update(): pl.pallas_call(update_kernel, out_shape=jax.ShapeDtypeStruct(matrix.shape...  11.5 us
    ppermute x3, waiting for transfers between devices, shift(): lax.ppermute(value, axis, [(i, (i + step) % size) for i in range(size)])  7.01 us
    ppermute x6, waiting for transfers between devices, turn(): return lax.ppermute(value, ('y', 'x', 'core'), pairs)  5.87 us
    ppermute x6, starting transfers between devices, turn(): return lax.ppermute(value, ('y', 'x', 'core'), pairs)  5.58 us
    ppermute x3, starting transfers between devices, shift(): lax.ppermute(value, axis, [(i, (i + step) % size) for i in range(size)])  3.68 us
  transfers between devices with their start and end apart: 25, of which 7 were waited for; matrix products, arithmetic and copies ran while one was open for 6% of the time, Pallas kernels for 11%

profile of v4, /device:TPU:1, one launch (start us, length us, event | category | flops | bytes accessed | tf_op | source)
XLA Modules:
  0.0 108.2 jit_solution(1515581520299390607)
XLA Ops:
  6.5 0.0 all-gather.3.cloned.1.call-start
  6.5 0.8 slice.48
  7.4 3.2 %collective-permute-start.12 = (f32[128,128]{1,0:T(8,128)S(1)}, f32[128,128]{1,0:T(8,128)S(1)}, u32[]{:S(2)}, u32[]{:S(2)}) collective-permute-start(f32[128,128]{1,0:T(8,128)S(1)} %slice.48), channel_id=1, source_target_pairs={{0,1},{1,0},{2,3},{3,2},{4,5},{5,4},{6,7},{7,6},{8,9},{9,8},{10,11... | collective-permute-start | bytes 196616 | tf_op jit(solution)/shard_map/ppermute | solution.py:312
  10.6 1.1 fusion
  11.7 3.1 %collective-permute-start.4 = (f32[32,1024]{1,0:T(8,128)S(1)}, f32[32,1024]{1,0:T(8,128)S(1)}, u32[]{:S(2)}, u32[]{:S(2)}) collective-permute-start(f32[32,1024]{1,0:T(8,128)S(1)} %get-tuple-element.11), channel_id=1, source_target_pairs={{0,128},{1,129},{2,130},{3,131},{4,132},{5,133},{6,134},{7,135},{8... | collective-permute-start | bytes 393224 | tf_op jit(solution)/shard_map/ppermute | solution.py:303
  14.8 1.1 fusion.1
  15.8 7.9 %collective-permute-start.1 = (f32[256,128]{1,0:T(8,128)S(1)}, f32[256,128]{1,0:T(8,128)S(1)}, u32[]{:S(2)}, u32[]{:S(2)}) collective-permute-start(f32[256,128]{1,0:T(8,128)S(1)} %get-tuple-element.14), channel_id=1, source_target_pairs={{0,12},{2,6},{1,13},{3,7},{16,28},{18,22},{17,29},{19,23},{32,44},... | collective-permute-start | bytes 393224 | tf_op jit(solution)/shard_map/ppermute | solution.py:303
  23.8 1.3 %collective-permute-start.2 = (f32[256,128]{1,0:T(8,128)S(1)}, f32[256,128]{1,0:T(8,128)S(1)}, u32[]{:S(2)}, u32[]{:S(2)}) collective-permute-start(f32[256,128]{1,0:T(8,128)S(1)} %get-tuple-element.15), channel_id=1, source_target_pairs={{0,10},{2,8},{1,11},{3,9},{16,26},{18,24},{17,27},{19,25},{32,42},... | collective-permute-start | bytes 393224 | tf_op jit(solution)/shard_map/ppermute | solution.py:303
  25.1 1.3 %collective-permute-start = (f32[256,128]{1,0:T(8,128)S(1)}, f32[256,128]{1,0:T(8,128)S(1)}, u32[]{:S(2)}, u32[]{:S(2)}) collective-permute-start(f32[256,128]{1,0:T(8,128)S(1)} %get-tuple-element.16), channel_id=1, source_target_pairs={{0,14},{2,4},{1,15},{3,5},{16,30},{18,20},{17,31},{19,21},{32,46},... | collective-permute-start | bytes 393224 | tf_op jit(solution)/shard_map/ppermute | solution.py:303
  26.4 0.0 collective-permute-done.12
  26.4 0.9 broadcast_select_fusion.1
  27.3 0.7 collective-permute-start.16
  28.0 0.0 collective-permute-done.1
  28.0 1.3 %collective-permute-start.15 = (f32[256,128]{1,0:T(8,128)S(1)}, f32[256,128]{1,0:T(8,128)S(1)}, u32[]{:S(2)}, u32[]{:S(2)}) collective-permute-start(f32[256,128]{1,0:T(8,128)S(1)} %pad_maximum_fusion.2), channel_id=1, source_target_pairs={{0,6},{1,10},{2,9},{3,13},{16,22},{17,26},{18,25},{19,29},{32,38},... | collective-permute-start | bytes 393224 | tf_op jit(solution)/shard_map/ppermute | solution.py:343
  29.3 0.0 collective-permute-done.2
  29.3 5.7 %collective-permute-start.14 = (f32[256,128]{1,0:T(8,128)S(1)}, f32[256,128]{1,0:T(8,128)S(1)}, u32[]{:S(2)}, u32[]{:S(2)}) collective-permute-start(f32[256,128]{1,0:T(8,128)S(1)} %pad_maximum_fusion.2), channel_id=1, source_target_pairs={{0,4},{1,12},{2,7},{3,15},{16,20},{17,28},{18,23},{19,31},{32,36},... | collective-permute-start | bytes 393224 | tf_op jit(solution)/shard_map/ppermute | solution.py:343
  35.0 0.0 collective-permute-done
  35.0 8.2 %collective-permute-start.13 = (f32[256,128]{1,0:T(8,128)S(1)}, f32[256,128]{1,0:T(8,128)S(1)}, u32[]{:S(2)}, u32[]{:S(2)}) collective-permute-start(f32[256,128]{1,0:T(8,128)S(1)} %pad_maximum_fusion.2), channel_id=1, source_target_pairs={{0,2},{1,14},{2,5},{3,1},{16,18},{17,30},{18,21},{19,17},{32,34},{... | collective-permute-start | bytes 393224 | tf_op jit(solution)/shard_map/ppermute | solution.py:343
  43.2 1.6 %add_select_fusion.2 = f32[256,128]{1,0:T(8,128)} fusion(f32[256,128]{1,0:T(8,128)S(1)} %collective-permute-done.2, f32[256,128]{1,0:T(8,128)S(1)} %collective-permute-done, f32[256,128]{1,0:T(8,128)S(1)} %collective-permute-done.1, f32[1024,1024]{1,0:T(8,128)} %a_ref.1, pred[]{:T(512)S(6)} %lt.3), kind=kLoop, calls=%fused_computation.6 | loop fusion | flops 98304 | bytes 655361 | tf_op jit(solution)/shard_map/jit(_where)/select_n | solution.py:351
  44.8 0.0 all-gather.3.cloned.1.call-update
  44.8 0.0 collective-permute-done.16
  44.8 1.3 %collective-permute-start.5 = (f32[32,1024]{1,0:T(8,128)S(1)}, f32[32,1024]{1,0:T(8,128)S(1)}, u32[]{:S(2)}, u32[]{:S(2)}) collective-permute-start(f32[32,1024]{1,0:T(8,128)S(1)} %get-tuple-element.12), channel_id=1, source_target_pairs={{0,192},{1,193},{2,194},{3,195},{4,196},{5,197},{6,198},{7,199},{8... | collective-permute-start | bytes 393224 | tf_op jit(solution)/shard_map/ppermute | solution.py:303
  46.1 0.0 collective-permute-done.15
  46.1 1.3 %collective-permute-start.3 = (f32[32,1024]{1,0:T(8,128)S(1)}, f32[32,1024]{1,0:T(8,128)S(1)}, u32[]{:S(2)}, u32[]{:S(2)}) collective-permute-start(f32[32,1024]{1,0:T(8,128)S(1)} %get-tuple-element.13), channel_id=1, source_target_pairs={{0,64},{1,65},{2,66},{3,67},{4,68},{5,69},{6,70},{7,71},{8,72},{9,... | collective-permute-start | bytes 393224 | tf_op jit(solution)/shard_map/ppermute | solution.py:303
  47.5 0.0 collective-permute-done.14
  47.5 0.0 collective-permute-done.13
  47.5 1.3 %collective-permute-start.19 = (f32[256,128]{1,0:T(8,128)S(1)}, f32[256,128]{1,0:T(8,128)S(1)}, u32[]{:S(2)}, u32[]{:S(2)}) collective-permute-start(f32[256,128]{1,0:T(8,128)S(1)} %add_select_fusion), channel_id=1, source_target_pairs={{0,192},{1,193},{2,194},{3,195},{4,196},{5,197},{6,198},{7,199},{8... | collective-permute-start | bytes 393224 | tf_op jit(solution)/shard_map/ppermute | solution.py:303
  48.8 1.3 %collective-permute-start.18 = (f32[256,128]{1,0:T(8,128)S(1)}, f32[256,128]{1,0:T(8,128)S(1)}, u32[]{:S(2)}, u32[]{:S(2)}) collective-permute-start(f32[256,128]{1,0:T(8,128)S(1)} %add_select_fusion), channel_id=1, source_target_pairs={{0,128},{1,129},{2,130},{3,131},{4,132},{5,133},{6,134},{7,135},{8... | collective-permute-start | bytes 393224 | tf_op jit(solution)/shard_map/ppermute | solution.py:303
  50.1 0.0 collective-permute-done.4
  50.1 1.3 %collective-permute-start.17 = (f32[256,128]{1,0:T(8,128)S(1)}, f32[256,128]{1,0:T(8,128)S(1)}, u32[]{:S(2)}, u32[]{:S(2)}) collective-permute-start(f32[256,128]{1,0:T(8,128)S(1)} %add_select_fusion), channel_id=1, source_target_pairs={{0,64},{1,65},{2,66},{3,67},{4,68},{5,69},{6,70},{7,71},{8,72},{9,... | collective-permute-start | bytes 393224 | tf_op jit(solution)/shard_map/ppermute | solution.py:303
  51.4 0.0 collective-permute-done.5
  51.5 0.0 collective-permute-done.3
  51.5 0.9 add_select_fusion.1
  52.4 0.6 slice.50
  53.7 0.0 collective-permute-done.19
  53.7 0.0 collective-permute-done.18
  53.7 0.0 collective-permute-done.17
  53.8 2.6 %collective-permute-start.22 = (f32[256,128]{1,0:T(8,128)S(1)}, f32[256,128]{1,0:T(8,128)S(1)}, u32[]{:S(2)}, u32[]{:S(2)}) collective-permute-start(f32[256,128]{1,0:T(8,128)S(1)} %select_add_fusion), channel_id=1, source_target_pairs={{0,48},{16,0},{32,16},{48,32},{1,49},{17,1},{33,17},{49,33},{2,50}... | collective-permute-start | bytes 393224 | tf_op jit(solution)/shard_map/ppermute | solution.py:308
  56.4 0.5 collective-permute-start.21
  56.9 0.6 collective-permute-start.20
  57.5 3.2 %collective-permute-done.22 = f32[256,128]{1,0:T(8,128)S(1)} collective-permute-done((f32[256,128]{1,0:T(8,128)S(1)}, f32[256,128]{1,0:T(8,128)S(1)}, u32[]{:S(2)}, u32[]{:S(2)}) %collective-permute-start.22) | collective-permute-done | bytes 131104 | tf_op jit(solution)/shard_map/ppermute | solution.py:308
  60.7 2.3 %collective-permute-done.21 = f32[256,128]{1,0:T(8,128)S(1)} collective-permute-done((f32[256,128]{1,0:T(8,128)S(1)}, f32[256,128]{1,0:T(8,128)S(1)}, u32[]{:S(2)}, u32[]{:S(2)}) %collective-permute-start.21) | collective-permute-done | bytes 131104 | tf_op jit(solution)/shard_map/ppermute | solution.py:308
  63.0 1.5 %collective-permute-done.20 = f32[256,128]{1,0:T(8,128)S(1)} collective-permute-done((f32[256,128]{1,0:T(8,128)S(1)}, f32[256,128]{1,0:T(8,128)S(1)}, u32[]{:S(2)}, u32[]{:S(2)}) %collective-permute-start.20) | collective-permute-done | bytes 131104 | tf_op jit(solution)/shard_map/ppermute | solution.py:308
  64.5 0.4 collective-permute-start.23
  65.0 0.0 collective-permute-start.8
  65.0 4.0 %collective-permute-start.7 = (f32[32,1024]{1,0:T(8,128)S(1)}, f32[32,1024]{1,0:T(8,128)S(1)}, u32[]{:S(2)}, u32[]{:S(2)}) collective-permute-start(f32[32,1024]{1,0:T(8,128)S(1)} %add_select_fusion.1), channel_id=1, source_target_pairs={{0,32},{1,129},{16,48},{17,145},{32,0},{33,161},{48,16},{49,177},{... | collective-permute-start | bytes 393224 | tf_op jit(solution)/shard_map/ppermute | solution.py:322
  69.0 0.0 collective-permute-start.6
  69.0 0.1 pad_add_fusion.place
  69.1 0.7 collective-permute-done.8
  69.7 1.9 %collective-permute-done.7 = f32[32,1024]{1,0:T(8,128)S(1)} collective-permute-done((f32[32,1024]{1,0:T(8,128)S(1)}, f32[32,1024]{1,0:T(8,128)S(1)}, u32[]{:S(2)}, u32[]{:S(2)}) %collective-permute-start.7) | collective-permute-done | bytes 131104 | tf_op jit(solution)/shard_map/ppermute | solution.py:322
  71.6 2.4 %collective-permute-done.6 = f32[32,1024]{1,0:T(8,128)S(1)} collective-permute-done((f32[32,1024]{1,0:T(8,128)S(1)}, f32[32,1024]{1,0:T(8,128)S(1)}, u32[]{:S(2)}, u32[]{:S(2)}) %collective-permute-start.6) | collective-permute-done | bytes 131104 | tf_op jit(solution)/shard_map/ppermute | solution.py:322
  74.1 0.4 collective-permute-start.11
  74.4 0.5 collective-permute-start.10
  75.0 0.7 collective-permute-start.9
  75.6 0.0 collective-permute-done.23.other
  75.6 12.3 %shard_map.17 = (f32[128,128]{1,0:T(8,128)S(1)}, f32[512,512]{1,0:T(8,128)S(1)}) custom-call(s32[4]{0:T(128)S(1)} %pad_add_fusion.place, f32[4,256,128]{2,1,0:T(8,128)S(1)} %pad_maximum_fusion.1.own, f32[4,256,128]{2,1,0:T(8,128)S(1)} %collective-permute-done.23.other), custom_call_target="tpu_custom_call" | custom-call | flops 30000001024 | bytes 4194304 | tf_op jit(solution)/shard_map/pallas_call | solution.py:187
  88.0 0.0 copy-start
  88.0 1.0 copy-done
  89.0 0.0 collective-permute-done.11.c3
  89.0 0.0 copy-start.1
  89.0 0.0 collective-permute-done.10.c2
  89.0 0.9 collective-permute-done.9.c1
  89.9 0.0 copy-done.1
  89.9 11.5 %shard_map.18 = f32[1024,1024]{1,0:T(8,128)} custom-call(s32[4]{0:T(128)S(1)} %pad_add_fusion.place, f32[1024,1024]{1,0:T(8,128)} %a_ref.1, f32[16,256,128]{2,1,0:T(8,128)} %bitcast.14, f32[16,256,128]{2,1,0:T(8,128)} %bitcast.15, f32[16,256,128]{2,1,0:T(8,128)} %bitcast.16, f32[16,256,128]{2,1,0:T(8,128)} %bitcast.17, ...), custom_call_target="tpu_custom_call" | custom-call | tf_op jit(solution)/shard_map/pallas_call | solution.py:284
  (6 shorter events, 0.2 us)
Async XLA Ops:
  6.5 83.4 %all-gather.3.cloned.1.call-start = ((), (), s32[]{:S(2)}) async-start(), calls=%async_computation | async-start | bytes 2228224 | tf_op jit(solution)/shard_map/all_gather | solution.py:352
  7.4 19.0 %collective-permute-start.12 = (f32[128,128]{1,0:T(8,128)S(1)}, f32[128,128]{1,0:T(8,128)S(1)}, u32[]{:S(2)}, u32[]{:S(2)}) collective-permute-start(f32[128,128]{1,0:T(8,128)S(1)} %slice.48), channel_id=1, source_target_pairs={{0,1},{1,0},{2,3},{3,2},{4,5},{5,4},{6,7},{7,6},{8,9},{9,8},{10,11... | collective-permute-start | bytes 196616 | tf_op jit(solution)/shard_map/ppermute | solution.py:312
  11.7 38.4 %collective-permute-start.4 = (f32[32,1024]{1,0:T(8,128)S(1)}, f32[32,1024]{1,0:T(8,128)S(1)}, u32[]{:S(2)}, u32[]{:S(2)}) collective-permute-start(f32[32,1024]{1,0:T(8,128)S(1)} %get-tuple-element.11), channel_id=1, source_target_pairs={{0,128},{1,129},{2,130},{3,131},{4,132},{5,133},{6,134},{7,135},{8... | collective-permute-start | bytes 393224 | tf_op jit(solution)/shard_map/ppermute | solution.py:303
  15.8 12.1 %collective-permute-start.1 = (f32[256,128]{1,0:T(8,128)S(1)}, f32[256,128]{1,0:T(8,128)S(1)}, u32[]{:S(2)}, u32[]{:S(2)}) collective-permute-start(f32[256,128]{1,0:T(8,128)S(1)} %get-tuple-element.14), channel_id=1, source_target_pairs={{0,12},{2,6},{1,13},{3,7},{16,28},{18,22},{17,29},{19,23},{32,44},... | collective-permute-start | bytes 393224 | tf_op jit(solution)/shard_map/ppermute | solution.py:303
  23.8 5.5 %collective-permute-start.2 = (f32[256,128]{1,0:T(8,128)S(1)}, f32[256,128]{1,0:T(8,128)S(1)}, u32[]{:S(2)}, u32[]{:S(2)}) collective-permute-start(f32[256,128]{1,0:T(8,128)S(1)} %get-tuple-element.15), channel_id=1, source_target_pairs={{0,10},{2,8},{1,11},{3,9},{16,26},{18,24},{17,27},{19,25},{32,42},... | collective-permute-start | bytes 393224 | tf_op jit(solution)/shard_map/ppermute | solution.py:303
  25.1 9.9 %collective-permute-start = (f32[256,128]{1,0:T(8,128)S(1)}, f32[256,128]{1,0:T(8,128)S(1)}, u32[]{:S(2)}, u32[]{:S(2)}) collective-permute-start(f32[256,128]{1,0:T(8,128)S(1)} %get-tuple-element.16), channel_id=1, source_target_pairs={{0,14},{2,4},{1,15},{3,5},{16,30},{18,20},{17,31},{19,21},{32,46},... | collective-permute-start | bytes 393224 | tf_op jit(solution)/shard_map/ppermute | solution.py:303
  27.3 17.5 %collective-permute-start.16 = (f32[256,128]{1,0:T(8,128)S(1)}, f32[256,128]{1,0:T(8,128)S(1)}, u32[]{:S(2)}, u32[]{:S(2)}) collective-permute-start(f32[256,128]{1,0:T(8,128)S(1)} %pad_maximum_fusion.2), channel_id=1, source_target_pairs={{0,8},{2,11},{16,24},{18,27},{32,40},{34,43},{48,56},{50,59},{64,7... | collective-permute-start | bytes 393224 | tf_op jit(solution)/shard_map/ppermute | solution.py:343
  28.0 18.1 %collective-permute-start.15 = (f32[256,128]{1,0:T(8,128)S(1)}, f32[256,128]{1,0:T(8,128)S(1)}, u32[]{:S(2)}, u32[]{:S(2)}) collective-permute-start(f32[256,128]{1,0:T(8,128)S(1)} %pad_maximum_fusion.2), channel_id=1, source_target_pairs={{0,6},{1,10},{2,9},{3,13},{16,22},{17,26},{18,25},{19,29},{32,38},... | collective-permute-start | bytes 393224 | tf_op jit(solution)/shard_map/ppermute | solution.py:343
  29.3 18.1 %collective-permute-start.14 = (f32[256,128]{1,0:T(8,128)S(1)}, f32[256,128]{1,0:T(8,128)S(1)}, u32[]{:S(2)}, u32[]{:S(2)}) collective-permute-start(f32[256,128]{1,0:T(8,128)S(1)} %pad_maximum_fusion.2), channel_id=1, source_target_pairs={{0,4},{1,12},{2,7},{3,15},{16,20},{17,28},{18,23},{19,31},{32,36},... | collective-permute-start | bytes 393224 | tf_op jit(solution)/shard_map/ppermute | solution.py:343
  35.0 12.5 %collective-permute-start.13 = (f32[256,128]{1,0:T(8,128)S(1)}, f32[256,128]{1,0:T(8,128)S(1)}, u32[]{:S(2)}, u32[]{:S(2)}) collective-permute-start(f32[256,128]{1,0:T(8,128)S(1)} %pad_maximum_fusion.2), channel_id=1, source_target_pairs={{0,2},{1,14},{2,5},{3,1},{16,18},{17,30},{18,21},{19,17},{32,34},{... | collective-permute-start | bytes 393224 | tf_op jit(solution)/shard_map/ppermute | solution.py:343
  44.8 6.6 %collective-permute-start.5 = (f32[32,1024]{1,0:T(8,128)S(1)}, f32[32,1024]{1,0:T(8,128)S(1)}, u32[]{:S(2)}, u32[]{:S(2)}) collective-permute-start(f32[32,1024]{1,0:T(8,128)S(1)} %get-tuple-element.12), channel_id=1, source_target_pairs={{0,192},{1,193},{2,194},{3,195},{4,196},{5,197},{6,198},{7,199},{8... | collective-permute-start | bytes 393224 | tf_op jit(solution)/shard_map/ppermute | solution.py:303
  46.1 5.3 %collective-permute-start.3 = (f32[32,1024]{1,0:T(8,128)S(1)}, f32[32,1024]{1,0:T(8,128)S(1)}, u32[]{:S(2)}, u32[]{:S(2)}) collective-permute-start(f32[32,1024]{1,0:T(8,128)S(1)} %get-tuple-element.13), channel_id=1, source_target_pairs={{0,64},{1,65},{2,66},{3,67},{4,68},{5,69},{6,70},{7,71},{8,72},{9,... | collective-permute-start | bytes 393224 | tf_op jit(solution)/shard_map/ppermute | solution.py:303
  47.5 6.2 %collective-permute-start.19 = (f32[256,128]{1,0:T(8,128)S(1)}, f32[256,128]{1,0:T(8,128)S(1)}, u32[]{:S(2)}, u32[]{:S(2)}) collective-permute-start(f32[256,128]{1,0:T(8,128)S(1)} %add_select_fusion), channel_id=1, source_target_pairs={{0,192},{1,193},{2,194},{3,195},{4,196},{5,197},{6,198},{7,199},{8... | collective-permute-start | bytes 393224 | tf_op jit(solution)/shard_map/ppermute | solution.py:303
  48.8 4.9 %collective-permute-start.18 = (f32[256,128]{1,0:T(8,128)S(1)}, f32[256,128]{1,0:T(8,128)S(1)}, u32[]{:S(2)}, u32[]{:S(2)}) collective-permute-start(f32[256,128]{1,0:T(8,128)S(1)} %add_select_fusion), channel_id=1, source_target_pairs={{0,128},{1,129},{2,130},{3,131},{4,132},{5,133},{6,134},{7,135},{8... | collective-permute-start | bytes 393224 | tf_op jit(solution)/shard_map/ppermute | solution.py:303
  50.1 3.6 %collective-permute-start.17 = (f32[256,128]{1,0:T(8,128)S(1)}, f32[256,128]{1,0:T(8,128)S(1)}, u32[]{:S(2)}, u32[]{:S(2)}) collective-permute-start(f32[256,128]{1,0:T(8,128)S(1)} %add_select_fusion), channel_id=1, source_target_pairs={{0,64},{1,65},{2,66},{3,67},{4,68},{5,69},{6,70},{7,71},{8,72},{9,... | collective-permute-start | bytes 393224 | tf_op jit(solution)/shard_map/ppermute | solution.py:303
  53.8 6.9 %collective-permute-start.22 = (f32[256,128]{1,0:T(8,128)S(1)}, f32[256,128]{1,0:T(8,128)S(1)}, u32[]{:S(2)}, u32[]{:S(2)}) collective-permute-start(f32[256,128]{1,0:T(8,128)S(1)} %select_add_fusion), channel_id=1, source_target_pairs={{0,48},{16,0},{32,16},{48,32},{1,49},{17,1},{33,17},{49,33},{2,50}... | collective-permute-start | bytes 393224 | tf_op jit(solution)/shard_map/ppermute | solution.py:308
  56.4 6.6 %collective-permute-start.21 = (f32[256,128]{1,0:T(8,128)S(1)}, f32[256,128]{1,0:T(8,128)S(1)}, u32[]{:S(2)}, u32[]{:S(2)}) collective-permute-start(f32[256,128]{1,0:T(8,128)S(1)} %select_add_fusion), channel_id=1, source_target_pairs={{0,32},{16,48},{32,0},{48,16},{1,33},{17,49},{33,1},{49,17},{2,34}... | collective-permute-start | bytes 393224 | tf_op jit(solution)/shard_map/ppermute | solution.py:308
  56.9 7.6 %collective-permute-start.20 = (f32[256,128]{1,0:T(8,128)S(1)}, f32[256,128]{1,0:T(8,128)S(1)}, u32[]{:S(2)}, u32[]{:S(2)}) collective-permute-start(f32[256,128]{1,0:T(8,128)S(1)} %select_add_fusion), channel_id=1, source_target_pairs={{0,16},{16,32},{32,48},{48,0},{1,17},{17,33},{33,49},{49,1},{2,18}... | collective-permute-start | bytes 393224 | tf_op jit(solution)/shard_map/ppermute | solution.py:308
  64.5 11.1 %collective-permute-start.23 = (f32[4,256,128]{2,1,0:T(8,128)S(1)}, f32[4,256,128]{2,1,0:T(8,128)S(1)}, u32[]{:S(2)}, u32[]{:S(2)}) collective-permute-start(f32[4,256,128]{2,1,0:T(8,128)S(1)} %pad_maximum_fusion.1.own), channel_id=1, source_target_pairs={{0,1},{1,0},{2,3},{3,2},{4,5},{5,4},{6,7},{7,6},{8,9},{9,8},{10,11... | collective-permute-start | bytes 1572872 | tf_op jit(solution)/shard_map/ppermute | solution.py:312
  65.0 4.8 %collective-permute-start.8 = (f32[32,1024]{1,0:T(8,128)S(1)}, f32[32,1024]{1,0:T(8,128)S(1)}, u32[]{:S(2)}, u32[]{:S(2)}) collective-permute-start(f32[32,1024]{1,0:T(8,128)S(1)} %add_select_fusion.1), channel_id=1, source_target_pairs={{0,48},{1,193},{16,0},{17,209},{32,16},{33,225},{48,32},{49,241},{... | collective-permute-start | bytes 393224 | tf_op jit(solution)/shard_map/ppermute | solution.py:322
  65.0 6.7 %collective-permute-start.7 = (f32[32,1024]{1,0:T(8,128)S(1)}, f32[32,1024]{1,0:T(8,128)S(1)}, u32[]{:S(2)}, u32[]{:S(2)}) collective-permute-start(f32[32,1024]{1,0:T(8,128)S(1)} %add_select_fusion.1), channel_id=1, source_target_pairs={{0,32},{1,129},{16,48},{17,145},{32,0},{33,161},{48,16},{49,177},{... | collective-permute-start | bytes 393224 | tf_op jit(solution)/shard_map/ppermute | solution.py:322
  69.0 5.0 %collective-permute-start.6 = (f32[32,1024]{1,0:T(8,128)S(1)}, f32[32,1024]{1,0:T(8,128)S(1)}, u32[]{:S(2)}, u32[]{:S(2)}) collective-permute-start(f32[32,1024]{1,0:T(8,128)S(1)} %add_select_fusion.1), channel_id=1, source_target_pairs={{0,16},{1,65},{16,32},{17,81},{32,48},{33,97},{48,0},{49,113},{64,... | collective-permute-start | bytes 393224 | tf_op jit(solution)/shard_map/ppermute | solution.py:322
  74.1 14.9 %collective-permute-start.11 = (f32[4,32,1024]{2,1,0:T(8,128)S(1)}, f32[4,32,1024]{2,1,0:T(8,128)S(1)}, u32[]{:S(2)}, u32[]{:S(2)}) collective-permute-start(f32[4,32,1024]{2,1,0:T(8,128)S(1)} %pad_maximum_fusion.c0), channel_id=1, source_target_pairs={{0,192},{1,49},{16,208},{17,1},{32,224},{33,17},{48,240},{49,33},{... | collective-permute-start | bytes 1572872 | tf_op jit(solution)/shard_map/ppermute | solution.py:322
  74.4 14.5 %collective-permute-start.10 = (f32[4,32,1024]{2,1,0:T(8,128)S(1)}, f32[4,32,1024]{2,1,0:T(8,128)S(1)}, u32[]{:S(2)}, u32[]{:S(2)}) collective-permute-start(f32[4,32,1024]{2,1,0:T(8,128)S(1)} %pad_maximum_fusion.c0), channel_id=1, source_target_pairs={{0,128},{1,33},{16,144},{17,49},{32,160},{33,1},{48,176},{49,17},{... | collective-permute-start | bytes 1572872 | tf_op jit(solution)/shard_map/ppermute | solution.py:322
  75.0 14.9 %collective-permute-start.9 = (f32[4,32,1024]{2,1,0:T(8,128)S(1)}, f32[4,32,1024]{2,1,0:T(8,128)S(1)}, u32[]{:S(2)}, u32[]{:S(2)}) collective-permute-start(f32[4,32,1024]{2,1,0:T(8,128)S(1)} %pad_maximum_fusion.c0), channel_id=1, source_target_pairs={{0,64},{1,17},{16,80},{17,33},{32,96},{33,49},{48,112},{49,1},{64,... | collective-permute-start | bytes 1572872 | tf_op jit(solution)/shard_map/ppermute | solution.py:322
  88.0 1.0 copy-start
  89.0 0.9 copy-start.1
Sparse Core Ops, SparseCore 0:
  44.9 33.3 all-gather.2

commit v5 on v4

--- a/solution.py
+++ b/solution.py
@@ -276,10 +276,10 @@
         return pl.BlockSpec(shape, lambda t, place: (0,) * len(shape), pipeline_mode=pl.Buffered(1))
 
     pieces = [
-        pl.BlockSpec(part, lambda t, place: (2 * ((8 - t) % 8), 0, 0)),
-        pl.BlockSpec(part, lambda t, place: (2 * ((8 - t) % 8) + 1, 0, 0)),
-        pl.BlockSpec(part, lambda t, place: (2 * (t + 1), 0, 0)),
-        pl.BlockSpec(part, lambda t, place: (2 * (t + 1) + 1, 0, 0)),
+        pl.BlockSpec(part, lambda t, place: (2 * t, 0, 0)),
+        pl.BlockSpec(part, lambda t, place: (jnp.where(t == 0, 8, 16 - 2 * t), 0, 0)),
+        pl.BlockSpec(part, lambda t, place: (jnp.where(t == 0, 11, 3 + 2 * t), 0, 0)),
+        pl.BlockSpec(part, lambda t, place: (2 * ((9 - t) % 8) + 1, 0, 0)),
     ]
     return pl.pallas_call(
         update_kernel,
@@ -326,36 +326,33 @@
     y, x = lax.axis_index("y"), lax.axis_index("x")
     z, c = lax.axis_index("z"), lax.axis_index("core")
     place = jnp.stack([y, x, z, c]).astype(jnp.int32)
-    depth = lax.axis_size("z")
 
     head = matrix[:BLOCK, :BLOCK]
     twin = swap(head)
     pair = jnp.concatenate([jnp.where(c == 0, head, twin), jnp.where(c == 0, twin, head)], 0)
     pairs = [[] for _ in range(4)]
     for (source_z, source_c), targets in (
-        ((0, 0), (1, 2, 3, 4)),
-        ((0, 1), (7, 6, 5)),
+        ((0, 0), (1, 2, 3)),
+        ((0, 1), (7, 6, 5, 4)),
         ((1, 0), (2, 3, 4, 5)),
         ((1, 1), (0, 7, 6)),
     ):
         for n, target in enumerate(targets):
             pairs[n].append((source_z * 2 + source_c, target * 2 + source_z))
-    got = [lax.ppermute(pair, ("z", "core"), group) for group in pairs]
-
-    lead = matrix[:, :BLOCK]
-    quarter = lead.shape[0] // 4
-    sent = [
-        send(lead[m * quarter : (m + 1) * quarter], "z", [(0, depth - m), (1, 1 + m)])
-        for m in (1, 2, 3)
+    quarter = matrix.shape[0] // 4
+    lead = [matrix[n * quarter : (n + 1) * quarter, :BLOCK] for n in range(4)]
+    got = [
+        lax.ppermute(jnp.concatenate([pair, lead[(n + 1) % 4]], 0), ("z", "core"), group)
+        for n, group in enumerate(pairs)
     ]
-    part = jnp.where(z < 2, lead[:quarter], sent[0] + sent[1] + sent[2])
+    mine = jnp.where(z == c, jnp.concatenate([pair, lead[0]], 0), got[0] + got[1] + got[2] + got[3])
+    pair, part = mine[: 2 * BLOCK], mine[2 * BLOCK :]
     rows = lax.all_gather(part, ("z", "core"))
 
     top = matrix[:BLOCK]
     sent = [send(top[m * SLAB : (m + 1) * SLAB], "y", [(0, m)]) for m in (1, 2, 3)]
     share = jnp.where(y == 0, top[:SLAB], sent[0] + sent[1] + sent[2])
 
-    pair = jnp.where(z == c, pair, got[0] + got[1] + got[2] + got[3])
     got = [send(pair, "y", [(0, m)]) for m in (1, 2, 3)]
     some = jnp.stack([share] + [turn(share, s, 0) for s in (1, 2, 3)])
     pair = after(jnp.where(y == 0, pair, got[0] + got[1] + got[2]), share)

time: 110 us -> 106 us (0.964); the launches traced: 108 us -> 106 us
  starting transfers between devices: 48.9 us -> 39.3 us
  waiting for transfers between devices: 13 us -> 21.3 us
    all_gather x1, waiting for transfers between devices: 0.01 us -> 7.02 us  [shards(): rows = lax.all_gather(part, ('z', 'core'))]
    ppermute x4, starting transfers between devices: 15.8 us -> 10.7 us  [shards(): lax.ppermute(jnp.concatenate([pair, lead[(n + 1) % 4]], 0), ('z', 'core')...]
    ppermute x9 -> x6, starting transfers between devices: 20.1 us -> 16.1 us  [send(): return lax.ppermute(value, axis, pairs)]
    ppermute x4, waiting for transfers between devices: 0.01 us -> 2.74 us  [shards(): lax.ppermute(jnp.concatenate([pair, lead[(n + 1) % 4]], 0), ('z', 'core')...]
    select_n x2 -> x1, other arithmetic: 1.62 us -> 0.06 us  [shards(): jnp.where(z == c, jnp.concatenate([pair, lead[0]], 0), got[0] + got[1] +...]
    ppermute x3, waiting for transfers between devices: 7.01 us -> 5.6 us  [shift(): lax.ppermute(value, axis, [(i, (i + step) % size) for i in range(size)])]
  transfers between devices with their start and end apart: 25 -> 22, of which waited for: 7 -> 9; matrix products, arithmetic and copies ran while one was open for 6% -> 4% of each run, Pallas kernels for 11% -> 12%
where the time goes in v5:
time: 106 us
  starting transfers between devices  39.3 us (37%)
  Pallas kernels  23.8 us (22%)
  waiting for transfers between devices  21.3 us (20%)
  between operations  14.3 us (13%)
  local copies, waits for them, and re-layouts  4.55 us (4%)
  other arithmetic  2.77 us (3%)
    ppermute x6, starting transfers between devices, send(): return lax.ppermute(value, axis, pairs)  16.1 us
    pallas_call x1, Pallas kernels, factor_head(): pl.pallas_call(head_kernel, out_shape=shapes, in_specs=[pl.BlockSpec(memo...  12.3 us
    pallas_call x1, Pallas kernels, update(): pl.pallas_call(update_kernel, out_shape=jax.ShapeDtypeStruct(matrix.shape...  11.5 us
    ppermute x4, starting transfers between devices, shards(): lax.ppermute(jnp.concatenate([pair, lead[(n + 1) % 4]], 0), ('z', 'core')...  10.7 us
    all_gather x1, waiting for transfers between devices, shards(): rows = lax.all_gather(part, ('z', 'core'))  7.02 us
    ppermute x6, waiting for transfers between devices, turn(): return lax.ppermute(value, ('y', 'x', 'core'), pairs)  5.87 us
    ppermute x3, waiting for transfers between devices, shift(): lax.ppermute(value, axis, [(i, (i + step) % size) for i in range(size)])  5.6 us
    ppermute x6, starting transfers between devices, turn(): return lax.ppermute(value, ('y', 'x', 'core'), pairs)  5.43 us
  transfers between devices with their start and end apart: 22, of which 9 were waited for; matrix products, arithmetic and copies ran while one was open for 4% of the time, Pallas kernels for 12%

profile of v5, /device:TPU:1, one launch (start us, length us, event | category | flops | bytes accessed | tf_op | source)
XLA Modules:
  0.0 106.0 jit_solution(6941713438500139562)
XLA Ops:
  6.5 0.0 all-gather.3.cloned.1.call-start
  6.5 0.8 slice.41
  7.4 3.2 %collective-permute-start = (f32[128,128]{1,0:T(8,128)S(1)}, f32[128,128]{1,0:T(8,128)S(1)}, u32[]{:S(2)}, u32[]{:S(2)}) collective-permute-start(f32[128,128]{1,0:T(8,128)S(1)} %slice.41), channel_id=1, source_target_pairs={{0,1},{1,0},{2,3},{3,2},{4,5},{5,4},{6,7},{7,6},{8,9},{9,8},{10,11... | collective-permute-start | bytes 196616 | tf_op jit(solution)/shard_map/ppermute | solution.py:312
  10.6 1.1 %fusion.4 = (f32[256,128]{1,0:T(8,128)S(1)}, f32[256,128]{1,0:T(8,128)S(1)}, f32[256,128]{1,0:T(8,128)S(1)}, f32[256,128]{1,0:T(8,128)S(1)}) fusion(f32[1024,1024]{1,0:T(8,128)} %a_ref.1), kind=kLoop, calls=%fused_computation.14 | loop fusion | bytes 1048576 | tf_op jit(solution)/shard_map/slice | solution.py:343
  11.8 0.0 collective-permute-done
  11.8 0.9 broadcast_select_fusion.1
  12.6 0.1 fusion.1
  12.7 6.2 %collective-permute-start.2 = (f32[512,128]{1,0:T(8,128)S(1)}, f32[512,128]{1,0:T(8,128)S(1)}, u32[]{:S(2)}, u32[]{:S(2)}) collective-permute-start(f32[512,128]{1,0:T(8,128)S(1)} %get-tuple-element.20), channel_id=1, source_target_pairs={{0,4},{1,12},{2,7},{3,15},{16,20},{17,28},{18,23},{19,31},{32,36},... | collective-permute-start | bytes 786440 | tf_op jit(solution)/shard_map/ppermute | solution.py:345
  18.9 1.9 %collective-permute-start.1 = (f32[512,128]{1,0:T(8,128)S(1)}, f32[512,128]{1,0:T(8,128)S(1)}, u32[]{:S(2)}, u32[]{:S(2)}) collective-permute-start(f32[512,128]{1,0:T(8,128)S(1)} %get-tuple-element.21), channel_id=1, source_target_pairs={{0,2},{1,14},{2,5},{3,1},{16,18},{17,30},{18,21},{19,17},{32,34},{... | collective-permute-start | bytes 786440 | tf_op jit(solution)/shard_map/ppermute | solution.py:345
  20.8 1.3 %collective-permute-start.3 = (f32[512,128]{1,0:T(8,128)S(1)}, f32[512,128]{1,0:T(8,128)S(1)}, u32[]{:S(2)}, u32[]{:S(2)}) collective-permute-start(f32[512,128]{1,0:T(8,128)S(1)} %get-tuple-element.22), channel_id=1, source_target_pairs={{0,6},{1,10},{2,9},{3,13},{16,22},{17,26},{18,25},{19,29},{32,38},... | collective-permute-start | bytes 786440 | tf_op jit(solution)/shard_map/ppermute | solution.py:345
  22.2 1.3 %collective-permute-start.4 = (f32[512,128]{1,0:T(8,128)S(1)}, f32[512,128]{1,0:T(8,128)S(1)}, u32[]{:S(2)}, u32[]{:S(2)}) collective-permute-start(f32[512,128]{1,0:T(8,128)S(1)} %get-tuple-element.23), channel_id=1, source_target_pairs={{1,8},{2,11},{17,24},{18,27},{33,40},{34,43},{49,56},{50,59},{65,7... | collective-permute-start | bytes 786440 | tf_op jit(solution)/shard_map/ppermute | solution.py:345
  23.5 1.1 %fusion.3 = (f32[32,1024]{1,0:T(8,128)S(1)}, f32[32,1024]{1,0:T(8,128)S(1)}, f32[32,1024]{1,0:T(8,128)S(1)}) fusion(f32[1024,1024]{1,0:T(8,128)} %a_ref.1), kind=kLoop, calls=%fused_computation.13 | loop fusion | bytes 786432 | tf_op jit(solution)/shard_map/slice | solution.py:353
  24.5 4.8 %collective-permute-start.6 = (f32[32,1024]{1,0:T(8,128)S(1)}, f32[32,1024]{1,0:T(8,128)S(1)}, u32[]{:S(2)}, u32[]{:S(2)}) collective-permute-start(f32[32,1024]{1,0:T(8,128)S(1)} %get-tuple-element.11), channel_id=1, source_target_pairs={{0,128},{1,129},{2,130},{3,131},{4,132},{5,133},{6,134},{7,135},{8... | collective-permute-start | bytes 393224 | tf_op jit(solution)/shard_map/ppermute | solution.py:303
  29.4 0.0 collective-permute-done.2
  29.4 1.3 %collective-permute-start.5 = (f32[32,1024]{1,0:T(8,128)S(1)}, f32[32,1024]{1,0:T(8,128)S(1)}, u32[]{:S(2)}, u32[]{:S(2)}) collective-permute-start(f32[32,1024]{1,0:T(8,128)S(1)} %get-tuple-element.12), channel_id=1, source_target_pairs={{0,64},{1,65},{2,66},{3,67},{4,68},{5,69},{6,70},{7,71},{8,72},{9,... | collective-permute-start | bytes 393224 | tf_op jit(solution)/shard_map/ppermute | solution.py:303
  30.7 2.7 %collective-permute-done.1 = f32[512,128]{1,0:T(8,128)S(1)} collective-permute-done((f32[512,128]{1,0:T(8,128)S(1)}, f32[512,128]{1,0:T(8,128)S(1)}, u32[]{:S(2)}, u32[]{:S(2)}) %collective-permute-start.1) | collective-permute-done | bytes 262176 | tf_op jit(solution)/shard_map/ppermute | solution.py:345
  33.4 4.6 %collective-permute-start.7 = (f32[32,1024]{1,0:T(8,128)S(1)}, f32[32,1024]{1,0:T(8,128)S(1)}, u32[]{:S(2)}, u32[]{:S(2)}) collective-permute-start(f32[32,1024]{1,0:T(8,128)S(1)} %get-tuple-element.13), channel_id=1, source_target_pairs={{0,192},{1,193},{2,194},{3,195},{4,196},{5,197},{6,198},{7,199},{8... | collective-permute-start | bytes 393224 | tf_op jit(solution)/shard_map/ppermute | solution.py:303
  38.1 0.0 collective-permute-done.3
  38.1 0.0 collective-permute-done.4
  38.1 0.1 add_select_fusion
  38.2 2.8 %collective-permute-start.16 = (f32[256,128]{1,0:T(8,128)S(1)}, f32[256,128]{1,0:T(8,128)S(1)}, u32[]{:S(2)}, u32[]{:S(2)}) collective-permute-start(f32[256,128]{1,0:T(8,128)S(1)} %slice.54), channel_id=1, source_target_pairs={{0,192},{1,193},{2,194},{3,195},{4,196},{5,197},{6,198},{7,199},{8... | collective-permute-start | bytes 393224 | tf_op jit(solution)/shard_map/ppermute | solution.py:303
  41.0 1.3 %collective-permute-start.15 = (f32[256,128]{1,0:T(8,128)S(1)}, f32[256,128]{1,0:T(8,128)S(1)}, u32[]{:S(2)}, u32[]{:S(2)}) collective-permute-start(f32[256,128]{1,0:T(8,128)S(1)} %slice.54), channel_id=1, source_target_pairs={{0,128},{1,129},{2,130},{3,131},{4,132},{5,133},{6,134},{7,135},{8... | collective-permute-start | bytes 393224 | tf_op jit(solution)/shard_map/ppermute | solution.py:303
  42.3 0.0 collective-permute-done.6
  42.3 1.3 %collective-permute-start.14 = (f32[256,128]{1,0:T(8,128)S(1)}, f32[256,128]{1,0:T(8,128)S(1)}, u32[]{:S(2)}, u32[]{:S(2)}) collective-permute-start(f32[256,128]{1,0:T(8,128)S(1)} %slice.54), channel_id=1, source_target_pairs={{0,64},{1,65},{2,66},{3,67},{4,68},{5,69},{6,70},{7,71},{8,72},{9,... | collective-permute-start | bytes 393224 | tf_op jit(solution)/shard_map/ppermute | solution.py:303
  43.6 0.0 collective-permute-done.5
  43.6 0.0 collective-permute-done.7
  43.6 0.9 add_select_fusion.1
  44.6 0.5 slice.55
  45.7 0.0 collective-permute-done.16
  45.7 0.0 collective-permute-done.15
  45.7 0.0 collective-permute-done.14
  45.8 0.7 select_add_fusion
  46.4 0.0 all-gather.3.cloned.1.call-update
  46.5 2.6 %collective-permute-start.19 = (f32[256,128]{1,0:T(8,128)S(1)}, f32[256,128]{1,0:T(8,128)S(1)}, u32[]{:S(2)}, u32[]{:S(2)}) collective-permute-start(f32[256,128]{1,0:T(8,128)S(1)} %get-tuple-element.18), channel_id=1, source_target_pairs={{0,48},{16,0},{32,16},{48,32},{1,49},{17,1},{33,17},{49,33},{2,50}... | collective-permute-start | bytes 393224 | tf_op jit(solution)/shard_map/ppermute | solution.py:308
  49.0 0.5 collective-permute-start.18
  49.5 0.6 collective-permute-start.17
  50.2 2.2 %collective-permute-done.19 = f32[256,128]{1,0:T(8,128)S(1)} collective-permute-done((f32[256,128]{1,0:T(8,128)S(1)}, f32[256,128]{1,0:T(8,128)S(1)}, u32[]{:S(2)}, u32[]{:S(2)}) %collective-permute-start.19) | collective-permute-done | bytes 131104 | tf_op jit(solution)/shard_map/ppermute | solution.py:308
  52.3 2.1 %collective-permute-done.18 = f32[256,128]{1,0:T(8,128)S(1)} collective-permute-done((f32[256,128]{1,0:T(8,128)S(1)}, f32[256,128]{1,0:T(8,128)S(1)}, u32[]{:S(2)}, u32[]{:S(2)}) %collective-permute-start.18) | collective-permute-done | bytes 131104 | tf_op jit(solution)/shard_map/ppermute | solution.py:308
  54.5 1.3 %collective-permute-done.17 = f32[256,128]{1,0:T(8,128)S(1)} collective-permute-done((f32[256,128]{1,0:T(8,128)S(1)}, f32[256,128]{1,0:T(8,128)S(1)}, u32[]{:S(2)}, u32[]{:S(2)}) %collective-permute-start.17) | collective-permute-done | bytes 131104 | tf_op jit(solution)/shard_map/ppermute | solution.py:308
  55.8 0.1 collective-permute-start.20
  55.9 0.5 collective-permute-start.10
  56.4 3.3 %collective-permute-start.9 = (f32[32,1024]{1,0:T(8,128)S(1)}, f32[32,1024]{1,0:T(8,128)S(1)}, u32[]{:S(2)}, u32[]{:S(2)}) collective-permute-start(f32[32,1024]{1,0:T(8,128)S(1)} %add_select_fusion.1), channel_id=1, source_target_pairs={{0,32},{1,129},{16,48},{17,145},{32,0},{33,161},{48,16},{49,177},{... | collective-permute-start | bytes 393224 | tf_op jit(solution)/shard_map/ppermute | solution.py:322
  59.8 0.0 collective-permute-start.8
  59.8 0.1 pad_add_fusion.place
  59.9 0.8 collective-permute-done.10
  60.6 1.8 %collective-permute-done.9 = f32[32,1024]{1,0:T(8,128)S(1)} collective-permute-done((f32[32,1024]{1,0:T(8,128)S(1)}, f32[32,1024]{1,0:T(8,128)S(1)}, u32[]{:S(2)}, u32[]{:S(2)}) %collective-permute-start.9) | collective-permute-done | bytes 131104 | tf_op jit(solution)/shard_map/ppermute | solution.py:322
  62.4 2.4 %collective-permute-done.8 = f32[32,1024]{1,0:T(8,128)S(1)} collective-permute-done((f32[32,1024]{1,0:T(8,128)S(1)}, f32[32,1024]{1,0:T(8,128)S(1)}, u32[]{:S(2)}, u32[]{:S(2)}) %collective-permute-start.8) | collective-permute-done | bytes 131104 | tf_op jit(solution)/shard_map/ppermute | solution.py:322
  64.9 0.4 collective-permute-start.13
  65.2 0.5 collective-permute-start.12
  65.7 0.7 collective-permute-start.11
  66.4 0.0 collective-permute-done.20.other
  66.4 12.3 %shard_map.17 = (f32[128,128]{1,0:T(8,128)S(1)}, f32[512,512]{1,0:T(8,128)S(1)}) custom-call(s32[4]{0:T(128)S(1)} %pad_add_fusion.place, f32[4,256,128]{2,1,0:T(8,128)S(1)} %pad_maximum_fusion.1.own, f32[4,256,128]{2,1,0:T(8,128)S(1)} %collective-permute-done.20.other), custom_call_target="tpu_custom_call" | custom-call | flops 30000001024 | bytes 4194304 | tf_op jit(solution)/shard_map/pallas_call | solution.py:187
  78.7 0.0 copy-start
  78.8 1.0 copy-done
  79.7 0.0 collective-permute-done.13.c3
  79.7 0.0 copy-start.1
  79.7 0.0 collective-permute-done.12.c2
  79.8 0.9 collective-permute-done.11.c1
  80.7 7.0 %all-gather.3.cloned.1.call-done = f32[4096,128]{1,0:T(8,128)} async-done(((f32[256,128]{1,0:T(8,128)}), f32[4096,128]{1,0:T(8,128)}) %all-gather.3.cloned.1.call-update) | async-done | bytes 2097168 | tf_op jit(solution)/shard_map/all_gather | solution.py:350
  87.7 0.0 copy-done.1
  87.7 11.5 %shard_map.18 = f32[1024,1024]{1,0:T(8,128)} custom-call(s32[4]{0:T(128)S(1)} %pad_add_fusion.place, f32[1024,1024]{1,0:T(8,128)} %a_ref.1, f32[16,256,128]{2,1,0:T(8,128)} %bitcast.14, f32[16,256,128]{2,1,0:T(8,128)} %bitcast.15, f32[16,256,128]{2,1,0:T(8,128)} %bitcast.16, f32[16,256,128]{2,1,0:T(8,128)} %bitcast.17, ...), custom_call_target="tpu_custom_call" | custom-call | tf_op jit(solution)/shard_map/pallas_call | solution.py:284
  (3 shorter events, 0.1 us)
Async XLA Ops:
  6.5 81.1 %all-gather.3.cloned.1.call-start = ((), (), s32[]{:S(2)}) async-start(), calls=%async_computation | async-start | bytes 2228224 | tf_op jit(solution)/shard_map/all_gather | solution.py:350
  7.4 4.4 %collective-permute-start = (f32[128,128]{1,0:T(8,128)S(1)}, f32[128,128]{1,0:T(8,128)S(1)}, u32[]{:S(2)}, u32[]{:S(2)}) collective-permute-start(f32[128,128]{1,0:T(8,128)S(1)} %slice.41), channel_id=1, source_target_pairs={{0,1},{1,0},{2,3},{3,2},{4,5},{5,4},{6,7},{7,6},{8,9},{9,8},{10,11... | collective-permute-start | bytes 196616 | tf_op jit(solution)/shard_map/ppermute | solution.py:312
  12.7 16.7 %collective-permute-start.2 = (f32[512,128]{1,0:T(8,128)S(1)}, f32[512,128]{1,0:T(8,128)S(1)}, u32[]{:S(2)}, u32[]{:S(2)}) collective-permute-start(f32[512,128]{1,0:T(8,128)S(1)} %get-tuple-element.20), channel_id=1, source_target_pairs={{0,4},{1,12},{2,7},{3,15},{16,20},{17,28},{18,23},{19,31},{32,36},... | collective-permute-start | bytes 786440 | tf_op jit(solution)/shard_map/ppermute | solution.py:345
  18.9 14.5 %collective-permute-start.1 = (f32[512,128]{1,0:T(8,128)S(1)}, f32[512,128]{1,0:T(8,128)S(1)}, u32[]{:S(2)}, u32[]{:S(2)}) collective-permute-start(f32[512,128]{1,0:T(8,128)S(1)} %get-tuple-element.21), channel_id=1, source_target_pairs={{0,2},{1,14},{2,5},{3,1},{16,18},{17,30},{18,21},{19,17},{32,34},{... | collective-permute-start | bytes 786440 | tf_op jit(solution)/shard_map/ppermute | solution.py:345
  20.8 17.2 %collective-permute-start.3 = (f32[512,128]{1,0:T(8,128)S(1)}, f32[512,128]{1,0:T(8,128)S(1)}, u32[]{:S(2)}, u32[]{:S(2)}) collective-permute-start(f32[512,128]{1,0:T(8,128)S(1)} %get-tuple-element.22), channel_id=1, source_target_pairs={{0,6},{1,10},{2,9},{3,13},{16,22},{17,26},{18,25},{19,29},{32,38},... | collective-permute-start | bytes 786440 | tf_op jit(solution)/shard_map/ppermute | solution.py:345
  22.2 15.9 %collective-permute-start.4 = (f32[512,128]{1,0:T(8,128)S(1)}, f32[512,128]{1,0:T(8,128)S(1)}, u32[]{:S(2)}, u32[]{:S(2)}) collective-permute-start(f32[512,128]{1,0:T(8,128)S(1)} %get-tuple-element.23), channel_id=1, source_target_pairs={{1,8},{2,11},{17,24},{18,27},{33,40},{34,43},{49,56},{50,59},{65,7... | collective-permute-start | bytes 786440 | tf_op jit(solution)/shard_map/ppermute | solution.py:345
  24.5 17.8 %collective-permute-start.6 = (f32[32,1024]{1,0:T(8,128)S(1)}, f32[32,1024]{1,0:T(8,128)S(1)}, u32[]{:S(2)}, u32[]{:S(2)}) collective-permute-start(f32[32,1024]{1,0:T(8,128)S(1)} %get-tuple-element.11), channel_id=1, source_target_pairs={{0,128},{1,129},{2,130},{3,131},{4,132},{5,133},{6,134},{7,135},{8... | collective-permute-start | bytes 393224 | tf_op jit(solution)/shard_map/ppermute | solution.py:303
  29.4 14.2 %collective-permute-start.5 = (f32[32,1024]{1,0:T(8,128)S(1)}, f32[32,1024]{1,0:T(8,128)S(1)}, u32[]{:S(2)}, u32[]{:S(2)}) collective-permute-start(f32[32,1024]{1,0:T(8,128)S(1)} %get-tuple-element.12), channel_id=1, source_target_pairs={{0,64},{1,65},{2,66},{3,67},{4,68},{5,69},{6,70},{7,71},{8,72},{9,... | collective-permute-start | bytes 393224 | tf_op jit(solution)/shard_map/ppermute | solution.py:303
  33.4 10.2 %collective-permute-start.7 = (f32[32,1024]{1,0:T(8,128)S(1)}, f32[32,1024]{1,0:T(8,128)S(1)}, u32[]{:S(2)}, u32[]{:S(2)}) collective-permute-start(f32[32,1024]{1,0:T(8,128)S(1)} %get-tuple-element.13), channel_id=1, source_target_pairs={{0,192},{1,193},{2,194},{3,195},{4,196},{5,197},{6,198},{7,199},{8... | collective-permute-start | bytes 393224 | tf_op jit(solution)/shard_map/ppermute | solution.py:303
  38.2 7.5 %collective-permute-start.16 = (f32[256,128]{1,0:T(8,128)S(1)}, f32[256,128]{1,0:T(8,128)S(1)}, u32[]{:S(2)}, u32[]{:S(2)}) collective-permute-start(f32[256,128]{1,0:T(8,128)S(1)} %slice.54), channel_id=1, source_target_pairs={{0,192},{1,193},{2,194},{3,195},{4,196},{5,197},{6,198},{7,199},{8... | collective-permute-start | bytes 393224 | tf_op jit(solution)/shard_map/ppermute | solution.py:303
  41.0 4.8 %collective-permute-start.15 = (f32[256,128]{1,0:T(8,128)S(1)}, f32[256,128]{1,0:T(8,128)S(1)}, u32[]{:S(2)}, u32[]{:S(2)}) collective-permute-start(f32[256,128]{1,0:T(8,128)S(1)} %slice.54), channel_id=1, source_target_pairs={{0,128},{1,129},{2,130},{3,131},{4,132},{5,133},{6,134},{7,135},{8... | collective-permute-start | bytes 393224 | tf_op jit(solution)/shard_map/ppermute | solution.py:303
  42.3 3.5 %collective-permute-start.14 = (f32[256,128]{1,0:T(8,128)S(1)}, f32[256,128]{1,0:T(8,128)S(1)}, u32[]{:S(2)}, u32[]{:S(2)}) collective-permute-start(f32[256,128]{1,0:T(8,128)S(1)} %slice.54), channel_id=1, source_target_pairs={{0,64},{1,65},{2,66},{3,67},{4,68},{5,69},{6,70},{7,71},{8,72},{9,... | collective-permute-start | bytes 393224 | tf_op jit(solution)/shard_map/ppermute | solution.py:303
  46.5 5.9 %collective-permute-start.19 = (f32[256,128]{1,0:T(8,128)S(1)}, f32[256,128]{1,0:T(8,128)S(1)}, u32[]{:S(2)}, u32[]{:S(2)}) collective-permute-start(f32[256,128]{1,0:T(8,128)S(1)} %get-tuple-element.18), channel_id=1, source_target_pairs={{0,48},{16,0},{32,16},{48,32},{1,49},{17,1},{33,17},{49,33},{2,50}... | collective-permute-start | bytes 393224 | tf_op jit(solution)/shard_map/ppermute | solution.py:308
  49.0 5.4 %collective-permute-start.18 = (f32[256,128]{1,0:T(8,128)S(1)}, f32[256,128]{1,0:T(8,128)S(1)}, u32[]{:S(2)}, u32[]{:S(2)}) collective-permute-start(f32[256,128]{1,0:T(8,128)S(1)} %get-tuple-element.18), channel_id=1, source_target_pairs={{0,32},{16,48},{32,0},{48,16},{1,33},{17,49},{33,1},{49,17},{2,34}... | collective-permute-start | bytes 393224 | tf_op jit(solution)/shard_map/ppermute | solution.py:308
  49.5 6.2 %collective-permute-start.17 = (f32[256,128]{1,0:T(8,128)S(1)}, f32[256,128]{1,0:T(8,128)S(1)}, u32[]{:S(2)}, u32[]{:S(2)}) collective-permute-start(f32[256,128]{1,0:T(8,128)S(1)} %get-tuple-element.18), channel_id=1, source_target_pairs={{0,16},{16,32},{32,48},{48,0},{1,17},{17,33},{33,49},{49,1},{2,18}... | collective-permute-start | bytes 393224 | tf_op jit(solution)/shard_map/ppermute | solution.py:308
  55.8 10.6 %collective-permute-start.20 = (f32[4,256,128]{2,1,0:T(8,128)S(1)}, f32[4,256,128]{2,1,0:T(8,128)S(1)}, u32[]{:S(2)}, u32[]{:S(2)}) collective-permute-start(f32[4,256,128]{2,1,0:T(8,128)S(1)} %pad_maximum_fusion.1.own), channel_id=1, source_target_pairs={{0,1},{1,0},{2,3},{3,2},{4,5},{5,4},{6,7},{7,6},{8,9},{9,8},{10,11... | collective-permute-start | bytes 1572872 | tf_op jit(solution)/shard_map/ppermute | solution.py:312
  55.9 4.7 %collective-permute-start.10 = (f32[32,1024]{1,0:T(8,128)S(1)}, f32[32,1024]{1,0:T(8,128)S(1)}, u32[]{:S(2)}, u32[]{:S(2)}) collective-permute-start(f32[32,1024]{1,0:T(8,128)S(1)} %add_select_fusion.1), channel_id=1, source_target_pairs={{0,48},{1,193},{16,0},{17,209},{32,16},{33,225},{48,32},{49,241},{... | collective-permute-start | bytes 393224 | tf_op jit(solution)/shard_map/ppermute | solution.py:322
  56.4 6.0 %collective-permute-start.9 = (f32[32,1024]{1,0:T(8,128)S(1)}, f32[32,1024]{1,0:T(8,128)S(1)}, u32[]{:S(2)}, u32[]{:S(2)}) collective-permute-start(f32[32,1024]{1,0:T(8,128)S(1)} %add_select_fusion.1), channel_id=1, source_target_pairs={{0,32},{1,129},{16,48},{17,145},{32,0},{33,161},{48,16},{49,177},{... | collective-permute-start | bytes 393224 | tf_op jit(solution)/shard_map/ppermute | solution.py:322
  59.8 5.0 %collective-permute-start.8 = (f32[32,1024]{1,0:T(8,128)S(1)}, f32[32,1024]{1,0:T(8,128)S(1)}, u32[]{:S(2)}, u32[]{:S(2)}) collective-permute-start(f32[32,1024]{1,0:T(8,128)S(1)} %add_select_fusion.1), channel_id=1, source_target_pairs={{0,16},{1,65},{16,32},{17,81},{32,48},{33,97},{48,0},{49,113},{64,... | collective-permute-start | bytes 393224 | tf_op jit(solution)/shard_map/ppermute | solution.py:322
  64.9 14.9 %collective-permute-start.13 = (f32[4,32,1024]{2,1,0:T(8,128)S(1)}, f32[4,32,1024]{2,1,0:T(8,128)S(1)}, u32[]{:S(2)}, u32[]{:S(2)}) collective-permute-start(f32[4,32,1024]{2,1,0:T(8,128)S(1)} %pad_maximum_fusion.c0), channel_id=1, source_target_pairs={{0,192},{1,49},{16,208},{17,1},{32,224},{33,17},{48,240},{49,33},{... | collective-permute-start | bytes 1572872 | tf_op jit(solution)/shard_map/ppermute | solution.py:322
  65.2 14.5 %collective-permute-start.12 = (f32[4,32,1024]{2,1,0:T(8,128)S(1)}, f32[4,32,1024]{2,1,0:T(8,128)S(1)}, u32[]{:S(2)}, u32[]{:S(2)}) collective-permute-start(f32[4,32,1024]{2,1,0:T(8,128)S(1)} %pad_maximum_fusion.c0), channel_id=1, source_target_pairs={{0,128},{1,33},{16,144},{17,49},{32,160},{33,1},{48,176},{49,17},{... | collective-permute-start | bytes 1572872 | tf_op jit(solution)/shard_map/ppermute | solution.py:322
  65.7 14.9 %collective-permute-start.11 = (f32[4,32,1024]{2,1,0:T(8,128)S(1)}, f32[4,32,1024]{2,1,0:T(8,128)S(1)}, u32[]{:S(2)}, u32[]{:S(2)}) collective-permute-start(f32[4,32,1024]{2,1,0:T(8,128)S(1)} %pad_maximum_fusion.c0), channel_id=1, source_target_pairs={{0,64},{1,17},{16,80},{17,33},{32,96},{33,49},{48,112},{49,1},{64,... | collective-permute-start | bytes 1572872 | tf_op jit(solution)/shard_map/ppermute | solution.py:322
  78.7 1.0 copy-start
  79.7 7.9 %copy-start.1 = (f32[4,32,1024]{2,1,0:T(8,128)}, f32[4,32,1024]{2,1,0:T(8,128)S(1)}, u32[]{:S(2)}) copy-start(f32[4,32,1024]{2,1,0:T(8,128)S(1)} %collective-permute-done.13.c3) | copy-start | bytes 1572868
Sparse Core Ops, SparseCore 0:
  46.6 41.0 all-gather.2
